TPU v7x, 128 devices: a whole 4x4x4 slice. The times are simulated.
128 devices in a mesh: fsdp: 64 (over y, z_lo, x, core), tp: 2 (over z_hi).
Axes of the slice: x: 4, y: 4, z: 4 (z_hi: 2, z_lo: 2; z = z_hi * 2 + z_lo), core: 2. Of those that a mesh axis runs over, the one named last changes fastest.
Arguments:
- x_in: bfloat16 [16384, 1024], P(('fsdp', 'tp')), may hold values from -6 to 6
- cotangent: bfloat16 [16384, 1024], P(('fsdp', 'tp')), may hold values from -6 to 6
- seq_lengths: int32 [64, 4], P('fsdp'), may hold values from 1 to 253, as said below
- gain_in: bfloat16 [2, 1024], replicated, may hold values from 0.5 to 1.5
- w_zx: bfloat16 [2, 1024, 2, 2048], P(None, 'fsdp', None, 'tp'), may hold values from -0.1875 to 0.1875
- w_bc: bfloat16 [2, 1024, 256], P(None, 'fsdp'), may hold values from -0.1875 to 0.1875
- w_dt: bfloat16 [2, 1024, 32], P(None, 'fsdp', 'tp'), may hold values from -0.1875 to 0.1875
- conv_x: bfloat16 [2, 4, 2048], P(None, None, 'tp'), may hold values from -0.5 to 0.5
- conv_bc: bfloat16 [2, 4, 256], replicated, may hold values from -0.5 to 0.5
- bias_x: bfloat16 [2, 2048], P(None, 'tp'), may hold values from -0.5 to 0.5
- bias_bc: bfloat16 [2, 256], replicated, may hold values from -0.5 to 0.5
- dt_bias: bfloat16 [2, 32], P(None, 'tp'), may hold values from -6 to -2
- a_log: bfloat16 [2, 32], P(None, 'tp'), may hold values from 0 to 2.5
- skip: bfloat16 [2, 32], P(None, 'tp'), may hold values from 0.5 to 1.5
- gain_gate: bfloat16 [2, 2048], P(None, 'tp'), may hold values from 0.5 to 1.5
- w_out: bfloat16 [2, 2048, 1024], P(None, 'tp', 'fsdp'), may hold values from -0.125 to 0.125
Outputs:
- act_out: bfloat16 [16384, 1024], P(('fsdp', 'tp'))
- grad_in: float32 [16384, 1024], P(('fsdp', 'tp'))
- grad_gain_in: float32 [2, 1024], replicated
- grad_w_zx: float32 [2, 1024, 2, 2048], P(None, 'fsdp', None, 'tp')
- grad_w_bc: float32 [2, 1024, 256], P(None, 'fsdp')
- grad_w_dt: float32 [2, 1024, 32], P(None, 'fsdp', 'tp')
- grad_conv_x: float32 [2, 4, 2048], P(None, None, 'tp')
- grad_conv_bc: float32 [2, 4, 256], replicated
- grad_bias_x: float32 [2, 2048], P(None, 'tp')
- grad_bias_bc: float32 [2, 256], replicated
- grad_dt_bias: float32 [2, 32], P(None, 'tp')
- grad_a_log: float32 [2, 32], P(None, 'tp')
- grad_skip: float32 [2, 32], P(None, 'tp')
- grad_gain_gate: float32 [2, 2048], P(None, 'tp')
- grad_w_out: float32 [2, 2048, 1024], P(None, 'tp', 'fsdp')
Inputs may be any that keep to these rules, and one draw needn't show every extreme that they name: `seq_lengths`: row g lists the lengths of the 4 sequences packed in order from the first row of group g; rows after their sum are padding. Every row sums to 192 or more and some row sums to 256; in every row one sequence holds both rows 127 and 128.
All inputs are finite; a program needn't handle non-finite values.
Results may differ from a plain program's by a relative error of at most 0.03.
Values may be sent and summed in bfloat16 or wider, within the bound.
A program may use at most 192 MiB of HBM per device.

v0:
```python
import jax
import jax.numpy as jnp
from jax import lax
from jax.sharding import PartitionSpec as P

SPAN = 256
SEQS = 4
INNER = 2048


EPS = 1e-05


def joined_along(parts, dim):
    shape = list(parts.shape[1:])
    shape[dim] *= parts.shape[0]
    return jnp.moveaxis(parts, 0, dim).reshape(shape)


def copy_for_each(shard, axis):
    length = lax.axis_size(axis)
    return lax.all_to_all(
        jnp.broadcast_to(shard[None], (length, *shard.shape)), axis, 0, 0, tiled=True
    )


def gather_directly(shard, axis, dim):
    return joined_along(copy_for_each(shard, axis), dim)


def taken_together(shard, axis):
    return copy_for_each(shard, axis).astype(jnp.float32).sum(axis=0)


def in_blocks(shard, dim, length):
    shape = shard.shape
    parts = shard.reshape(*shape[:dim], length, shape[dim] // length, *shape[dim + 1 :])
    return jnp.moveaxis(parts, dim, 0)


def sent_and_summed(shard, axis, dim):
    parts = in_blocks(shard, dim, lax.axis_size(axis))
    arrived = lax.all_to_all(parts, axis, split_axis=0, concat_axis=0, tiled=True)
    return arrived.astype(jnp.float32).sum(axis=0)


def segment_rows(lengths, row_count):
    positions = jnp.arange(row_count, dtype=jnp.int32)
    bounds = jnp.cumsum(lengths)
    return jnp.sum((positions[:, None] >= bounds[None, :]).astype(jnp.int32), axis=1)


def conv_mix(signal, weight, bias, segment_ids):
    row_count, channel_count = signal.shape
    tap_count = weight.shape[0]
    summed = bias[None, :] + weight[tap_count - 1][None, :] * signal
    for offset in range(1, tap_count):
        earlier = jnp.concatenate(
            [jnp.zeros((offset, channel_count), signal.dtype), signal[: row_count - offset]], axis=0
        )
        earlier_ids = jnp.concatenate(
            [jnp.full((offset,), -1, jnp.int32), segment_ids[: row_count - offset]]
        )
        same_seq = (earlier_ids == segment_ids).astype(signal.dtype)
        summed = summed + weight[tap_count - 1 - offset][None, :] * earlier * same_seq[:, None]
    return jax.nn.silu(summed)


def ssd_scan(values, steps, rates, b_mat, c_mat, skip_gain, segment_ids):
    row_count, head_count, head_width = values.shape
    state_width = b_mat.shape[1]
    block_count = row_count // SPAN
    lower = (jnp.arange(SPAN)[:, None] >= jnp.arange(SPAN)[None, :]).astype(values.dtype)
    highest = lax.Precision.HIGHEST

    def one_block(carry, block):
        state, last_segment = carry
        block_values, block_steps, block_b, block_c, block_ids = block
        log_steps = block_steps * rates[None, :]
        cumulative = jnp.dot(lower, log_steps, precision=highest)
        same_seq = (block_ids[:, None] == block_ids[None, :]) & (lower > 0)
        gaps = cumulative[:, None, :] - cumulative[None, :, :]
        decays = jnp.where(
            same_seq[:, :, None], jnp.exp(jnp.where(same_seq[:, :, None], gaps, 0.0)), 0.0
        )
        scores = jnp.dot(block_c, block_b.T, precision=highest)
        weights = scores[:, :, None] * decays * block_steps[None, :, :]
        inside = jnp.einsum("tsh,shp->thp", weights, block_values, precision=highest)
        carried = (block_ids == last_segment).astype(values.dtype)
        from_state = (
            jnp.einsum("tn,hpn->thp", block_c, state, precision=highest)
            * (carried[:, None] * jnp.exp(cumulative))[:, :, None]
        )
        final_segment = block_ids[SPAN - 1]
        in_final = (block_ids == final_segment)[:, None]
        tails = (
            jnp.where(
                in_final,
                jnp.exp(jnp.where(in_final, cumulative[SPAN - 1][None, :] - cumulative, 0.0)),
                0.0,
            )
            * block_steps
        )
        keeping = (last_segment == final_segment).astype(values.dtype)
        new_state = keeping * jnp.exp(cumulative[SPAN - 1])[:, None, None] * state + jnp.einsum(
            "sh,shp,sn->hpn", tails, block_values, block_b, precision=highest
        )
        output = inside + from_state + skip_gain[None, :, None] * block_values
        return ((new_state, final_segment), output)

    blocks = (
        values.reshape(block_count, SPAN, head_count, head_width),
        steps.reshape(block_count, SPAN, head_count),
        b_mat.reshape(block_count, SPAN, state_width),
        c_mat.reshape(block_count, SPAN, state_width),
        segment_ids.reshape(block_count, SPAN),
    )
    initial = (
        jnp.zeros((head_count, head_width, state_width), values.dtype),
        jnp.array(-1, jnp.int32),
    )
    unused, outputs = lax.scan(jax.checkpoint(one_block), initial, blocks)
    return outputs.reshape(row_count, head_count, head_width)


def term_builder(entries):
    pieces_out = []
    contract_rows = (((0,), (0,)), ((), ()))
    for gathered_rows, d_proj_all, cot_rows, normed_rows in entries:
        pieces_out.append(
            lax.dot_general(
                gathered_rows, d_proj_all, contract_rows, preferred_element_type=jnp.float32
            )
        )
        pieces_out.append(
            lax.dot_general(
                cot_rows, normed_rows, contract_rows, preferred_element_type=jnp.float32
            )
        )
    return jnp.concatenate(pieces_out, axis=1)


def shards(
    x_in,
    cotangent,
    seq_lengths,
    gain_in,
    w_zx,
    w_bc,
    w_dt,
    conv_x,
    conv_bc,
    bias_x,
    bias_bc,
    dt_bias,
    a_log,
    skip,
    gain_gate,
    w_out,
):
    f32 = jnp.float32
    bf16 = jnp.bfloat16
    own_count = x_in.shape[0]
    model_width = x_in.shape[1]
    tp_count = lax.axis_size("tp")
    tp_place = lax.axis_index("tp")
    group_count = own_count * tp_count
    row_start = tp_place * own_count
    layer_count = w_zx.shape[0]
    local_rows = w_zx.shape[1]
    local_inner = w_zx.shape[3]
    local_heads = dt_bias.shape[1]
    head_width = local_inner // local_heads
    pair_width = w_bc.shape[2]
    state_width = pair_width // 2
    segment_ids = segment_rows(seq_lengths[0], group_count)
    live_group = (segment_ids < SEQS).astype(f32)
    live_own = lax.dynamic_slice_in_dim(live_group, row_start, own_count, 0)
    positions = jnp.arange(group_count, dtype=jnp.int32)
    own_flags = ((positions >= row_start) & (positions < row_start + own_count)).astype(f32)

    def widen(part):
        full_shape = part.shape[:-1] + (part.shape[-1] * tp_count,)
        return lax.dynamic_update_slice_in_dim(
            jnp.zeros(full_shape, f32), part, tp_place * part.shape[-1], part.ndim - 1
        )

    def conv_apply(signal_in, weight_in, bias_in):
        return conv_mix(signal_in, weight_in, bias_in, segment_ids)

    def ssd_apply(values_in, raw_in, bias_in, log_in, skip_in, b_in, c_in):
        steps = jax.nn.softplus(raw_in + bias_in[None, :])
        result = ssd_scan(
            values_in.reshape(group_count, local_heads, head_width),
            steps,
            -jnp.exp(log_in),
            b_in,
            c_in,
            skip_in,
            segment_ids,
        )
        return result.reshape(group_count, local_inner)

    hidden = x_in.astype(f32)
    saved = []
    for layer_index in range(layer_count):
        gain_norm = gain_in[layer_index].astype(f32)
        scale = lax.rsqrt(jnp.mean(hidden * hidden, axis=1) + EPS)
        normed_own = (hidden * scale[:, None] * gain_norm[None, :]).astype(bf16)
        gathered = lax.all_gather(normed_own, "tp", axis=0, tiled=True)

        def add_rows(totals, pieces, first_row, gathered=gathered):
            piece_zx, piece_bc, piece_dt = pieces
            count = piece_zx.shape[0]
            return (
                jnp.dot(
                    gathered, piece_zx.reshape(count, 2 * local_inner), preferred_element_type=f32
                ),
                jnp.dot(gathered, piece_bc, preferred_element_type=f32),
                jnp.dot(gathered, piece_dt, preferred_element_type=f32),
            )

        starting = (
            jnp.zeros((group_count, 2 * local_inner), f32),
            jnp.zeros((group_count, pair_width), f32),
            jnp.zeros((group_count, local_heads), f32),
        )
        proj_zx, proj_bc, proj_dt = add_rows(
            starting,
            (
                lax.all_gather(w_zx[layer_index], "fsdp", axis=0, tiled=True),
                lax.all_gather(w_bc[layer_index], "fsdp", axis=0, tiled=True),
                lax.all_gather(w_dt[layer_index], "fsdp", axis=0, tiled=True),
            ),
            jnp.int32(0),
        )
        proj_zx = proj_zx.astype(bf16)
        proj_bc = proj_bc.astype(bf16)
        proj_dt = proj_dt.astype(bf16)
        gate_pre = proj_zx[:, :local_inner].astype(f32)
        signal = jnp.concatenate([proj_zx[:, local_inner:], proj_bc], axis=1).astype(f32)
        conv_weight = jnp.concatenate([conv_x[layer_index], conv_bc[layer_index]], axis=1).astype(
            f32
        )
        conv_bias = jnp.concatenate([bias_x[layer_index], bias_bc[layer_index]]).astype(f32)
        activated, conv_back = jax.vjp(conv_apply, signal, conv_weight, conv_bias)
        rounded = lax.optimization_barrier(activated.astype(bf16)).astype(f32)
        values = rounded[:, :local_inner]
        b_mat = rounded[:, local_inner : local_inner + state_width]
        c_mat = rounded[:, local_inner + state_width :]
        ssd_out, ssd_back = jax.vjp(
            ssd_apply,
            values,
            proj_dt.astype(f32),
            dt_bias[layer_index].astype(f32),
            a_log[layer_index].astype(f32),
            skip[layer_index].astype(f32),
            b_mat,
            c_mat,
        )
        gated = ssd_out * jax.nn.silu(gate_pre)
        squares = lax.psum(jnp.sum(gated * gated, axis=1), "tp")
        gate_scale = lax.rsqrt(squares / INNER + EPS)
        gain_inner = gain_gate[layer_index].astype(f32)
        normed_gate = (gated * gate_scale[:, None] * gain_inner[None, :]).astype(bf16)

        def project_cols(weight_piece, first_row, normed_gate=normed_gate):
            return jnp.dot(normed_gate, weight_piece, preferred_element_type=f32)

        partial_mix = project_cols(gather_directly(w_out[layer_index], "fsdp", 1), jnp.int32(0))
        mixed_own = lax.psum_scatter(partial_mix, "tp", scatter_dimension=0, tiled=True)
        saved.append(
            (
                hidden,
                scale,
                gathered,
                conv_back,
                ssd_back,
                ssd_out,
                gate_pre,
                gated,
                gate_scale,
                normed_gate,
            )
        )
        hidden = hidden + live_own[:, None] * mixed_own
    act_out = hidden.astype(bf16)
    grad_hidden = cotangent.astype(f32)
    weight_sums = [None] * layer_count
    small_terms = [None] * layer_count
    kept_terms = [None] * layer_count
    contract_cols = (((1,), (1,)), ((), ()))
    for layer_index in reversed(range(layer_count)):
        (
            hidden_in,
            scale,
            gathered,
            conv_back,
            ssd_back,
            ssd_out,
            gate_pre,
            gated,
            gate_scale,
            normed_gate,
        ) = saved[layer_index]
        cot_own = (live_own[:, None] * grad_hidden).astype(bf16)
        cot_all = lax.all_gather(cot_own, "tp", axis=0, tiled=True)

        def add_back(totals, weight_piece, first_row, cot_all=cot_all):
            count = weight_piece.shape[1]
            return lax.dot_general(cot_all, weight_piece, contract_cols, preferred_element_type=f32)

        d_normed_gate = add_back(
            jnp.zeros((group_count, local_inner), f32),
            lax.all_gather(w_out[layer_index], "fsdp", axis=1, tiled=True),
            jnp.int32(0),
        )
        gain_inner = gain_gate[layer_index].astype(f32)
        weighted_gate = d_normed_gate * gain_inner[None, :]
        d_gain_gate = jnp.sum(d_normed_gate * gated * gate_scale[:, None], axis=0)
        inner_dot = lax.psum(jnp.sum(weighted_gate * gated, axis=1), "tp")
        d_gated = (
            gate_scale[:, None] * weighted_gate
            - gated * (gate_scale * gate_scale * gate_scale * inner_dot / INNER)[:, None]
        )
        sigmoid_gate = jax.nn.sigmoid(gate_pre)
        d_ssd_out = d_gated * jax.nn.silu(gate_pre)
        d_gate_pre = d_gated * ssd_out * sigmoid_gate * (1.0 + gate_pre * (1.0 - sigmoid_gate))
        d_values, d_raw, d_dt_bias, d_a_log, d_skip, d_b_mat, d_c_mat = ssd_back(d_ssd_out)
        d_signal, d_conv_weight, d_conv_bias = conv_back(
            jnp.concatenate([d_values, d_b_mat, d_c_mat], axis=1)
        )
        d_pair = taken_together(d_signal[:, local_inner:].astype(jnp.bfloat16), "tp").astype(
            jnp.float32
        )
        d_proj_zx = jnp.concatenate([d_gate_pre, d_signal[:, :local_inner]], axis=1).astype(bf16)
        d_proj_bc = d_pair.astype(bf16)
        d_proj_dt = d_raw.astype(bf16)
        d_pair_own = d_proj_bc * own_flags[:, None].astype(bf16)

        def back_cols(
            pieces, first_row, d_proj_zx=d_proj_zx, d_pair_own=d_pair_own, d_proj_dt=d_proj_dt
        ):
            piece_zx, piece_bc, piece_dt = pieces
            count = piece_zx.shape[0]
            return (
                lax.dot_general(
                    d_proj_zx,
                    piece_zx.reshape(count, 2 * local_inner),
                    contract_cols,
                    preferred_element_type=f32,
                )
                + lax.dot_general(d_pair_own, piece_bc, contract_cols, preferred_element_type=f32)
                + lax.dot_general(d_proj_dt, piece_dt, contract_cols, preferred_element_type=f32)
            )

        d_normed_part = back_cols(
            lax.all_gather(
                (w_zx[layer_index], w_bc[layer_index], w_dt[layer_index]),
                "fsdp",
                axis=0,
                tiled=True,
            ),
            jnp.int32(0),
        )
        d_normed = sent_and_summed(d_normed_part.astype(jnp.bfloat16), "tp", 0)
        gain_norm = gain_in[layer_index].astype(f32)
        weighted_norm = d_normed * gain_norm[None, :]
        d_gain_norm = jnp.sum(d_normed * hidden_in * scale[:, None], axis=0)
        grad_hidden = (
            grad_hidden
            + scale[:, None] * weighted_norm
            - hidden_in
            * (scale * scale * scale * jnp.sum(weighted_norm * hidden_in, axis=1) / model_width)[
                :, None
            ]
        )
        kept_terms[layer_index] = (
            gathered,
            jnp.concatenate([d_proj_zx, d_proj_bc, d_proj_dt], axis=1),
            cot_all,
            normed_gate,
        )
        small_terms[layer_index] = (
            d_gain_norm,
            widen(d_conv_weight[:, :local_inner]),
            d_conv_weight[:, local_inner:],
            widen(d_conv_bias[:local_inner]),
            d_conv_bias[local_inner:],
            widen(jnp.stack([d_dt_bias, d_a_log, d_skip])),
            widen(d_gain_gate),
        )
    joined = lax.psum_scatter(term_builder(kept_terms), "fsdp", scatter_dimension=0, tiled=True)
    block_width = joined.shape[1] // layer_count
    weight_sums = [
        joined[:, layer_index * block_width : (layer_index + 1) * block_width]
        for layer_index in range(layer_count)
    ]
    zx_end = 2 * local_inner
    bc_end = zx_end + pair_width
    dt_end = bc_end + local_heads
    grad_w_zx = jnp.stack(
        [block[:, :zx_end].reshape(local_rows, 2, local_inner) for block in weight_sums]
    )
    grad_w_bc = jnp.stack([block[:, zx_end:bc_end] for block in weight_sums])
    grad_w_dt = jnp.stack([block[:, bc_end:dt_end] for block in weight_sums])
    grad_w_out = jnp.stack([block[:, dt_end:].T for block in weight_sums])
    gains_all = jnp.stack([entry[0] for entry in small_terms])
    taps_x_all = jnp.stack([entry[1] for entry in small_terms])
    taps_bc_all = jnp.stack([entry[2] for entry in small_terms])
    shift_x_all = jnp.stack([entry[3] for entry in small_terms])
    shift_bc_all = jnp.stack([entry[4] for entry in small_terms])
    heads_all = jnp.stack([entry[5] for entry in small_terms])
    gate_all = jnp.stack([entry[6] for entry in small_terms])
    summed_small = lax.psum(
        (gains_all, taps_x_all, taps_bc_all, shift_x_all, shift_bc_all, heads_all, gate_all),
        ("fsdp", "tp"),
    )
    grad_gain_in = summed_small[0]
    grad_conv_x = lax.dynamic_slice_in_dim(summed_small[1], tp_place * local_inner, local_inner, 2)
    grad_conv_bc = summed_small[2]
    grad_bias_x = lax.dynamic_slice_in_dim(summed_small[3], tp_place * local_inner, local_inner, 1)
    grad_bias_bc = summed_small[4]
    heads_own = lax.dynamic_slice_in_dim(summed_small[5], tp_place * local_heads, local_heads, 2)
    grad_gain_gate = lax.dynamic_slice_in_dim(
        summed_small[6], tp_place * local_inner, local_inner, 1
    )
    return (
        act_out,
        grad_hidden,
        grad_gain_in,
        grad_w_zx,
        grad_w_bc,
        grad_w_dt,
        grad_conv_x,
        grad_conv_bc,
        grad_bias_x,
        grad_bias_bc,
        heads_own[:, 0],
        heads_own[:, 1],
        heads_own[:, 2],
        grad_gain_gate,
        grad_w_out,
    )


def solution(mesh):
    placed = (
        P(("fsdp", "tp"), None),
        P(("fsdp", "tp"), None),
        P("fsdp", None),
        P(),
        P(None, "fsdp", None, "tp"),
        P(None, "fsdp", None),
        P(None, "fsdp", "tp"),
        P(None, None, "tp"),
        P(),
        P(None, "tp"),
        P(),
        P(None, "tp"),
        P(None, "tp"),
        P(None, "tp"),
        P(None, "tp"),
        P(None, "tp", "fsdp"),
    )
    return jax.shard_map(
        shards,
        mesh=mesh,
        in_specs=placed,
        out_specs=(
            P(("fsdp", "tp"), None),
            P(("fsdp", "tp"), None),
            P(),
            P(None, "fsdp", None, "tp"),
            P(None, "fsdp", None),
            P(None, "fsdp", "tp"),
            P(None, None, "tp"),
            P(),
            P(None, "tp"),
            P(),
            P(None, "tp"),
            P(None, "tp"),
            P(None, "tp"),
            P(None, "tp"),
            P(None, "tp", "fsdp"),
        ),
        check_vma=False,
    )
```

profile of v0, /device:TPU:0, one launch (start us, length us, event | category | flops | bytes accessed | tf_op | source)
XLA Modules:
  0.0 1194.5 jit_solution(16386980826223418317)
XLA Ops:
  12.8 9.8 all-to-all-start
  23.5 100.9 %all-gather.2 = bf16[1,1024,16]{2,1,0:T(8,128)(2,1)S(1)} all-gather(bf16[1,16,16]{2,1,0:T(8,128)(2,1)S(1)} %get-tuple-element.662), channel_id=4, replica_groups=mesh['fsdp'=64,'tp'=2] {'fsdp'}, dimensions={1}, use_global_device_ids=true | all-gather | bytes 33280 | tf_op jit(solution)/shard_map/all_gather | solution.py:233
  128.0 11.3 all_gather.42
  144.7 78.1 %all-gather.1 = bf16[1,1024,256]{2,1,0:T(8,128)(2,1)S(1)} all-gather(bf16[1,16,256]{2,1,0:T(8,128)(2,1)S(1)} %get-tuple-element.660), channel_id=3, replica_groups=mesh['fsdp'=64,'tp'=2] {'fsdp'}, dimensions={1}, use_global_device_ids=true | all-gather | bytes 532480 | tf_op jit(solution)/shard_map/all_gather | solution.py:232
  223.2 3.7 copy.375
  235.2 4.4 fusion.64
  244.6 6.4 psum.77
  251.6 3.3 fusion.265
  256.6 5.7 all-to-all-start.1
  263.1 97.8 %all-gather.5 = bf16[1,1024,16]{2,1,0:T(8,128)(2,1)S(1)} all-gather(bf16[1,16,16]{2,1,0:T(8,128)(2,1)S(1)} %copy-done.132), channel_id=7, replica_groups=mesh['fsdp'=64,'tp'=2] {'fsdp'}, dimensions={1}, use_global_device_ids=true | all-gather | bytes 33280 | tf_op jit(solution)/shard_map/all_gather | solution.py:233
  360.9 78.6 %all-gather.4 = bf16[1,1024,256]{2,1,0:T(8,128)(2,1)S(1)} all-gather(bf16[1,16,256]{2,1,0:T(8,128)(2,1)S(1)} %copy-done.115), channel_id=6, replica_groups=mesh['fsdp'=64,'tp'=2] {'fsdp'}, dimensions={1}, use_global_device_ids=true | all-gather | bytes 532480 | tf_op jit(solution)/shard_map/all_gather | solution.py:232
  439.6 5.7 copy.376
  448.2 10.7 all_gather.46
  458.9 3.6 convolution_convert_fusion
  474.6 3.3 fusion.67
  485.6 6.4 psum.78
  492.1 3.7 fusion.267
  500.2 15.8 %all_gather.50 = bf16[256,1024]{1,0:T(8,128)(2,1)S(1)} all-gather(bf16[128,1024]{1,0:T(8,128)(2,1)} %get-tuple-element.683), channel_id=1, replica_groups=mesh['fsdp'=64,'tp'=2] {'tp'}, dimensions={0}, use_global_device_ids=true | all-gather | bytes 786432 | tf_op jit(solution)/shard_map/all_gather | solution.py:307
  516.0 4.4 multiply_reduce_fusion.12
  520.5 6.9 psum.79
  528.0 3.8 fusion.121
  539.9 2.9 fusion.104
  550.3 8.1 fusion.27
  558.5 4.8 fusion.79
  569.8 3.2 convolution_bitcast_fusion.2
  588.4 4.9 all-to-all-start.2
  596.5 3.0 fusion.266
  608.1 4.9 all-to-all-start.3
  613.1 6.3 fusion.96
  627.0 8.6 all_gather.52
  635.6 4.1 multiply_reduce_fusion.13
  639.8 7.1 psum.80
  647.6 3.5 fusion.115
  660.6 2.9 fusion.105
  670.8 7.9 fusion.29
  678.8 4.8 fusion.76
  690.2 3.2 convolution_bitcast_fusion
  699.8 2.9 fusion.264
  703.6 3.4 all-to-all-start.4
  708.9 4.8 all-to-all-done.4
  713.8 5.1 fusion.88
  718.9 19.6 %pad_maximum_fusion = f32[1024,6688]{0,1:T(8,128)} fusion(f32[1024,1024]{0,1:T(8,128)} %fusion.266, f32[1024,2320]{0,1:T(8,128)} %fusion.96, f32[1024,1024]{0,1:T(8,128)} %fusion.264, f32[1024,2320]{0,1:T(8,128)} %fusion.88), kind=kLoop, calls=%fused_computation | loop fusion | flops 20545536 | bytes 54788096 | tf_op jit(solution)/shard_map/concatenate | solution.py:140
  738.5 26.7 %copy.363 = f32[1024,6688]{1,0:T(8,128)} copy(f32[1024,6688]{0,1:T(8,128)} %pad_maximum_fusion) | data formatting | bytes 54788096
  767.2 3.5 fusion.126
  771.9 3.6 all-to-all-start.5
  775.6 70.0 %all-reduce.29.cloned.1.call-done = f32[2,4,2048]{2,1,0:T(4,128)} async-done(((f32[2,4,2048]{2,1,0:T(4,128)}), f32[2,4,2048]{2,1,0:T(4,128)}) %all-reduce.29.cloned.1.call-update) | async-done | bytes 65552 | tf_op jit(solution)/shard_map/psum | solution.py:415
  847.3 68.0 %all-reduce.26 = (f32[2,1024]{1,0:T(2,128)}, f32[2,4,256]{2,1,0:T(4,128)}, f32[2,2048]{1,0:T(2,128)S(1)}, f32[2,256]{1,0:T(2,128)}, f32[2,3,32]{2,0,1:T(2,128)S(1)}, /*index=5*/f32[2,2048]{1,0:T(2,128)S(1)}) all-reduce(f32[2,1024]{1,0:T(2,128)S(1)} %pad_maximum_fusion.10, ...), channel_id=1, replica_groups=mesh['fsdp'=64,'tp'=2] {'fsdp','tp'}, use_global_device_ids=true, to_apply=%region_36.38 | all-reduce | flops 12992 | bytes 103936 | tf_op jit(solution)/shard_map/psum | solution.py:415
  918.3 260.8 %reduce-scatter.10.cloned.1.call-done = f32[16,6688]{1,0:T(8,128)} async-done(((f32[1024,6688]{1,0:T(8,128)}), f32[16,6688]{1,0:T(8,128)}) %reduce-scatter.10.cloned.1.call-update) | async-done | bytes 428048
  (608 shorter events, 163.0 us)
Async XLA Ops:
  7.2 216.0 %all-gather.13.cloned.1.call-start = ((), (), s32[]{:S(2)}) async-start(), calls=%async_computation.12 | async-start | bytes 4259840 | tf_op jit(solution)/shard_map/all_gather | solution.py:231
  8.9 430.7 %all-gather.15.cloned.1.call-start = ((), (), s32[]{:S(2)}) async-start(), calls=%async_computation.13 | async-start | bytes 4259840 | tf_op jit(solution)/shard_map/all_gather | solution.py:231
  12.7 111.7 %copy-start.158 = (bf16[2,256]{1,0:T(2,128)(2,1)S(1)}, bf16[2,256]{1,0:T(2,128)(2,1)}, u32[]{:S(2)}) copy-start(bf16[2,256]{1,0:T(2,128)(2,1)} %param.27) | copy-start | bytes 3076
  12.7 112.3 %copy-start.133 = (bf16[2,1024]{1,0:T(2,128)(2,1)S(1)}, bf16[2,1024]{1,0:T(2,128)(2,1)}, u32[]{:S(2)}) copy-start(bf16[2,1024]{1,0:T(2,128)(2,1)} %param.26) | copy-start | bytes 12292
  12.7 113.0 %copy-start.159 = (bf16[2,4,256]{2,1,0:T(4,128)(2,1)S(1)}, bf16[2,4,256]{2,1,0:T(4,128)(2,1)}, u32[]{:S(2)}) copy-start(bf16[2,4,256]{2,1,0:T(4,128)(2,1)} %param.25) | copy-start | bytes 12292
  12.7 113.0 %copy-start.134 = (bf16[2,4,1024]{2,1,0:T(4,128)(2,1)S(1)}, bf16[2,4,1024]{2,1,0:T(4,128)(2,1)}, u32[]{:S(2)}) copy-start(bf16[2,4,1024]{2,1,0:T(4,128)(2,1)} %param.24) | copy-start | bytes 49156
  12.8 113.7 %copy-start.29 = (bf16[128,1024]{1,0:T(8,128)(2,1)S(1)}, bf16[128,1024]{1,0:T(8,128)(2,1)}, u32[]{:S(2)}) copy-start(bf16[128,1024]{1,0:T(8,128)(2,1)} %param.17) | copy-start | bytes 786436
  12.8 114.5 %copy-start.136 = (bf16[2,1024]{1,0:T(2,128)(2,1)S(1)}, bf16[2,1024]{1,0:T(2,128)(2,1)}, u32[]{:S(2)}) copy-start(bf16[2,1024]{1,0:T(2,128)(2,1)} %param.20) | copy-start | bytes 12292
  12.8 238.3 %all-to-all-start = ((bf16[64,1024,16]{1,2,0:T(8,128)(2,1)}), bf16[64,1024,16]{1,2,0:T(8,128)(2,1)}, u32[]{:S(2)}, u32[]{:S(2)}) async-start(bf16[64,1024,16]{1,2,0:T(8,128)(2,1)} %broadcast_in_dim.406), calls=%async_computation | async-start | bytes 4194304 | tf_op jit(solution)/shard_map/all_to_all | solution.py:22
  22.6 116.7 %copy-start.168 = (bf16[2,16]{1,0:T(2,128)(2,1)S(1)}, bf16[2,16]{1,0:T(2,128)(2,1)}, u32[]{:S(2)}) copy-start(bf16[2,16]{1,0:T(2,128)(2,1)} %param.28) | copy-start | bytes 196
  22.6 117.3 %copy-start.169 = (bf16[2,16]{1,0:T(2,128)(2,1)S(1)}, bf16[2,16]{1,0:T(2,128)(2,1)}, u32[]{:S(2)}) copy-start(bf16[2,16]{1,0:T(2,128)(2,1)} %param.30) | copy-start | bytes 196
  22.6 117.8 %copy-start.144 = (bf16[2,16]{1,0:T(2,128)(2,1)S(1)}, bf16[2,16]{1,0:T(2,128)(2,1)}, u32[]{:S(2)}) copy-start(bf16[2,16]{1,0:T(2,128)(2,1)} %param.29) | copy-start | bytes 196
  22.6 118.9 %copy-start.137 = (bf16[2,1024]{1,0:T(2,128)(2,1)S(1)}, bf16[2,1024]{1,0:T(2,128)(2,1)}, u32[]{:S(2)}) copy-start(bf16[2,1024]{1,0:T(2,128)(2,1)} %param.31) | copy-start | bytes 12292
  22.6 119.5 %copy-start.135 = (bf16[2,16,256]{2,1,0:T(8,128)(2,1)S(1)}, bf16[2,16,256]{2,1,0:T(8,128)(2,1)}, u32[]{:S(2)}) copy-start(bf16[2,16,256]{2,1,0:T(8,128)(2,1)} %param.22) | copy-start | bytes 49156
  22.6 422.7 %reduce-scatter.6.cloned.1.call-start = ((), (), s32[]{:S(2)}) async-start(), calls=%async_computation.9 | async-start | bytes 1572864 | tf_op jit(solution)/shard_map/reduce_scatter | solution.py:271
  126.5 103.4 %copy-start.84 = (f32[1280]{0:T(1024)}, f32[1280]{0:T(1024)S(1)}, u32[]{:S(2)}) copy-start(f32[1280]{0:T(1024)S(1)} %get-tuple-element.573) | copy-start | bytes 15364
  126.5 103.3 %copy-start.86 = (f32[1280]{0:T(1024)}, f32[1280]{0:T(1024)S(1)}, u32[]{:S(2)}) copy-start(f32[1280]{0:T(1024)S(1)} %get-tuple-element.576) | copy-start | bytes 15364
  126.5 103.3 %copy-start.88 = (f32[1280]{0:T(1024)}, f32[1280]{0:T(1024)S(1)}, u32[]{:S(2)}) copy-start(f32[1280]{0:T(1024)S(1)} %get-tuple-element.575) | copy-start | bytes 15364
  126.5 103.3 %copy-start.90 = (f32[1280]{0:T(1024)}, f32[1280]{0:T(1024)S(1)}, u32[]{:S(2)}) copy-start(f32[1280]{0:T(1024)S(1)} %get-tuple-element.574) | copy-start | bytes 15364
  127.8 94.9 %copy-start.101 = (f32[1,1024]{1,0:T(1,128)}, f32[1,1024]{1,0:T(1,128)S(1)}, u32[]{:S(2)}) copy-start(f32[1,1024]{1,0:T(1,128)S(1)} %get-tuple-element.668) | copy-start | bytes 12292
  141.5 88.3 %copy-start.118 = (f32[256]{0:T(256)}, f32[256]{0:T(256)S(1)}, u32[]{:S(2)}) copy-start(f32[256]{0:T(256)S(1)} %get-tuple-element.679) | copy-start | bytes 3076
  141.5 88.3 %copy-start.122 = (f32[256]{0:T(256)}, f32[256]{0:T(256)S(1)}, u32[]{:S(2)}) copy-start(f32[256]{0:T(256)S(1)} %get-tuple-element.680) | copy-start | bytes 3076
  141.5 88.3 %copy-start.126 = (f32[256]{0:T(256)}, f32[256]{0:T(256)S(1)}, u32[]{:S(2)}) copy-start(f32[256]{0:T(256)S(1)} %get-tuple-element.678) | copy-start | bytes 3076
  256.6 104.3 %copy-start.115 = (bf16[1,16,256]{2,1,0:T(8,128)(2,1)S(1)}, bf16[1,16,256]{2,1,0:T(8,128)(2,1)}, u32[]{:S(2)}) copy-start(bf16[1,16,256]{2,1,0:T(8,128)(2,1)} %get-tuple-element.659) | copy-start | bytes 24580
  256.6 182.9 %copy-start.179 = (f32[256]{0:T(256)S(1)}, f32[256]{0:T(256)}, u32[]{:S(2)}) copy-start(f32[256]{0:T(256)} %get-tuple-element.676) | copy-start | bytes 3076
  256.6 183.0 %copy-start.147 = (bf16[1024]{0:T(1024)(128)(2,1)S(1)}, bf16[1024]{0:T(1024)(128)(2,1)}, u32[]{:S(2)}) copy-start(bf16[1024]{0:T(1024)(128)(2,1)} %get-tuple-element.577) | copy-start | bytes 6148
  256.6 183.0 %copy-start.170 = (bf16[256]{0:T(256)(128)(2,1)S(1)}, bf16[256]{0:T(256)(128)(2,1)}, u32[]{:S(2)}) copy-start(bf16[256]{0:T(256)(128)(2,1)} %get-tuple-element.579) | copy-start | bytes 1540
  256.6 235.5 %all-to-all-start.1 = ((bf16[64,1024,16]{1,2,0:T(8,128)(2,1)}), bf16[64,1024,16]{1,2,0:T(8,128)(2,1)}, u32[]{:S(2)}, u32[]{:S(2)}) async-start(bf16[64,1024,16]{1,2,0:T(8,128)(2,1)} %broadcast_in_dim.408), calls=%async_computation.2 | async-start | bytes 4194304 | tf_op jit(solution)/shard_map/all_to_all | solution.py:22
  262.3 253.7 %all-gather.17.cloned.1.call-start = ((), (), s32[]{:S(2)}) async-start(), calls=%async_computation.14 | async-start | bytes 2129920 | tf_op jit(solution)/shard_map/all_gather | solution.py:315
  262.9 361.7 %reduce-scatter.8.cloned.1.call-start = ((), (), s32[]{:S(2)}) async-start(), calls=%async_computation.10 | async-start | bytes 1572864 | tf_op jit(solution)/shard_map/reduce_scatter | solution.py:271
  263.0 200.6 %copy-start.92 = (f32[1280]{0:T(1024)}, f32[1280]{0:T(1024)S(1)}, u32[]{:S(2)}) copy-start(f32[1280]{0:T(1024)S(1)} %get-tuple-element.569) | copy-start | bytes 15364
  263.0 200.6 %copy-start.94 = (f32[1280]{0:T(1024)}, f32[1280]{0:T(1024)S(1)}, u32[]{:S(2)}) copy-start(f32[1280]{0:T(1024)S(1)} %get-tuple-element.572) | copy-start | bytes 15364
  263.0 200.6 %copy-start.96 = (f32[1280]{0:T(1024)}, f32[1280]{0:T(1024)S(1)}, u32[]{:S(2)}) copy-start(f32[1280]{0:T(1024)S(1)} %get-tuple-element.571) | copy-start | bytes 15364
  263.0 200.6 %copy-start.98 = (f32[1280]{0:T(1024)}, f32[1280]{0:T(1024)S(1)}, u32[]{:S(2)}) copy-start(f32[1280]{0:T(1024)S(1)} %get-tuple-element.570) | copy-start | bytes 15364
  360.9 112.0 %copy-start.47 = (bf16[1,1024,16]{2,1,0:T(8,128)(2,1)}, bf16[1,1024,16]{2,1,0:T(8,128)(2,1)S(1)}, u32[]{:S(2)}) copy-start(bf16[1,1024,16]{2,1,0:T(8,128)(2,1)S(1)} %all-gather.5) | copy-start | bytes 98308
  495.8 139.9 %all-gather.19.cloned.1.call-start = ((), (), s32[]{:S(2)}) async-start(), calls=%async_computation.15 | async-start | bytes 2129920 | tf_op jit(solution)/shard_map/all_gather | solution.py:315
  588.4 15.6 %all-to-all-start.2 = ((bf16[2,256,256]{2,1,0:T(8,128)(2,1)}), bf16[2,256,256]{2,1,0:T(8,128)(2,1)}, u32[]{:S(2)}, u32[]{:S(2)}) async-start(bf16[2,256,256]{2,1,0:T(8,128)(2,1)} %broadcast_in_dim.412), calls=%async_computation.4 | async-start | bytes 524288 | tf_op jit(solution)/shard_map/all_to_all | solution.py:22
  608.1 13.3 %all-to-all-start.3 = ((bf16[2,128,1024]{2,1,0:T(8,128)(2,1)}), bf16[2,128,1024]{2,1,0:T(8,128)(2,1)}, u32[]{:S(2)}, u32[]{:S(2)}) async-start(bf16[2,128,1024]{2,1,0:T(8,128)(2,1)} %bitcast.336), calls=%async_computation.5 | async-start | bytes 1048576 | tf_op jit(solution)/shard_map/all_to_all | solution.py:43
  703.6 10.1 all-to-all-start.4
  707.1 138.6 %all-reduce.29.cloned.1.call-start = ((), (), s32[]{:S(2)}) async-start(), calls=%async_computation.11 | async-start | bytes 131072 | tf_op jit(solution)/shard_map/psum | solution.py:415
  708.6 470.6 %reduce-scatter.10.cloned.1.call-start = ((), (), s32[]{:S(2)}) async-start(), calls=%async_computation.16 | async-start | bytes 28221440
  771.9 145.3 %copy-start.181 = (f32[128]{0:T(128)S(1)}, f32[128]{0:T(128)}, u32[]{:S(2)}) copy-start(f32[128]{0:T(128)} %copy-done.180) | copy-start | bytes 1540
  771.9 145.3 %copy-start.25 = (f32[128,1024]{1,0:T(8,128)S(1)}, f32[128,1024]{1,0:T(8,128)}, u32[]{:S(2)}) copy-start(f32[128,1024]{1,0:T(8,128)} %copy-done.24) | copy-start | bytes 1572868
  771.9 145.3 %copy-start.44 = (bf16[128,1024]{1,0:T(8,128)(2,1)S(1)}, bf16[128,1024]{1,0:T(8,128)(2,1)}, u32[]{:S(2)}) copy-start(bf16[128,1024]{1,0:T(8,128)(2,1)} %param.18) | copy-start | bytes 786436
  771.9 145.3 %copy-start.82 = (f32[1,1024]{1,0:T(1,128)S(1)}, f32[1,1024]{1,0:T(1,128)}, u32[]{:S(2)}) copy-start(f32[1,1024]{1,0:T(1,128)} %get-tuple-element.667) | copy-start | bytes 12292
  771.9 145.3 %copy-start.143 = (f32[128]{0:T(128)S(1)}, f32[128]{0:T(128)}, u32[]{:S(2)}) copy-start(f32[128]{0:T(128)} %copy-done.142) | copy-start | bytes 1540
  771.9 145.3 %copy-start.160 = (f32[128]{0:T(128)S(1)}, f32[128]{0:T(128)}, u32[]{:S(2)}) copy-start(f32[128]{0:T(128)} %fusion.249) | copy-start | bytes 1540
  771.9 75.1 %all-to-all-start.5 = ((bf16[2,128,1024]{2,1,0:T(8,128)(2,1)}), bf16[2,128,1024]{2,1,0:T(8,128)(2,1)S(1)}, u32[]{:S(2)}, u32[]{:S(2)}) async-start(bf16[2,128,1024]{2,1,0:T(8,128)(2,1)} %bitcast.65), calls=%async_computation.7 | async-start | bytes 1048576 | tf_op jit(solution)/shard_map/all_to_all | solution.py:43
  (151 other events, 1362.0 us)
Sparse Core Ops, SparseCore 0:
  10.3 122.1 all-gather.12
  134.8 105.9 all-gather.14
  255.1 45.0 reduce-scatter.5
  301.9 102.1 all-gather.16
  495.9 25.7 reduce-scatter.7
  523.9 99.3 all-gather.18
  713.2 132.3 all-reduce.28
  848.2 330.9 reduce-scatter.9
where the time goes:
time: 1200 us; the launch traced here: 1190 us
  blocking collectives  497 us (41%)
  waiting for transfers between devices  340 us (28%)
  matrix products  121 us (10%)
  local copies, waits for them, and re-layouts  112 us (9%)
  other arithmetic  73.5 us (6%)
  starting transfers between devices  33 us (3%)
  between operations  18 us (2%)
    unnamed x9, waiting for transfers between devices  263 us
    all_gather x2, blocking collectives, shards(): lax.all_gather(w_dt[layer_index], 'fsdp', axis=0, tiled=True)  199 us
    all_gather x2, blocking collectives, shards(): lax.all_gather(w_bc[layer_index], 'fsdp', axis=0, tiled=True)  157 us
    psum x1, waiting for transfers between devices, shards(): lax.psum((gains_all, taps_x_all, taps_bc_all, shift_x_all, shift_bc_all,...  70 us
    psum x1, blocking collectives, shards(): lax.psum((gains_all, taps_x_all, taps_bc_all, shift_x_all, shift_bc_all,...  68 us
    unnamed x383, local copies, waits for them, and re-layouts  51.6 us
    dot_general x6, matrix products, one_block(): jnp.einsum('tsh,shp->thp', weights, block_values, precision=highest)  33.4 us
    all_gather x2, blocking collectives, shards(): cot_all = lax.all_gather(cot_own, 'tp', axis=0, tiled=True)  24.5 us
  transfers between devices with their start and end apart: 14, of which 4 were waited for; matrix products, arithmetic and copies ran while one was open for 19% of the time, Pallas kernels for 0%

commit v1 on v0

--- a/solution.py
+++ b/solution.py
@@ -1,7 +1,13 @@
+import functools
+
 import jax
 import jax.numpy as jnp
 from jax import lax
+from jax.experimental import pallas as pl
+from jax.experimental.pallas import tpu as pltpu
 from jax.sharding import PartitionSpec as P
+
+MESH = pl.DeviceIdType.MESH
 
 SPAN = 256
 SEQS = 4
@@ -42,6 +48,298 @@
     parts = in_blocks(shard, dim, lax.axis_size(axis))
     arrived = lax.all_to_all(parts, axis, split_axis=0, concat_axis=0, tiled=True)
     return arrived.astype(jnp.float32).sum(axis=0)
+
+
+def place():
+    index = lax.axis_index("fsdp")
+    return index // 16, (index // 8) % 2, (index // 2) % 4, index % 2
+
+
+def index_of(y, z, x, c):
+    return ((y * 2 + z) * 4 + x) * 2 + c
+
+
+PLANE_ZX = [(dz, dx) for dz in range(2) for dx in range(4) if (dz, dx) != (0, 0)]
+PLANE_YZ = [(dy, dz) for dy in range(4) for dz in range(2) if (dy, dz) != (0, 0)]
+
+
+def peers_of():
+    y, z, x, c = place()
+    found = [index_of(y, (z + dz) % 2, (x + dx) % 4, c) for dz, dx in PLANE_ZX]
+    found += [index_of((y + dy) % 4, (z + dz) % 2, x, c) for dy, dz in PLANE_YZ if dy != 0]
+    found.append(index_of(y, z, x, 1 - c))
+    return found
+
+
+def greet_all(with_tp):
+    barrier = pltpu.get_barrier_semaphore()
+    peers = peers_of()
+    for peer in peers:
+        pl.semaphore_signal(barrier, inc=1, device_id={"fsdp": peer}, device_id_type=MESH)
+    count = len(peers)
+    if with_tp:
+        other = 1 - lax.axis_index("tp")
+        pl.semaphore_signal(barrier, inc=1, device_id={"tp": other}, device_id_type=MESH)
+        count += 1
+    pl.semaphore_wait(barrier, count)
+
+
+def send(src, dst, sems, slot, **where):
+    copy = pltpu.make_async_remote_copy(
+        src_ref=src,
+        dst_ref=dst,
+        send_sem=sems.at[0, slot],
+        recv_sem=sems.at[1, slot],
+        device_id=where,
+        device_id_type=MESH,
+    )
+    copy.start()
+    return copy
+
+
+GATHER_COPIES = 28
+
+
+class Gather:
+    def __init__(self, whole, sems, first, half, end):
+        self.whole, self.sems = whole, sems
+        self.cols = (pl.ds(first, half - first), pl.ds(half, end - half))
+        self.started = []
+
+    def plane(self):
+        y, z, x, c = place()
+        cols_a, cols_b = self.cols
+        self.first = []
+        for slot, (dz, dx) in enumerate(PLANE_ZX):
+            ref = self.whole.at[y, z, x, c, :, cols_a]
+            self.first.append(
+                send(ref, ref, self.sems, slot, fsdp=index_of(y, (z + dz) % 2, (x + dx) % 4, c))
+            )
+        for slot, (dy, dz) in enumerate(PLANE_YZ):
+            ref = self.whole.at[y, z, x, c, :, cols_b]
+            self.first.append(
+                send(ref, ref, self.sems, 7 + slot, fsdp=index_of((y + dy) % 4, (z + dz) % 2, x, c))
+            )
+
+    def line(self):
+        y, z, x, c = place()
+        cols_a, cols_b = self.cols
+        for copy in self.first:
+            copy.wait_recv()
+        self.second = []
+        for step in range(1, 4):
+            ref = self.whole.at[y, :, :, c, :, cols_a]
+            self.second.append(
+                send(ref, ref, self.sems, 14 + step - 1, fsdp=index_of((y + step) % 4, z, x, c))
+            )
+            ref = self.whole.at[:, :, x, c, :, cols_b]
+            self.second.append(
+                send(ref, ref, self.sems, 17 + step - 1, fsdp=index_of(y, z, (x + step) % 4, c))
+            )
+        self.third = []
+        self.hand_over(0)
+
+    def hand_over(self, step):
+        y, z, x, c = place()
+        cols_a, cols_b = self.cols
+        ref = self.whole.at[(y - step + 4) % 4, :, :, c, :, cols_a]
+        self.third.append(send(ref, ref, self.sems, 20 + step, fsdp=index_of(y, z, x, 1 - c)))
+        ref = self.whole.at[:, :, (x - step + 4) % 4, c, :, cols_b]
+        self.third.append(send(ref, ref, self.sems, 24 + step, fsdp=index_of(y, z, x, 1 - c)))
+
+    def core(self):
+        for step in (1, 3, 2):
+            self.second[2 * (step - 1)].wait_recv()
+            self.second[2 * (step - 1) + 1].wait_recv()
+            self.hand_over(step)
+
+    def finish(self):
+        for copy in self.third:
+            copy.wait_recv()
+        for copy in self.first + self.second + self.third:
+            copy.wait_send()
+
+
+REDUCE_COPIES = 21
+
+
+class Reduce:
+    def __init__(self, grad, from_core, from_line_a, from_line_b, from_plane_a, from_plane_b, sems, half, end):
+        self.grad, self.from_core, self.sems = grad, from_core, sems
+        self.line_a, self.line_b = from_line_a, from_line_b
+        self.plane_a, self.plane_b = from_plane_a, from_plane_b
+        self.cols = (pl.ds(0, half), pl.ds(half, end - half))
+
+    def core(self):
+        y, z, x, c = place()
+        self.copies = [
+            send(
+                self.grad.at[:, :, :, 1 - c],
+                self.from_core,
+                self.sems,
+                0,
+                fsdp=index_of(y, z, x, 1 - c),
+            )
+        ]
+
+    def line(self):
+        y, z, x, c = place()
+        cols_a, cols_b = self.cols
+        self.copies[0].wait_recv()
+
+        @pl.loop(0, 32)
+        def _(block):
+            iy, iz, ix = block // 8, (block // 4) % 2, block % 4
+            mine = self.grad[iy, iz, ix, c].astype(jnp.float32)
+            theirs = self.from_core[iy, iz, ix].astype(jnp.float32)
+            self.from_core[iy, iz, ix] = (mine + theirs).astype(jnp.bfloat16)
+
+        self.second = []
+        for step in range(1, 4):
+            to = (y + step) % 4
+            self.second.append(
+                send(
+                    self.from_core.at[to, :, :, :, cols_a],
+                    self.line_a.at[step - 1],
+                    self.sems,
+                    step,
+                    fsdp=index_of(to, z, x, c),
+                )
+            )
+            to = (x + step) % 4
+            self.second.append(
+                send(
+                    self.from_core.at[:, :, to, :, cols_b],
+                    self.line_b.at[step - 1],
+                    self.sems,
+                    3 + step,
+                    fsdp=index_of(y, z, to, c),
+                )
+            )
+
+    def plane(self):
+        y, z, x, c = place()
+        cols_a, cols_b = self.cols
+        for copy in self.second:
+            copy.wait_recv()
+
+        @pl.loop(0, 8)
+        def _(block):
+            iz, ix = block // 4, block % 4
+            total = self.from_core[y, iz, ix, :, cols_a].astype(jnp.float32)
+            for step in range(3):
+                total = total + self.line_a[step, iz, ix].astype(jnp.float32)
+            self.line_a[0, iz, ix] = total.astype(jnp.bfloat16)
+            iy, iz = block // 2, block % 2
+            total = self.from_core[iy, iz, x, :, cols_b].astype(jnp.float32)
+            for step in range(3):
+                total = total + self.line_b[step, iy, iz].astype(jnp.float32)
+            self.line_b[0, iy, iz] = total.astype(jnp.bfloat16)
+
+        self.third = []
+        for slot, (dz, dx) in enumerate(PLANE_ZX):
+            tz, tx = (z + dz) % 2, (x + dx) % 4
+            self.third.append(
+                send(
+                    self.line_a.at[0, tz, tx],
+                    self.plane_a.at[slot],
+                    self.sems,
+                    7 + slot,
+                    fsdp=index_of(y, tz, tx, c),
+                )
+            )
+        for slot, (dy, dz) in enumerate(PLANE_YZ):
+            ty, tz = (y + dy) % 4, (z + dz) % 2
+            self.third.append(
+                send(
+                    self.line_b.at[0, ty, tz],
+                    self.plane_b.at[slot],
+                    self.sems,
+                    14 + slot,
+                    fsdp=index_of(ty, tz, x, c),
+                )
+            )
+
+    def finish(self, out):
+        y, z, x, c = place()
+        cols_a, cols_b = self.cols
+        for copy in self.third:
+            copy.wait_recv()
+        total = self.line_a[0, z, x].astype(jnp.float32)
+        for slot in range(7):
+            total = total + self.plane_a[slot].astype(jnp.float32)
+        out[:, cols_a] = total
+        total = self.line_b[0, y, z].astype(jnp.float32)
+        for slot in range(7):
+            total = total + self.plane_b[slot].astype(jnp.float32)
+        out[:, cols_b] = total
+        for copy in self.copies + self.second + self.third:
+            copy.wait_send()
+
+ZX, PAIR, DT, OUT = 2048, 256, 128, 1024
+COLS = ZX + PAIR + DT + OUT
+IN_COLS = ZX + PAIR + DT
+
+
+def gather_kernel(own, out, sems, local_sem):
+    y, z, x, c = place()
+    keep = pltpu.make_async_copy(own, out.at[y, z, x, c], local_sem)
+    keep.start()
+    greet_all(False)
+    keep.wait()
+    width = out.shape[-1]
+    job = Gather(out, sems, 0, width // 2, width)
+    job.plane()
+    job.line()
+    job.core()
+    job.finish()
+
+
+def gather_rows(own):
+    return pl.pallas_call(
+        gather_kernel,
+        out_shape=jax.ShapeDtypeStruct((4, 2, 4, 2, *own.shape), own.dtype),
+        in_specs=[pl.BlockSpec(memory_space=pltpu.VMEM)],
+        out_specs=pl.BlockSpec(memory_space=pltpu.VMEM),
+        scratch_shapes=[pltpu.SemaphoreType.DMA((2, GATHER_COPIES)), pltpu.SemaphoreType.DMA],
+        compiler_params=pltpu.CompilerParams(
+            collective_id=0, has_side_effects=True, vmem_limit_bytes=40 << 20
+        ),
+        name="gather_rows",
+    )(own)
+
+
+def reduce_kernel(grad, out, from_core, line_a, line_b, plane_a, plane_b, sems):
+    greet_all(False)
+    width = grad.shape[-1]
+    job = Reduce(grad, from_core, line_a, line_b, plane_a, plane_b, sems, width // 2, width)
+    job.core()
+    job.line()
+    job.plane()
+    job.finish(out)
+
+
+def reduce_rows(grad):
+    rows, width = grad.shape[-2:]
+    half = width // 2
+    return pl.pallas_call(
+        reduce_kernel,
+        out_shape=jax.ShapeDtypeStruct((rows, width), jnp.float32),
+        in_specs=[pl.BlockSpec(memory_space=pltpu.VMEM)],
+        out_specs=pl.BlockSpec(memory_space=pltpu.VMEM),
+        scratch_shapes=[
+            pltpu.VMEM((4, 2, 4, rows, width), jnp.bfloat16),
+            pltpu.VMEM((3, 2, 4, rows, half), jnp.bfloat16),
+            pltpu.VMEM((3, 4, 2, rows, width - half), jnp.bfloat16),
+            pltpu.VMEM((7, rows, half), jnp.bfloat16),
+            pltpu.VMEM((7, rows, width - half), jnp.bfloat16),
+            pltpu.SemaphoreType.DMA((2, REDUCE_COPIES)),
+        ],
+        compiler_params=pltpu.CompilerParams(
+            collective_id=1, has_side_effects=True, vmem_limit_bytes=40 << 20
+        ),
+        name="reduce_rows",
+    )(grad)
 
 
 def segment_rows(lengths, row_count):
@@ -203,6 +501,17 @@
 
     hidden = x_in.astype(f32)
     saved = []
+    packed = jnp.concatenate(
+        [
+            w_zx.reshape(layer_count, local_rows, 2 * local_inner),
+            w_bc,
+            jnp.pad(w_dt, ((0, 0), (0, 0), (0, DT - local_heads))),
+            jnp.swapaxes(w_out, 1, 2),
+        ],
+        axis=2,
+    )
+    packed = jnp.moveaxis(packed, 0, 1).reshape(local_rows, layer_count * COLS)
+    whole = gather_rows(packed).reshape(model_width, layer_count, COLS)
     for layer_index in range(layer_count):
         gain_norm = gain_in[layer_index].astype(f32)
         scale = lax.rsqrt(jnp.mean(hidden * hidden, axis=1) + EPS)
@@ -228,9 +537,9 @@
         proj_zx, proj_bc, proj_dt = add_rows(
             starting,
             (
-                lax.all_gather(w_zx[layer_index], "fsdp", axis=0, tiled=True),
-                lax.all_gather(w_bc[layer_index], "fsdp", axis=0, tiled=True),
-                lax.all_gather(w_dt[layer_index], "fsdp", axis=0, tiled=True),
+                whole[:, layer_index, :ZX].reshape(model_width, 2, local_inner),
+                whole[:, layer_index, ZX : ZX + PAIR],
+                whole[:, layer_index, ZX + PAIR : ZX + PAIR + local_heads],
             ),
             jnp.int32(0),
         )
@@ -267,7 +576,7 @@
         def project_cols(weight_piece, first_row, normed_gate=normed_gate):
             return jnp.dot(normed_gate, weight_piece, preferred_element_type=f32)
 
-        partial_mix = project_cols(gather_directly(w_out[layer_index], "fsdp", 1), jnp.int32(0))
+        partial_mix = project_cols(whole[:, layer_index, IN_COLS:].T, jnp.int32(0))
         mixed_own = lax.psum_scatter(partial_mix, "tp", scatter_dimension=0, tiled=True)
         saved.append(
             (
@@ -312,7 +621,7 @@
 
         d_normed_gate = add_back(
             jnp.zeros((group_count, local_inner), f32),
-            lax.all_gather(w_out[layer_index], "fsdp", axis=1, tiled=True),
+            whole[:, layer_index, IN_COLS:].T,
             jnp.int32(0),
         )
         gain_inner = gain_gate[layer_index].astype(f32)
@@ -355,11 +664,10 @@
             )
 
         d_normed_part = back_cols(
-            lax.all_gather(
-                (w_zx[layer_index], w_bc[layer_index], w_dt[layer_index]),
-                "fsdp",
-                axis=0,
-                tiled=True,
+            (
+                whole[:, layer_index, :ZX].reshape(model_width, 2, local_inner),
+                whole[:, layer_index, ZX : ZX + PAIR],
+                whole[:, layer_index, ZX + PAIR : ZX + PAIR + local_heads],
             ),
             jnp.int32(0),
         )
@@ -377,7 +685,9 @@
         )
         kept_terms[layer_index] = (
             gathered,
-            jnp.concatenate([d_proj_zx, d_proj_bc, d_proj_dt], axis=1),
+            jnp.concatenate(
+                [d_proj_zx, d_proj_bc, jnp.pad(d_proj_dt, ((0, 0), (0, DT - local_heads)))], axis=1
+            ),
             cot_all,
             normed_gate,
         )
@@ -390,7 +700,8 @@
             widen(jnp.stack([d_dt_bias, d_a_log, d_skip])),
             widen(d_gain_gate),
         )
-    joined = lax.psum_scatter(term_builder(kept_terms), "fsdp", scatter_dimension=0, tiled=True)
+    terms = term_builder(kept_terms).astype(bf16)
+    joined = reduce_rows(terms.reshape(4, 2, 4, 2, local_rows, layer_count * COLS))
     block_width = joined.shape[1] // layer_count
     weight_sums = [
         joined[:, layer_index * block_width : (layer_index + 1) * block_width]
@@ -398,12 +709,12 @@
     ]
     zx_end = 2 * local_inner
     bc_end = zx_end + pair_width
-    dt_end = bc_end + local_heads
+    dt_end = bc_end + DT
     grad_w_zx = jnp.stack(
         [block[:, :zx_end].reshape(local_rows, 2, local_inner) for block in weight_sums]
     )
     grad_w_bc = jnp.stack([block[:, zx_end:bc_end] for block in weight_sums])
-    grad_w_dt = jnp.stack([block[:, bc_end:dt_end] for block in weight_sums])
+    grad_w_dt = jnp.stack([block[:, bc_end : bc_end + local_heads] for block in weight_sums])
     grad_w_out = jnp.stack([block[:, dt_end:].T for block in weight_sums])
     gains_all = jnp.stack([entry[0] for entry in small_terms])
     taps_x_all = jnp.stack([entry[1] for entry in small_terms])

time: 1200 us -> 804 us (0.67)
  blocking collectives: 497 us -> 131 us
  waiting for transfers between devices: 340 us -> 153 us
  Pallas kernels: 0 us -> 151 us
  matrix products: 121 us -> 139 us
  starting transfers between devices: 33 us -> 15.9 us
  local copies, waits for them, and re-layouts: 112 us -> 125 us
    all_gather x4 -> x0, blocking collectives: 355 us -> none  [the longest x2 199 us: shards(): lax.all_gather(w_dt[layer_index], 'fsdp', axis=0, tiled=True)]
    unnamed x9 -> x3, waiting for transfers between devices: 263 us -> 0.05 us
    pallas_call x0 -> x2, Pallas kernels: none -> 151 us  [the longest x1 80.4 us: reduce_rows(): pl.pallas_call(reduce_kernel, out_shape=jax.ShapeDtypeStruct((rows, width...]
    psum x1, waiting for transfers between devices: 70 us -> 123 us  [shards(): lax.psum((gains_all, taps_x_all, taps_bc_all, shift_x_all, shift_bc_all,...]
    unnamed x383 -> x337, local copies, waits for them, and re-layouts: 51.6 us -> 19.9 us
    reshape x0 -> x3, local copies, waits for them, and re-layouts: none -> 28.7 us  [the longest x1 27.6 us: shards(): whole = gather_rows(packed).reshape(model_width, layer_count, COLS)]
    slice x6 -> x4, local copies, waits for them, and re-layouts: 5.31 us -> 30.9 us  [the longest x1 13.1 us: shards(): whole[:, layer_index, :ZX].reshape(model_width, 2, local_inner)]
    reduce_scatter x2, waiting for transfers between devices: 0.01 us -> 20.7 us  [shards(): lax.psum_scatter(partial_mix, 'tp', scatter_dimension=0, tiled=True)]
  transfers between devices with their start and end apart: 14 -> 7, of which waited for: 4 -> 4; matrix products, arithmetic and copies ran while one was open for 19% -> 5% of each run, Pallas kernels for 0% -> 0%
where the time goes in v1:
time: 804 us; the launch traced here: 795 us
  waiting for transfers between devices  153 us (19%)
  Pallas kernels  151 us (19%)
  matrix products  139 us (17%)
  blocking collectives  131 us (16%)
  local copies, waits for them, and re-layouts  125 us (16%)
  other arithmetic  62.3 us (8%)
  between operations  17.5 us (2%)
  starting transfers between devices  15.9 us (2%)
    psum x1, waiting for transfers between devices, shards(): lax.psum((gains_all, taps_x_all, taps_bc_all, shift_x_all, shift_bc_all,...  123 us
    pallas_call x1, Pallas kernels, reduce_rows(): pl.pallas_call(reduce_kernel, out_shape=jax.ShapeDtypeStruct((rows, width...  80.4 us
    pallas_call x1, Pallas kernels, gather_rows(): pl.pallas_call(gather_kernel, out_shape=jax.ShapeDtypeStruct((4, 2, 4, 2,...  70.7 us
    psum x1, blocking collectives, shards(): lax.psum((gains_all, taps_x_all, taps_bc_all, shift_x_all, shift_bc_all,...  63.4 us
    dot_general x6, matrix products, one_block(): jnp.einsum('tsh,shp->thp', weights, block_values, precision=highest)  35.1 us
    reshape x1, local copies, waits for them, and re-layouts, shards(): whole = gather_rows(packed).reshape(model_width, layer_count, COLS)  27.6 us
    all_gather x2, blocking collectives, shards(): gathered = lax.all_gather(normed_own, 'tp', axis=0, tiled=True)  21.8 us
    reduce_scatter x2, waiting for transfers between devices, shards(): lax.psum_scatter(partial_mix, 'tp', scatter_dimension=0, tiled=True)  20.7 us
  transfers between devices with their start and end apart: 7, of which 4 were waited for; matrix products, arithmetic and copies ran while one was open for 5% of the time, Pallas kernels for 0%

profile of v1, /device:TPU:0, one launch (start us, length us, event | category | flops | bytes accessed | tf_op | source)
XLA Modules:
  0.0 794.7 jit_solution(10040705688602505343)
XLA Ops:
  10.9 70.7 %gather_rows.1 = bf16[4,2,4,2,16,6912]{5,4,3,2,1,0:T(8,128)(2,1)S(1)} custom-call(bf16[16,6912]{1,0:T(8,128)(2,1)S(1)} %bitcast.287), custom_call_target="tpu_custom_call" | custom-call | tf_op jit(solution)/shard_map/gather_rows/pallas_call | solution.py:299
  81.7 5.1 copy-done
  86.7 27.6 %reshape.640 = bf16[1024,2,3456]{2,1,0:T(2,128)(2,1)} reshape(bf16[4,2,4,2,16,6912]{5,4,3,2,1,0:T(8,128)(2,1)} %copy-done) | data formatting | bytes 28311552 | tf_op jit(solution)/shard_map/reshape | solution.py:514
  114.3 3.1 fusion.278
  117.4 3.8 fusion.280
  121.2 10.9 %fusion.281 = (bf16[1024,1,1024]{2,1,0:T(2,128)(2,1)}, bf16[1024,1,1024]{2,1,0:T(2,128)(2,1)}) fusion(bf16[1024,2,3456]{2,1,0:T(2,128)(2,1)} %reshape.640), kind=kLoop, calls=%fused_computation.493 | loop fusion | bytes 8388608 | tf_op jit(solution)/shard_map/slice | solution.py:579
  132.3 13.1 %fusion.279 = (bf16[1024,1,2048]{2,1,0:T(2,128)(2,1)}, bf16[1024,1,2048]{2,1,0:T(2,128)(2,1)}) fusion(bf16[1024,2,3456]{2,1,0:T(2,128)(2,1)S(1)} %copy-done.1), kind=kLoop, calls=%fused_computation.491 | loop fusion | bytes 16777216 | tf_op jit(solution)/shard_map/slice | solution.py:540
  149.1 11.3 %all_gather.12 = bf16[256,1024]{1,0:T(8,128)(2,1)S(1)} all-gather(bf16[128,1024]{1,0:T(8,128)(2,1)S(1)} %fusion.148), channel_id=1, replica_groups=mesh['fsdp'=64,'tp'=2] {'tp'}, dimensions={0}, use_global_device_ids=true | all-gather | bytes 786432 | tf_op jit(solution)/shard_map/all_gather | solution.py:519
  160.8 6.3 convolution_convert_fusion.3
  180.8 4.7 fusion.64
  191.4 6.4 psum.77
  198.5 4.1 fusion.139
  207.1 20.7 %reduce-scatter.3.cloned.1.call-done = f32[128,1024]{1,0:T(8,128)} async-done(((f32[256,1024]{1,0:T(8,128)}), f32[128,1024]{1,0:T(8,128)}) %reduce-scatter.3.cloned.1.call-update) | async-done | bytes 524304 | tf_op jit(solution)/shard_map/reduce_scatter | solution.py:580
  230.6 10.5 %all_gather.13 = bf16[256,1024]{1,0:T(8,128)(2,1)S(1)} all-gather(bf16[128,1024]{1,0:T(8,128)(2,1)S(1)} %multiply_convert_fusion.5), channel_id=1, replica_groups=mesh['fsdp'=64,'tp'=2] {'tp'}, dimensions={0}, use_global_device_ids=true | all-gather | bytes 786432 | tf_op jit(solution)/shard_map/all_gather | solution.py:519
  241.9 6.2 convolution_convert_fusion.2
  255.8 9.3 %all_gather.14 = bf16[256,1024]{1,0:T(8,128)(2,1)S(1)} all-gather(bf16[128,1024]{1,0:T(8,128)(2,1)S(1)} %get-tuple-element.591), channel_id=1, replica_groups=mesh['fsdp'=64,'tp'=2] {'tp'}, dimensions={0}, use_global_device_ids=true | all-gather | bytes 786432 | tf_op jit(solution)/shard_map/all_gather | solution.py:616
  272.0 4.7 fusion.67
  281.8 3.2 multiply_reduce_fusion.18
  285.0 7.1 psum.78
  293.3 4.4 fusion.141
  297.7 5.1 multiply_reduce_fusion.12
  302.9 7.6 psum.79
  311.2 3.8 fusion.121
  321.3 3.4 convolution_convert_fusion.4
  338.1 7.9 fusion.29
  346.0 4.9 fusion.77
  357.3 3.2 convolution_bitcast_fusion.2
  367.5 3.7 all-to-all-start
  371.3 7.8 fusion.57
  383.3 4.9 all-to-all-start.1
  388.2 5.1 convolution_convert_fusion
  393.3 3.0 all-to-all-done.1
  400.8 8.5 %all_gather.15 = bf16[256,1024]{1,0:T(8,128)(2,1)S(1)} all-gather(bf16[128,1024]{1,0:T(8,128)(2,1)S(1)} %get-tuple-element.547), channel_id=1, replica_groups=mesh['fsdp'=64,'tp'=2] {'tp'}, dimensions={0}, use_global_device_ids=true | all-gather | bytes 786432 | tf_op jit(solution)/shard_map/all_gather | solution.py:616
  409.4 5.0 multiply_reduce_fusion.13
  414.3 7.1 psum.80
  422.1 3.4 fusion.115
  432.0 3.2 convolution_convert_fusion.5
  448.6 8.1 %fusion.31 = (f32[256,16]{0,1:T(8,128)}, f32[256,16]{0,1:T(8,128)}, f32[256,16]{0,1:T(8,128)}, f32[256,256]{1,0:T(8,128)}) fusion(f32[256,16]{0,1:T(8,128)S(1)} %get-tuple-element.448, f32[256,16]{0,1:T(8,128)S(1)} %fusion.212, f32[256,256]{1,0:T(8,128)S(1)} %fusion.286, pred[256,256]{1,0:T(8,128)(4,1)S(1)} %compare_and_fusion, ...), kind=kOutput, calls=%fused_computation.47 | convolution fusion | flops 820957184 | bytes 2768896 | tf_op jit(solution)/shard_map/transpose(jvp())/while/body/eval_jaxpr/checkpoint/tsh,shp->thp/dot_general | solution.py:386
  456.7 4.8 fusion.74
  477.0 3.4 all-to-all-start.2
  481.2 7.3 fusion.56
  488.6 122.8 %all-reduce.32.cloned.1.call-done = f32[2,4,2048]{2,1,0:T(4,128)} async-done(((f32[2,4,2048]{2,1,0:T(4,128)}), f32[2,4,2048]{2,1,0:T(4,128)}) %all-reduce.32.cloned.1.call-update) | async-done | bytes 65552 | tf_op jit(solution)/shard_map/psum | solution.py:726
  612.9 2.9 convolution_convert_fusion.1
  615.8 10.2 %pad_maximum_fusion.grad = bf16[4,2,4,2,16,6912]{5,4,3,2,1,0:T(8,128)(2,1)S(1)} fusion(bf16[4,2,4,2,16,1024]{5,4,3,2,1,0:T(8,128)(2,1)S(1)} %bitcast.318, bf16[4,2,4,2,16,2432]{5,4,3,2,1,0:T(8,128)(2,1)} %bitcast.320, bf16[4,2,4,2,16,1024]{5,4,3,2,1,0:T(8,128)(2,1)S(1)} %bitcast.319, bf16[4,2,4,2,16,2432]{5,4,3,2,1,0:T(8,128)(2,1)S(1)} %bitcast.321), kind=kLoop, calls=%fused_computation | loop fusion | flops 56623104 | bytes 28311552 | tf_op jit(solution)/shard_map/concatenate | solution.py:438
  626.0 80.4 %reduce_rows.1 = f32[16,6912]{1,0:T(8,128)S(1)} custom-call(bf16[4,2,4,2,16,6912]{5,4,3,2,1,0:T(8,128)(2,1)S(1)} %pad_maximum_fusion.grad), custom_call_target="tpu_custom_call" | custom-call | tf_op jit(solution)/shard_map/reduce_rows/pallas_call | solution.py:325
  708.4 3.8 all-to-all-start.3
  715.2 6.0 all-to-all-done.3
  722.8 63.4 %all-reduce.29 = (f32[2,1024]{1,0:T(2,128)}, f32[2,4,256]{2,1,0:T(4,128)}, f32[2,2048]{1,0:T(2,128)S(1)}, f32[2,256]{1,0:T(2,128)}, f32[2,3,32]{2,0,1:T(2,128)S(1)}, /*index=5*/f32[2,2048]{1,0:T(2,128)S(1)}) all-reduce(f32[2,1024]{1,0:T(2,128)S(1)} %pad_maximum_fusion.10, ...), channel_id=1, replica_groups=mesh['fsdp'=64,'tp'=2] {'fsdp','tp'}, use_global_device_ids=true, to_apply=%region_36.38 | all-reduce | flops 12992 | bytes 103936 | tf_op jit(solution)/shard_map/psum | solution.py:726
  (539 shorter events, 143.2 us)
Async XLA Ops:
  7.2 220.6 %reduce-scatter.3.cloned.1.call-start = ((), (), s32[]{:S(2)}) async-start(), calls=%async_computation.6 | async-start | bytes 1572864 | tf_op jit(solution)/shard_map/reduce_scatter | solution.py:580
  121.2 39.2 %copy-start.35 = (bf16[1024,1,256]{2,1,0:T(2,128)(2,1)}, bf16[1024,1,256]{2,1,0:T(2,128)(2,1)S(1)}, u32[]{:S(2)}) copy-start(bf16[1024,1,256]{2,1,0:T(2,128)(2,1)S(1)} %get-tuple-element.530) | copy-start | bytes 1572868
  121.2 10.9 %copy-start.1 = (bf16[1024,2,3456]{2,1,0:T(2,128)(2,1)S(1)}, bf16[1024,2,3456]{2,1,0:T(2,128)(2,1)}, u32[]{:S(2)}) copy-start(bf16[1024,2,3456]{2,1,0:T(2,128)(2,1)} %reshape.640) | copy-start | bytes 42467332
  132.2 13.2 %copy-start.24 = (bf16[128,1024]{1,0:T(8,128)(2,1)S(1)}, bf16[128,1024]{1,0:T(8,128)(2,1)}, u32[]{:S(2)}) copy-start(bf16[128,1024]{1,0:T(8,128)(2,1)} %param.17) | copy-start | bytes 786436
  132.2 13.3 %copy-start.164 = (s32[1,4]{1,0:T(1,128)S(1)}, s32[1,4]{1,0:T(1,128)}, u32[]{:S(2)}) copy-start(s32[1,4]{1,0:T(1,128)} %param.19) | copy-start | bytes 52
  132.2 13.6 %copy-start.139 = (bf16[2,256]{1,0:T(2,128)(2,1)S(1)}, bf16[2,256]{1,0:T(2,128)(2,1)}, u32[]{:S(2)}) copy-start(bf16[2,256]{1,0:T(2,128)(2,1)} %param.27) | copy-start | bytes 3076
  132.2 14.1 %copy-start.140 = (bf16[2,4,256]{2,1,0:T(4,128)(2,1)S(1)}, bf16[2,4,256]{2,1,0:T(4,128)(2,1)}, u32[]{:S(2)}) copy-start(bf16[2,4,256]{2,1,0:T(4,128)(2,1)} %param.25) | copy-start | bytes 12292
  132.2 14.1 %copy-start.117 = (bf16[2,1024]{1,0:T(2,128)(2,1)S(1)}, bf16[2,1024]{1,0:T(2,128)(2,1)}, u32[]{:S(2)}) copy-start(bf16[2,1024]{1,0:T(2,128)(2,1)} %param.26) | copy-start | bytes 12292
  132.2 14.7 %copy-start.119 = (bf16[2,1024]{1,0:T(2,128)(2,1)S(1)}, bf16[2,1024]{1,0:T(2,128)(2,1)}, u32[]{:S(2)}) copy-start(bf16[2,1024]{1,0:T(2,128)(2,1)} %param.20) | copy-start | bytes 12292
  132.3 15.3 %copy-start.118 = (bf16[2,4,1024]{2,1,0:T(4,128)(2,1)S(1)}, bf16[2,4,1024]{2,1,0:T(4,128)(2,1)}, u32[]{:S(2)}) copy-start(bf16[2,4,1024]{2,1,0:T(4,128)(2,1)} %param.24) | copy-start | bytes 49156
  145.5 15.3 %copy-start.131 = (f32[128]{0:T(128)}, f32[128]{0:T(128)S(1)}, u32[]{:S(2)}) copy-start(f32[128]{0:T(128)S(1)} %add_rsqrt_fusion.3) | copy-start | bytes 1540
  145.8 22.4 %copy-start.66 = (s32[256]{0:T(256)}, s32[256]{0:T(256)S(1)}, u32[]{:S(2)}) copy-start(s32[256]{0:T(256)S(1)} %convert_reduce_fusion.2) | copy-start | bytes 3076
  147.5 13.3 %copy-start.91 = (f32[1,1024]{1,0:T(1,128)}, f32[1,1024]{1,0:T(1,128)S(1)}, u32[]{:S(2)}) copy-start(f32[1,1024]{1,0:T(1,128)S(1)} %get-tuple-element.576) | copy-start | bytes 12292
  148.2 20.5 %copy-start.73 = (f32[1280]{0:T(1024)}, f32[1280]{0:T(1024)S(1)}, u32[]{:S(2)}) copy-start(f32[1280]{0:T(1024)S(1)} %get-tuple-element.483) | copy-start | bytes 15364
  148.2 20.5 %copy-start.75 = (f32[1280]{0:T(1024)}, f32[1280]{0:T(1024)S(1)}, u32[]{:S(2)}) copy-start(f32[1280]{0:T(1024)S(1)} %get-tuple-element.486) | copy-start | bytes 15364
  148.2 20.5 %copy-start.77 = (f32[1280]{0:T(1024)}, f32[1280]{0:T(1024)S(1)}, u32[]{:S(2)}) copy-start(f32[1280]{0:T(1024)S(1)} %get-tuple-element.485) | copy-start | bytes 15364
  148.3 20.5 %copy-start.79 = (f32[1280]{0:T(1024)}, f32[1280]{0:T(1024)S(1)}, u32[]{:S(2)}) copy-start(f32[1280]{0:T(1024)S(1)} %get-tuple-element.484) | copy-start | bytes 15364
  160.5 18.3 %copy-start.40 = (bf16[256,1024]{1,0:T(8,128)(2,1)}, bf16[256,1024]{1,0:T(8,128)(2,1)S(1)}, u32[]{:S(2)}) copy-start(bf16[256,1024]{1,0:T(8,128)(2,1)S(1)} %all_gather.12) | copy-start | bytes 1572868
  191.4 11.1 %copy-start.14 = (f32[256,1024]{1,0:T(8,128)}, f32[256,1024]{1,0:T(8,128)S(1)}, u32[]{:S(2)}) copy-start(f32[256,1024]{1,0:T(8,128)S(1)} %get-tuple-element.522) | copy-start | bytes 3145732
  202.6 25.2 %copy-start.25 = (bf16[128,1024]{1,0:T(8,128)(2,1)S(1)}, bf16[128,1024]{1,0:T(8,128)(2,1)}, u32[]{:S(2)}) copy-start(bf16[128,1024]{1,0:T(8,128)(2,1)} %param.17) | copy-start | bytes 786436
  202.6 25.2 %copy-start.31 = (bf16[128,1024]{1,0:T(8,128)(2,1)S(1)}, bf16[128,1024]{1,0:T(8,128)(2,1)}, u32[]{:S(2)}) copy-start(bf16[128,1024]{1,0:T(8,128)(2,1)} %param.18) | copy-start | bytes 786436
  202.6 195.8 %reduce-scatter.5.cloned.1.call-start = ((), (), s32[]{:S(2)}) async-start(), calls=%async_computation.7 | async-start | bytes 1572864 | tf_op jit(solution)/shard_map/reduce_scatter | solution.py:580
  204.5 24.6 %copy-start.147 = (f32[128]{0:T(128)}, f32[128]{0:T(128)S(1)}, u32[]{:S(2)}) copy-start(f32[128]{0:T(128)S(1)} %dynamic_slice.73) | copy-start | bytes 1540
  206.3 148.4 %copy-start.11 = (f32[256,256]{1,0:T(8,128)}, f32[256,256]{1,0:T(8,128)S(1)}, u32[]{:S(2)}) copy-start(f32[256,256]{1,0:T(8,128)S(1)} %fusion.165) | copy-start | bytes 786436
  207.1 34.0 %copy-start.37 = (bf16[1024,1,256]{2,1,0:T(2,128)(2,1)S(1)}, bf16[1024,1,256]{2,1,0:T(2,128)(2,1)}, u32[]{:S(2)}) copy-start(bf16[1024,1,256]{2,1,0:T(2,128)(2,1)} %get-tuple-element.529) | copy-start | bytes 1572868
  229.1 12.3 %copy-start.9 = (f32[128,1024]{1,0:T(8,128)}, f32[128,1024]{1,0:T(8,128)S(1)}, u32[]{:S(2)}) copy-start(f32[128,1024]{1,0:T(8,128)S(1)} %get-tuple-element.520) | copy-start | bytes 1572868
  333.8 12.2 %copy-start.68 = (f32[256,16]{0,1:T(8,128)}, f32[256,16]{0,1:T(8,128)S(1)}, u32[]{:S(2)}) copy-start(f32[256,16]{0,1:T(8,128)S(1)} %get-tuple-element.474) | copy-start | bytes 49156
  334.1 11.9 %copy-start.65 = (f32[256,16]{0,1:T(8,128)}, f32[256,16]{0,1:T(8,128)S(1)}, u32[]{:S(2)}) copy-start(f32[256,16]{0,1:T(8,128)S(1)} %fusion.226) | copy-start | bytes 49156
  334.9 11.1 %copy-start.136 = (f32[16]{0:T(128)}, f32[16]{0:T(128)S(1)}, u32[]{:S(2)}) copy-start(f32[16]{0:T(128)S(1)} %get-tuple-element.568) | copy-start | bytes 196
  367.5 13.0 %all-to-all-start = ((bf16[2,256,256]{2,1,0:T(8,128)(2,1)}), bf16[2,256,256]{2,1,0:T(8,128)(2,1)S(1)}, u32[]{:S(2)}, u32[]{:S(2)}) async-start(bf16[2,256,256]{2,1,0:T(8,128)(2,1)} %broadcast_in_dim.394), calls=%async_computation.2 | async-start | bytes 524288 | tf_op jit(solution)/shard_map/all_to_all | solution.py:28
  371.3 9.2 %copy-start.38 = (bf16[1024,1,256]{2,1,0:T(2,128)(2,1)S(1)}, bf16[1024,1,256]{2,1,0:T(2,128)(2,1)}, u32[]{:S(2)}) copy-start(bf16[1024,1,256]{2,1,0:T(2,128)(2,1)} %get-tuple-element.529) | copy-start | bytes 1572868
  371.3 9.2 %copy-start.144 = (bf16[256]{0:T(256)(128)(2,1)S(1)}, bf16[256]{0:T(256)(128)(2,1)}, u32[]{:S(2)}) copy-start(bf16[256]{0:T(256)(128)(2,1)} %fusion.242) | copy-start | bytes 1540
  383.3 13.0 %all-to-all-start.1 = ((bf16[2,128,1024]{2,1,0:T(8,128)(2,1)}), bf16[2,128,1024]{2,1,0:T(8,128)(2,1)S(1)}, u32[]{:S(2)}, u32[]{:S(2)}) async-start(bf16[2,128,1024]{2,1,0:T(8,128)(2,1)} %bitcast.49), calls=%async_computation.3 | async-start | bytes 1048576 | tf_op jit(solution)/shard_map/all_to_all | solution.py:49
  388.2 223.2 %all-reduce.32.cloned.1.call-start = ((), (), s32[]{:S(2)}) async-start(), calls=%async_computation.8 | async-start | bytes 131072 | tf_op jit(solution)/shard_map/psum | solution.py:726
  398.4 10.9 %copy-start.15 = (f32[256,1024]{1,0:T(8,128)S(1)}, f32[256,1024]{1,0:T(8,128)}, u32[]{:S(2)}) copy-start(f32[256,1024]{1,0:T(8,128)} %copy-done.14) | copy-start | bytes 3145732
  398.4 10.9 %copy-start.96 = (f32[1,1024]{1,0:T(1,128)S(1)}, f32[1,1024]{1,0:T(1,128)}, u32[]{:S(2)}) copy-start(f32[1,1024]{1,0:T(1,128)} %get-tuple-element.572) | copy-start | bytes 12292
  398.4 10.9 %copy-start.124 = (f32[256]{0:T(256)S(1)}, f32[256]{0:T(256)}, u32[]{:S(2)}) copy-start(f32[256]{0:T(256)} %copy-done.123) | copy-start | bytes 3076
  444.6 12.1 %copy-start.64 = (f32[256,16]{0,1:T(8,128)}, f32[256,16]{0,1:T(8,128)S(1)}, u32[]{:S(2)}) copy-start(f32[256,16]{0,1:T(8,128)S(1)} %fusion.212) | copy-start | bytes 49156
  475.1 13.4 %copy-start.56 = (bf16[256,1024]{1,0:T(8,128)(2,1)}, bf16[256,1024]{1,0:T(8,128)(2,1)S(1)}, u32[]{:S(2)}) copy-start(bf16[256,1024]{1,0:T(8,128)(2,1)S(1)} %slice.419) | copy-start | bytes 1572868
  477.0 135.8 %all-to-all-start.2 = ((bf16[2,256,256]{2,1,0:T(8,128)(2,1)}), bf16[2,256,256]{2,1,0:T(8,128)(2,1)S(1)}, u32[]{:S(2)}, u32[]{:S(2)}) async-start(bf16[2,256,256]{2,1,0:T(8,128)(2,1)} %broadcast_in_dim.397), calls=%async_computation.4 | async-start | bytes 524288 | tf_op jit(solution)/shard_map/all_to_all | solution.py:28
  481.2 131.6 %copy-start.41 = (bf16[256,1024]{1,0:T(8,128)(2,1)S(1)}, bf16[256,1024]{1,0:T(8,128)(2,1)}, u32[]{:S(2)}) copy-start(bf16[256,1024]{1,0:T(8,128)(2,1)} %copy-done.40) | copy-start | bytes 1572868
  626.0 80.5 %copy-start.36 = (bf16[1024,1,256]{2,1,0:T(2,128)(2,1)S(1)}, bf16[1024,1,256]{2,1,0:T(2,128)(2,1)}, u32[]{:S(2)}) copy-start(bf16[1024,1,256]{2,1,0:T(2,128)(2,1)} %copy-done.35) | copy-start | bytes 1572868
  626.0 80.5 %copy-start.53 = (f32[256,1024]{1,0:T(8,128)S(1)}, f32[256,1024]{1,0:T(8,128)}, u32[]{:S(2)}) copy-start(f32[256,1024]{1,0:T(8,128)} %fusion.56) | copy-start | bytes 3145732
  626.0 80.5 %copy-start.145 = (bf16[256]{0:T(256)(128)(2,1)S(1)}, bf16[256]{0:T(256)(128)(2,1)}, u32[]{:S(2)}) copy-start(bf16[256]{0:T(256)(128)(2,1)} %fusion.242) | copy-start | bytes 1540
  708.4 12.9 %all-to-all-start.3 = ((bf16[2,128,1024]{2,1,0:T(8,128)(2,1)}), bf16[2,128,1024]{2,1,0:T(8,128)(2,1)S(1)}, u32[]{:S(2)}, u32[]{:S(2)}) async-start(bf16[2,128,1024]{2,1,0:T(8,128)(2,1)} %bitcast.63), calls=%async_computation.5 | async-start | bytes 1048576 | tf_op jit(solution)/shard_map/all_to_all | solution.py:49
  712.2 9.2 %copy-start.26 = (bf16[128,1024]{1,0:T(8,128)(2,1)S(1)}, bf16[128,1024]{1,0:T(8,128)(2,1)}, u32[]{:S(2)}) copy-start(bf16[128,1024]{1,0:T(8,128)(2,1)} %param.17) | copy-start | bytes 786436
  712.2 9.2 %copy-start.92 = (f32[1,1024]{1,0:T(1,128)S(1)}, f32[1,1024]{1,0:T(1,128)}, u32[]{:S(2)}) copy-start(f32[1,1024]{1,0:T(1,128)} %copy-done.91) | copy-start | bytes 12292
  712.2 9.2 %copy-start.132 = (f32[128]{0:T(128)S(1)}, f32[128]{0:T(128)}, u32[]{:S(2)}) copy-start(f32[128]{0:T(128)} %copy-done.131) | copy-start | bytes 1540
  (124 other events, 403.8 us)
Sparse Core Ops, SparseCore 0:
  202.7 25.0 reduce-scatter.2
  366.8 24.8 reduce-scatter.4
  476.4 134.9 all-reduce.31

commit v2 on v1

v2 whole, which is shorter than its diff:
```python
import jax
import jax.numpy as jnp
from jax import lax
from jax.experimental import pallas as pl
from jax.experimental.pallas import tpu as pltpu
from jax.sharding import PartitionSpec as P

MESH = pl.DeviceIdType.MESH
INNER = 2048
EPS = 1e-05


def place():
    index = lax.axis_index("fsdp")
    return index // 16, (index // 8) % 2, (index // 2) % 4, index % 2


def index_of(y, z, x, c):
    return ((y * 2 + z) * 4 + x) * 2 + c


PLANE_ZX = [(dz, dx) for dz in range(2) for dx in range(4) if (dz, dx) != (0, 0)]
PLANE_YZ = [(dy, dz) for dy in range(4) for dz in range(2) if (dy, dz) != (0, 0)]


def peers_of():
    y, z, x, c = place()
    found = [index_of(y, (z + dz) % 2, (x + dx) % 4, c) for dz, dx in PLANE_ZX]
    found += [index_of((y + dy) % 4, (z + dz) % 2, x, c) for dy, dz in PLANE_YZ if dy != 0]
    found.append(index_of(y, z, x, 1 - c))
    return found


def greet_all(with_tp):
    barrier = pltpu.get_barrier_semaphore()
    peers = peers_of()
    for peer in peers:
        pl.semaphore_signal(barrier, inc=1, device_id={"fsdp": peer}, device_id_type=MESH)
    count = len(peers)
    if with_tp:
        other = 1 - lax.axis_index("tp")
        pl.semaphore_signal(barrier, inc=1, device_id={"tp": other}, device_id_type=MESH)
        count += 1
    pl.semaphore_wait(barrier, count)


def send(src, dst, sems, slot, **where):
    copy = pltpu.make_async_remote_copy(
        src_ref=src,
        dst_ref=dst,
        send_sem=sems.at[0, slot],
        recv_sem=sems.at[1, slot],
        device_id=where,
        device_id_type=MESH,
    )
    copy.start()
    return copy


GATHER_COPIES = 28


class Gather:
    def __init__(self, whole, sems, first, half, end):
        self.whole, self.sems = whole, sems
        self.cols = (pl.ds(first, half - first), pl.ds(half, end - half))
        self.started = []

    def plane(self):
        y, z, x, c = place()
        cols_a, cols_b = self.cols
        self.first = []
        for slot, (dz, dx) in enumerate(PLANE_ZX):
            ref = self.whole.at[y, z, x, c, :, cols_a]
            self.first.append(
                send(ref, ref, self.sems, slot, fsdp=index_of(y, (z + dz) % 2, (x + dx) % 4, c))
            )
        for slot, (dy, dz) in enumerate(PLANE_YZ):
            ref = self.whole.at[y, z, x, c, :, cols_b]
            self.first.append(
                send(ref, ref, self.sems, 7 + slot, fsdp=index_of((y + dy) % 4, (z + dz) % 2, x, c))
            )

    def line(self):
        y, z, x, c = place()
        cols_a, cols_b = self.cols
        for copy in self.first:
            copy.wait_recv()
        self.second = []
        for step in range(1, 4):
            ref = self.whole.at[y, :, :, c, :, cols_a]
            self.second.append(
                send(ref, ref, self.sems, 14 + step - 1, fsdp=index_of((y + step) % 4, z, x, c))
            )
            ref = self.whole.at[:, :, x, c, :, cols_b]
            self.second.append(
                send(ref, ref, self.sems, 17 + step - 1, fsdp=index_of(y, z, (x + step) % 4, c))
            )
        self.third = []
        self.hand_over(0)

    def hand_over(self, step):
        y, z, x, c = place()
        cols_a, cols_b = self.cols
        ref = self.whole.at[(y - step + 4) % 4, :, :, c, :, cols_a]
        self.third.append(send(ref, ref, self.sems, 20 + step, fsdp=index_of(y, z, x, 1 - c)))
        ref = self.whole.at[:, :, (x - step + 4) % 4, c, :, cols_b]
        self.third.append(send(ref, ref, self.sems, 24 + step, fsdp=index_of(y, z, x, 1 - c)))

    def core(self):
        for step in (1, 3, 2):
            self.second[2 * (step - 1)].wait_recv()
            self.second[2 * (step - 1) + 1].wait_recv()
            self.hand_over(step)

    def finish(self):
        for copy in self.third:
            copy.wait_recv()
        for copy in self.first + self.second + self.third:
            copy.wait_send()


REDUCE_COPIES = 21


class Reduce:
    def __init__(self, grad, from_core, from_line_a, from_line_b, from_plane_a, from_plane_b, sems, half, end):
        self.grad, self.from_core, self.sems = grad, from_core, sems
        self.line_a, self.line_b = from_line_a, from_line_b
        self.plane_a, self.plane_b = from_plane_a, from_plane_b
        self.cols = (pl.ds(0, half), pl.ds(half, end - half))

    def core(self):
        y, z, x, c = place()
        self.copies = [
            send(
                self.grad.at[:, :, :, 1 - c],
                self.from_core,
                self.sems,
                0,
                fsdp=index_of(y, z, x, 1 - c),
            )
        ]

    def line(self):
        y, z, x, c = place()
        cols_a, cols_b = self.cols
        self.copies[0].wait_recv()

        @pl.loop(0, 32)
        def _(block):
            iy, iz, ix = block // 8, (block // 4) % 2, block % 4
            mine = self.grad[iy, iz, ix, c].astype(jnp.float32)
            theirs = self.from_core[iy, iz, ix].astype(jnp.float32)
            self.from_core[iy, iz, ix] = (mine + theirs).astype(jnp.bfloat16)

        self.second = []
        for step in range(1, 4):
            to = (y + step) % 4
            self.second.append(
                send(
                    self.from_core.at[to, :, :, :, cols_a],
                    self.line_a.at[step - 1],
                    self.sems,
                    step,
                    fsdp=index_of(to, z, x, c),
                )
            )
            to = (x + step) % 4
            self.second.append(
                send(
                    self.from_core.at[:, :, to, :, cols_b],
                    self.line_b.at[step - 1],
                    self.sems,
                    3 + step,
                    fsdp=index_of(y, z, to, c),
                )
            )

    def plane(self):
        y, z, x, c = place()
        cols_a, cols_b = self.cols
        for copy in self.second:
            copy.wait_recv()

        @pl.loop(0, 8)
        def _(block):
            iz, ix = block // 4, block % 4
            total = self.from_core[y, iz, ix, :, cols_a].astype(jnp.float32)
            for step in range(3):
                total = total + self.line_a[step, iz, ix].astype(jnp.float32)
            self.line_a[0, iz, ix] = total.astype(jnp.bfloat16)
            iy, iz = block // 2, block % 2
            total = self.from_core[iy, iz, x, :, cols_b].astype(jnp.float32)
            for step in range(3):
                total = total + self.line_b[step, iy, iz].astype(jnp.float32)
            self.line_b[0, iy, iz] = total.astype(jnp.bfloat16)

        self.third = []
        for slot, (dz, dx) in enumerate(PLANE_ZX):
            tz, tx = (z + dz) % 2, (x + dx) % 4
            self.third.append(
                send(
                    self.line_a.at[0, tz, tx],
                    self.plane_a.at[slot],
                    self.sems,
                    7 + slot,
                    fsdp=index_of(y, tz, tx, c),
                )
            )
        for slot, (dy, dz) in enumerate(PLANE_YZ):
            ty, tz = (y + dy) % 4, (z + dz) % 2
            self.third.append(
                send(
                    self.line_b.at[0, ty, tz],
                    self.plane_b.at[slot],
                    self.sems,
                    14 + slot,
                    fsdp=index_of(ty, tz, x, c),
                )
            )

    def finish(self, out):
        y, z, x, c = place()
        cols_a, cols_b = self.cols
        for copy in self.third:
            copy.wait_recv()
        total = self.line_a[0, z, x].astype(jnp.float32)
        for slot in range(7):
            total = total + self.plane_a[slot].astype(jnp.float32)
        out[:, cols_a] = total
        total = self.line_b[0, y, z].astype(jnp.float32)
        for slot in range(7):
            total = total + self.plane_b[slot].astype(jnp.float32)
        out[:, cols_b] = total
        for copy in self.copies + self.second + self.third:
            copy.wait_send()


ROWS, WIDTH, INNER_OWN, STATE, HEADS_OWN = 256, 1024, 1024, 128, 16
ZX, PAIR, DT, OUT = 2048, 256, 128, 1024
IN_COLS = ZX + PAIR + DT
COLS = IN_COLS + OUT
SIGNAL = INNER_OWN + PAIR
F32, BF16 = jnp.float32, jnp.bfloat16
NN = (((1,), (0,)), ((), ()))
NT = (((1,), (1,)), ((), ()))
TN = (((0,), (0,)), ((), ()))


def dot(a, b, dims=NN):
    return lax.dot_general(a, b, dims, preferred_element_type=F32)


def exact_dot(a, b, dims=NN):
    return lax.dot_general(
        a, b, dims, preferred_element_type=F32, precision=lax.Precision.HIGHEST
    )


def tile(index, width):
    return pl.ds(pl.multiple_of(index * width, width), width)


def twice(part):
    return jnp.concatenate([part, part], axis=1)


def column(part, head):
    lane = lax.broadcasted_iota(jnp.int32, part.shape, 1)
    return jnp.sum(jnp.where(lane == head, part, 0.0), axis=1, keepdims=True)


def body(
    x_ref, cot_ref, own_ref, lens_ref, vec_ref, conv_ref, head_ref,
    act_ref, gin_ref, gw_ref, small_ref,
    wz0, wo0, w1, hid, norm_t, proj, vals, ssd, ngate, steps, cums, cums_t, scales, gscales, sig_dt,
    xs, cots, normed, cot_b, cot_t, grad, du, dact, dproj, scores, dscores, mask, same, live, acc, dcum, dstep,
    mixs, mixr, row_s, row_r, smalls, slots, bc_s, bc_r,
    core1, la1, lb1, pa1, pb1, core0, la0, lb0, pa0, pb0, coreo, lao, lbo, pao, pbo,
    gsem, rsem, tsem, ssem, lsem,
):
    y, z, x, c = place()
    t = lax.axis_index("tp")
    other = 1 - t
    own_rows = pl.ds(pl.multiple_of(t * 128, 128), 128)
    peer_rows = pl.ds(pl.multiple_of(other * 128, 128), 128)

    def wz(layer, cols):
        ref = wz0 if layer == 0 else w1
        return ref.at[:, :, :, :, :, cols]

    def load_cols(ref, cols):
        part = ref[:, :, :, :, :, cols]
        return part.reshape(WIDTH, part.shape[-1])

    def store_cols(ref, cols, part):
        ref[:, :, :, :, :, cols] = part.astype(BF16).reshape(4, 2, 4, 2, 16, part.shape[-1])

    z_ref = (wz0, w1)
    o_ref = (wo0, w1)
    o_first = (0, IN_COLS)

    keeps = [
        pltpu.make_async_copy(own_ref.at[0, :, pl.ds(0, IN_COLS)], wz0.at[y, z, x, c], lsem.at[0]),
        pltpu.make_async_copy(own_ref.at[0, :, pl.ds(IN_COLS, OUT)], wo0.at[y, z, x, c], lsem.at[1]),
        pltpu.make_async_copy(own_ref.at[1], w1.at[y, z, x, c], lsem.at[2]),
    ]
    for keep in keeps:
        keep.start()
    greet_all(True)
    for keep in keeps:
        keep.wait()
    gather_z0 = Gather(wz0, gsem.at[0], 0, 1280, IN_COLS)
    gather_o0 = Gather(wo0, gsem.at[1], 0, 512, OUT)
    gather_1 = Gather(w1, gsem.at[2], 0, 1792, COLS)
    gather_z0.plane()
    send_x = send(x_ref, xs.at[own_rows], tsem, 0, tp=other)
    send_cot = send(cot_ref, cots.at[own_rows], tsem, 1, tp=other)
    xs[own_rows, :] = x_ref[...]
    cots[own_rows, :] = cot_ref[...]

    bounds = [lens_ref[0, 0]]
    for j in range(1, 4):
        bounds.append(bounds[-1] + lens_ref[0, j])

    def ids_at(pos):
        total = jnp.zeros(pos.shape, jnp.int32)
        for bound in bounds:
            total = total + (pos >= bound).astype(jnp.int32)
        return total

    pos = lax.broadcasted_iota(jnp.int32, (ROWS, 128), 0)
    ids = ids_at(pos)
    live[...] = (ids < 4).astype(F32)
    for back in range(1, 4):
        same[back - 1] = ((ids == ids_at(pos - back)) & (pos >= back)).astype(F32)
    at = lax.broadcasted_iota(jnp.int32, (ROWS, ROWS), 0)
    src = lax.broadcasted_iota(jnp.int32, (ROWS, ROWS), 1)
    mask[...] = jnp.where((ids_at(at) == ids_at(src)) & (src <= at), 0.0, -1e30)
    smalls[...] = jnp.zeros_like(smalls)

    def spread_rows(part):
        return jnp.broadcast_to(part[0:1, :], (128, ROWS)).T

    def send_rows(which):
        total = jnp.sum(acc[...], axis=1, keepdims=True)
        row_s[which] = jnp.broadcast_to(total, (ROWS, 128)).T[:8, :]
        return send(row_s.at[which], row_r.at[which], tsem, 2 + which, tp=other)

    def norm_layer(layer):
        @pl.loop(0, 4)
        def _(step):
            rows = tile(step, 64)
            part = hid[layer, rows, :]
            scale = lax.rsqrt(jnp.mean(part * part, axis=1, keepdims=True) + EPS)
            scales[layer, rows, :] = jnp.broadcast_to(scale, (64, 128))
            normed[rows, :] = (part * scale * vec_ref[layer, 0:1, :]).astype(BF16)

    def transposed(from_ref, to_ref):
        @pl.loop(0, 8)
        def _(step):
            cols = tile(step, 128)
            to_ref[cols, :] = from_ref[:, cols].astype(F32).T.astype(BF16)

    def conv_pre(layer, signal, cols):
        pre = conv_ref[layer, 4:5, cols] + conv_ref[layer, 3:4, cols] * signal
        shifted = []
        for back in range(1, 4):
            earlier = pltpu.roll(signal, back, 0) * twice(same[back - 1])
            shifted.append(earlier)
            pre = pre + conv_ref[layer, 3 - back : 4 - back, cols] * earlier
        return pre, shifted

    def shift_cols(step):
        return pl.ds(pl.multiple_of(INNER_OWN + step * 256, 256), 256)

    def forward_in(layer):
        norm_layer(layer)

        @pl.loop(0, 9)
        def _(step):
            cols = tile(step, 256)
            proj[layer, :, cols] = dot(normed[...], load_cols(z_ref[layer], cols)).astype(BF16)

        raw = dot(normed[...], load_cols(z_ref[layer], pl.ds(ZX + PAIR, DT)))
        raw = raw.astype(BF16).astype(F32) + head_ref[layer, 0:1, :]
        sig_dt[layer] = jax.nn.sigmoid(raw)
        step_sizes = jnp.maximum(raw, 0.0) + jnp.log1p(jnp.exp(-jnp.abs(raw)))
        steps[layer] = step_sizes
        rate = -jnp.exp(head_ref[layer, 1:2, :])
        lower = (src <= at).astype(F32)
        summed = exact_dot(lower, step_sizes * rate)
        cums[layer] = summed
        cums_t[layer] = summed.T

    def forward_conv(layer):
        @pl.loop(0, 5)
        def _(step):
            signal = proj[layer, :, shift_cols(step)].astype(F32)
            pre, unused = conv_pre(layer, signal, tile(step, 256))
            vals[layer, :, tile(step, 256)] = (pre * jax.nn.sigmoid(pre)).astype(BF16)

    def set_scores(layer):
        b_mat = vals[layer, :, pl.ds(INNER_OWN, STATE)]
        c_mat = vals[layer, :, pl.ds(INNER_OWN + STATE, STATE)]
        scores[...] = dot(c_mat, b_mat, NT)

    def decays(layer, head):
        return jnp.exp(
            column(cums[layer], head) - cums_t[layer, pl.ds(head, 1), :] + mask[...]
        )

    def forward_ssd(layer):
        set_scores(layer)
        acc[...] = jnp.zeros_like(acc)

        @pl.loop(0, 8)
        def _(step):
            cols = tile(step, 128)
            values = vals[layer, :, cols].astype(F32)
            upper = lax.broadcasted_iota(jnp.int32, (ROWS, 128), 1) >= 64
            total = vec_ref[layer, 2:3, cols] * values
            for half in range(2):
                head = 2 * step + half
                weights = (scores[...] * decays(layer, head)).astype(BF16)
                scaled = values * column(steps[layer], head)
                scaled = jnp.where(upper == (half == 1), scaled, 0.0).astype(BF16)
                total = total + dot(weights, scaled)
            ssd[layer, :, cols] = total
            gate = proj[layer, :, cols].astype(F32)
            gated = total * gate * jax.nn.sigmoid(gate)
            acc[...] += gated * gated
            ngate[:, cols] = (gated * vec_ref[layer, 1:2, cols]).astype(BF16)

    def mix_copy(which, step, rows):
        ref_s = mixs.at[which, rows, tile(step, 256)]
        ref_r = mixr.at[which, rows, tile(step, 256)]
        return pltpu.make_async_remote_copy(
            src_ref=ref_s,
            dst_ref=ref_r,
            send_sem=tsem.at[0, 8 + 4 * which + step],
            recv_sem=tsem.at[1, 8 + 4 * which + step],
            device_id={"tp": other},
            device_id_type=MESH,
        )

    def wait_mix(which, rows):
        @pl.loop(0, 4)
        def _(step):
            copy = mix_copy(which, step, rows)
            copy.wait_recv()
            copy.wait_send()

    def forward_out(layer, rows):
        ref, first = o_ref[layer], o_first[layer]

        @pl.loop(0, 4)
        def _(step):
            weight = ref[step, :, :, :, :, pl.ds(first, OUT)].reshape(256, OUT)
            mixs[layer, :, tile(step, 256)] = dot(ngate[...], weight, NT).astype(BF16)
            mix_copy(layer, step, rows).start()

    def take_gate_scale(layer, copy):
        copy.wait_recv()
        total = row_s[layer] + row_r[layer]
        gscales[layer] = spread_rows(lax.rsqrt(total / INNER + EPS))

    def mixed_rows(layer, rows):
        part = mixs[layer, rows, :].astype(F32) + mixr[layer, rows, :].astype(F32)
        return part * (gscales[layer, rows, 0:1] * live[rows, 0:1])

    gather_z0.line()
    send_x.wait_recv()

    @pl.loop(0, 4)
    def _(step):
        rows = tile(step, 64)
        hid[0, rows, :] = xs[rows, :].astype(F32)

    gather_z0.core()
    gather_o0.plane()
    gather_1.plane()
    gather_z0.finish()
    forward_in(0)
    gather_o0.line()
    transposed(normed, norm_t.at[0])
    forward_conv(0)
    gather_o0.core()
    gather_1.line()
    forward_ssd(0)
    squares_0 = send_rows(0)
    gather_o0.finish()
    forward_out(0, pl.ds(0, ROWS))
    gather_1.core()
    take_gate_scale(0, squares_0)
    wait_mix(0, pl.ds(0, ROWS))

    @pl.loop(0, 4)
    def _(step):
        rows = tile(step, 64)
        hid[1, rows, :] = hid[0, rows, :] + mixed_rows(0, rows)

    gather_1.finish()
    forward_in(1)
    transposed(normed, norm_t.at[1])
    forward_conv(1)
    forward_ssd(1)
    squares_1 = send_rows(1)
    forward_out(1, peer_rows)
    send_cot.wait_recv()

    @pl.loop(0, 4)
    def _(step):
        rows = tile(step, 64)
        grad[rows, :] = cots[rows, :].astype(F32)

    take_gate_scale(1, squares_1)

    def backward_gate(layer):
        @pl.loop(0, 4)
        def _(step):
            rows = tile(step, 64)
            cot_b[rows, :] = (live[rows, 0:1] * grad[rows, :]).astype(BF16)

        transposed(cot_b, cot_t)
        acc[...] = jnp.zeros_like(acc)

        @pl.loop(0, 4)
        def _(step):
            cols = tile(step, 256)
            first = pl.ds(pl.multiple_of(o_first[layer] + step * 256, 128), 256)
            d_normed_gate = dot(cot_b[...], load_cols(o_ref[layer], first))
            gate = proj[layer, :, cols].astype(F32)
            gated = ssd[layer, :, cols] * gate * jax.nn.sigmoid(gate)
            normal = gated * twice(gscales[layer])
            gain = vec_ref[layer, 1:2, cols]
            ngate[:, cols] = (normal * gain).astype(BF16)
            smalls[layer, 1:2, cols] = jnp.sum(d_normed_gate * normal, axis=0, keepdims=True)
            weighted = d_normed_gate * gain
            du[:, cols] = weighted
            inner = weighted * gated
            acc[...] += inner[:, :128] + inner[:, 128:]

    def backward_wo(layer):
        ref, first = o_ref[layer], o_first[layer]

        @pl.loop(0, 4)
        def _(step):
            part = dot(cot_t[tile(step, 256), :], ngate[...]).astype(BF16)
            ref[step, :, :, :, :, pl.ds(first, OUT)] = part.reshape(2, 4, 2, 16, OUT)

    def backward_ssd(layer, copy, which):
        copy.wait_recv()
        inner = spread_rows(row_s[which] + row_r[which])
        gs = gscales[layer]
        acc[...] = gs * gs * gs * inner / INNER
        set_scores(layer)
        dscores[...] = jnp.zeros_like(dscores)
        dcum[...] = jnp.zeros_like(dcum)
        dstep[...] = jnp.zeros_like(dstep)

        @pl.loop(0, 8)
        def _(step):
            cols = tile(step, 128)
            lane = lax.broadcasted_iota(jnp.int32, (ROWS, 128), 1)
            upper = lane >= 64
            gate = proj[layer, :, cols].astype(F32)
            out = ssd[layer, :, cols]
            sigmoid = jax.nn.sigmoid(gate)
            silu = gate * sigmoid
            d_gated = gscales[layer] * du[:, cols] - out * silu * acc[...]
            d_out = d_gated * silu
            dproj[:, cols] = (d_gated * out * sigmoid * (1.0 + gate * (1.0 - sigmoid))).astype(BF16)
            values = vals[layer, :, cols].astype(F32)
            size = jnp.where(
                upper, column(steps[layer], 2 * step + 1), column(steps[layer], 2 * step)
            )
            scaled = (values * size).astype(BF16)
            back = jnp.zeros((ROWS, 128), F32)
            for half in range(2):
                head = 2 * step + half
                decay = decays(layer, head)
                weights = (scores[...] * decay).astype(BF16)
                d_half = jnp.where(upper == (half == 1), d_out, 0.0).astype(BF16)
                dscores[...] += dot(d_half, scaled, NT) * decay
                back = back + dot(weights, d_half, TN)
            skip = vec_ref[layer, 2:3, cols]
            dact[:, cols] = skip * d_out + size * back
            smalls[layer, 2:3, cols] = jnp.sum(d_out * values, axis=0, keepdims=True)
            inside = out - skip * values
            turn = d_out.astype(BF16).astype(F32) * inside - scaled.astype(F32) * back
            size_turn = values * back
            for half in range(2):
                head = 2 * step + half
                mine = upper == (half == 1)
                dcum[...] += jnp.where(
                    lane == head,
                    jnp.sum(jnp.where(mine, turn, 0.0), axis=1, keepdims=True),
                    0.0,
                )
                dstep[...] += jnp.where(
                    lane == head,
                    jnp.sum(jnp.where(mine, size_turn, 0.0), axis=1, keepdims=True),
                    0.0,
                )

        rate = -jnp.exp(head_ref[layer, 1:2, :])
        later = (src >= at).astype(F32)
        d_log = exact_dot(later, dcum[...])
        d_raw = (dstep[...] + rate * d_log) * sig_dt[layer]
        smalls[layer, 9:10, pl.ds(256, 128)] = jnp.sum(d_raw, axis=0, keepdims=True)
        smalls[layer, 9:10, pl.ds(384, 128)] = rate * jnp.sum(
            steps[layer] * d_log, axis=0, keepdims=True
        )
        dproj[:, pl.ds(ZX + PAIR, DT)] = d_raw.astype(BF16)
        d_scores = dscores[...].astype(BF16)
        b_mat = vals[layer, :, pl.ds(INNER_OWN, STATE)]
        c_mat = vals[layer, :, pl.ds(INNER_OWN + STATE, STATE)]
        dact[:, pl.ds(INNER_OWN, STATE)] = dot(d_scores, c_mat, TN)
        dact[:, pl.ds(INNER_OWN + STATE, STATE)] = dot(d_scores, b_mat)

    def backward_conv(layer):
        def one(signal_cols, cols):
            signal = proj[layer, :, signal_cols].astype(F32)
            pre, shifted = conv_pre(layer, signal, cols)
            sigmoid = jax.nn.sigmoid(pre)
            d_pre = dact[:, cols] * sigmoid * (1.0 + pre * (1.0 - sigmoid))
            d_signal = conv_ref[layer, 3:4, cols] * d_pre
            d_taps = [jnp.sum(d_pre * signal, axis=0, keepdims=True)]
            for back in range(1, 4):
                d_signal = d_signal + conv_ref[layer, 3 - back : 4 - back, cols] * pltpu.roll(
                    d_pre * twice(same[back - 1]), ROWS - back, 0
                )
                d_taps.append(jnp.sum(d_pre * shifted[back - 1], axis=0, keepdims=True))
            dproj[:, signal_cols] = d_signal.astype(BF16)
            return jnp.sum(d_pre, axis=0, keepdims=True), d_taps

        @pl.loop(0, 4)
        def _(step):
            cols = tile(step, 256)
            d_bias, d_taps = one(shift_cols(step), cols)
            smalls[layer, 3:4, cols] = d_bias
            for back in range(4):
                smalls[layer, 7 - back : 8 - back, cols] = d_taps[back]

        d_bias, d_taps = one(pl.ds(ZX, PAIR), pl.ds(INNER_OWN, PAIR))
        smalls[layer, 9:10, pl.ds(0, PAIR)] = d_bias
        for back in range(4):
            smalls[layer, 8:9, pl.ds((3 - back) * PAIR, PAIR)] = d_taps[back]

    def backward_in(layer, which, rows):
        ref = z_ref[layer]

        @pl.loop(0, 4)
        def _(step):
            cols = tile(step, 256)
            weight = ref[step, :, :, :, :, pl.ds(0, IN_COLS)].reshape(256, IN_COLS)
            part = dot(dproj[...], weight, NT)
            mixs[which, :, cols] = part.astype(BF16)
            mix_copy(which, step, rows).start()
            smalls[layer, 0:1, cols] = jnp.sum(
                part * hid[layer, :, cols] * twice(scales[layer]), axis=0, keepdims=True
            )

    def backward_wz(layer):
        @pl.loop(0, 9)
        def _(step):
            cols = tile(step, 256)
            store_cols(z_ref[layer], cols, dot(norm_t[layer], dproj[:, cols]))

        cols = pl.ds(ZX + PAIR, DT)
        store_cols(z_ref[layer], cols, dot(norm_t[layer], dproj[:, cols]))

    def next_grad(layer, which, rows):
        part = mixs[which, rows, :].astype(F32) + mixr[which, rows, :].astype(F32)
        part = part * vec_ref[layer, 0:1, :]
        before = hid[layer, rows, :]
        scale = scales[layer, rows, 0:1]
        inner = jnp.sum(part * before, axis=1, keepdims=True)
        return grad[rows, :] + scale * part - before * (scale * scale * scale * inner / WIDTH)

    class Smalls:
        def __init__(self, layer):
            self.layer = layer
            self.copies = []

        def start(self, first, count, mine, where, base):
            layer = self.layer
            slots[layer, first + mine] = smalls[layer]
            ref = slots.at[layer, first + mine]
            for step in range(1, count):
                self.copies.append(send(ref, ref, ssem.at[layer], base + step - 1, **where(step)))
            self.pending = self.copies[len(self.copies) - count + 1 :]

        def take(self, first, count):
            layer = self.layer
            for copy in self.pending:
                copy.wait_recv()
            total = slots[layer, first]
            for step in range(1, count):
                total = total + slots[layer, first + step]
            smalls[layer] = total

        def core(self):
            self.start(0, 2, c, lambda step: {"fsdp": index_of(y, z, x, 1 - c)}, 0)

        def along_x(self):
            self.take(0, 2)
            self.start(2, 4, x, lambda step: {"fsdp": index_of(y, z, (x + step) % 4, c)}, 1)

        def along_y(self):
            self.take(2, 4)
            self.start(6, 4, y, lambda step: {"fsdp": index_of((y + step) % 4, z, x, c)}, 4)

        def along_z(self):
            self.take(6, 4)
            self.start(10, 2, z, lambda step: {"fsdp": index_of(y, 1 - z, x, c)}, 7)

        def across(self):
            self.take(10, 2)
            self.start(12, 2, t, lambda step: {"tp": other}, 8)

        def finish(self):
            layer = self.layer
            mine = smalls[layer]
            self.take(12, 2)
            both = smalls[layer]
            row = lax.broadcasted_iota(jnp.int32, both.shape, 0)
            lane = lax.broadcasted_iota(jnp.int32, both.shape, 1)
            shared = (row == 0) | (row == 8) | ((row == 9) & (lane < PAIR))
            small_ref[layer] = jnp.where(shared, both, mine)
            for copy in self.copies:
                copy.wait_send()

    reduce_1 = Reduce(w1, core1, la1, lb1, pa1, pb1, rsem.at[0], 1792, COLS)
    reduce_o0 = Reduce(wo0, coreo, lao, lbo, pao, pbo, rsem.at[1], 512, OUT)
    reduce_z0 = Reduce(wz0, core0, la0, lb0, pa0, pb0, rsem.at[2], 1280, IN_COLS)
    smalls_1, smalls_0 = Smalls(1), Smalls(0)

    backward_gate(1)
    inner_1 = send_rows(2)
    backward_wo(1)
    backward_ssd(1, inner_1, 2)
    backward_conv(1)
    backward_in(1, 2, pl.ds(0, ROWS))
    backward_wz(1)
    reduce_1.core()
    smalls_1.core()
    wait_mix(2, pl.ds(0, ROWS))

    @pl.loop(0, 4)
    def _(step):
        rows = tile(step, 64)
        grad[rows, :] = next_grad(1, 2, rows)

    reduce_1.line()
    smalls_1.along_x()
    wait_mix(1, peer_rows)
    act_ref[...] = (hid[1, own_rows, :] + mixed_rows(1, own_rows)).astype(BF16)

    backward_gate(0)
    inner_0 = send_rows(3)
    backward_wo(0)
    reduce_o0.core()
    backward_ssd(0, inner_0, 3)
    smalls_1.along_y()
    reduce_1.plane()
    reduce_o0.line()
    backward_conv(0)
    smalls_1.along_z()
    backward_in(0, 3, peer_rows)
    reduce_o0.plane()
    reduce_1.finish(gw_ref.at[1])
    bc_s[1] = gw_ref[1, :, pl.ds(ZX, PAIR)]
    bc_1 = send(bc_s.at[1], bc_r.at[1], tsem, 6, tp=other)
    smalls_1.across()
    backward_wz(0)
    reduce_z0.core()
    smalls_0.core()
    wait_mix(3, peer_rows)
    gin_ref[...] = next_grad(0, 3, own_rows)
    reduce_z0.line()
    smalls_0.along_x()
    smalls_1.finish()
    reduce_o0.finish(gw_ref.at[0, :, pl.ds(IN_COLS, OUT)])
    smalls_0.along_y()
    reduce_z0.plane()
    smalls_0.along_z()
    reduce_z0.finish(gw_ref.at[0, :, pl.ds(0, IN_COLS)])
    bc_s[0] = gw_ref[0, :, pl.ds(ZX, PAIR)]
    bc_0 = send(bc_s.at[0], bc_r.at[0], tsem, 7, tp=other)
    smalls_0.across()
    for layer, copy in ((1, bc_1), (0, bc_0)):
        copy.wait_recv()
        gw_ref[layer, :, pl.ds(ZX, PAIR)] = bc_s[layer] + bc_r[layer]
        copy.wait_send()
    smalls_0.finish()
    for copy in (send_x, send_cot, squares_0, squares_1, inner_1, inner_0):
        copy.wait_send()


def reduce_scratch(width, half):
    return [
        pltpu.VMEM((4, 2, 4, 16, width), BF16),
        pltpu.VMEM((3, 2, 4, 16, half), BF16),
        pltpu.VMEM((3, 4, 2, 16, width - half), BF16),
        pltpu.VMEM((7, 16, half), BF16),
        pltpu.VMEM((7, 16, width - half), BF16),
    ]


def whole_step(x_in, cotangent, own, lengths, vec, conv, head):
    scratch = [
        pltpu.VMEM((4, 2, 4, 2, 16, IN_COLS), BF16),
        pltpu.VMEM((4, 2, 4, 2, 16, OUT), BF16),
        pltpu.VMEM((4, 2, 4, 2, 16, COLS), BF16),
        pltpu.VMEM((2, ROWS, WIDTH), F32),
        pltpu.VMEM((2, WIDTH, ROWS), BF16),
        pltpu.VMEM((2, ROWS, ZX + PAIR), BF16),
        pltpu.VMEM((2, ROWS, SIGNAL), BF16),
        pltpu.VMEM((2, ROWS, INNER_OWN), F32),
        pltpu.VMEM((ROWS, INNER_OWN), BF16),
        pltpu.VMEM((2, ROWS, 128), F32),
        pltpu.VMEM((2, ROWS, 128), F32),
        pltpu.VMEM((2, 128, ROWS), F32),
        pltpu.VMEM((2, ROWS, 128), F32),
        pltpu.VMEM((2, ROWS, 128), F32),
        pltpu.VMEM((2, ROWS, 128), F32),
        pltpu.VMEM((ROWS, WIDTH), BF16),
        pltpu.VMEM((ROWS, WIDTH), BF16),
        pltpu.VMEM((ROWS, WIDTH), BF16),
        pltpu.VMEM((ROWS, WIDTH), BF16),
        pltpu.VMEM((WIDTH, ROWS), BF16),
        pltpu.VMEM((ROWS, WIDTH), F32),
        pltpu.VMEM((ROWS, INNER_OWN), F32),
        pltpu.VMEM((ROWS, SIGNAL), F32),
        pltpu.VMEM((ROWS, IN_COLS), BF16),
        pltpu.VMEM((ROWS, ROWS), F32),
        pltpu.VMEM((ROWS, ROWS), F32),
        pltpu.VMEM((ROWS, ROWS), F32),
        pltpu.VMEM((3, ROWS, 128), F32),
        pltpu.VMEM((ROWS, 128), F32),
        pltpu.VMEM((ROWS, 128), F32),
        pltpu.VMEM((ROWS, 128), F32),
        pltpu.VMEM((ROWS, 128), F32),
        pltpu.VMEM((4, ROWS, WIDTH), BF16),
        pltpu.VMEM((4, ROWS, WIDTH), BF16),
        pltpu.VMEM((4, 8, ROWS), F32),
        pltpu.VMEM((4, 8, ROWS), F32),
        pltpu.VMEM((2, 16, 1024), F32),
        pltpu.VMEM((2, 14, 16, 1024), F32),
        pltpu.VMEM((2, 16, PAIR), F32),
        pltpu.VMEM((2, 16, PAIR), F32),
        *reduce_scratch(COLS, 1792),
        *reduce_scratch(IN_COLS, 1280),
        *reduce_scratch(OUT, 512),
        pltpu.SemaphoreType.DMA((3, 2, GATHER_COPIES)),
        pltpu.SemaphoreType.DMA((3, 2, REDUCE_COPIES)),
        pltpu.SemaphoreType.DMA((2, 24)),
        pltpu.SemaphoreType.DMA((2, 2, 9)),
        pltpu.SemaphoreType.DMA((3,)),
    ]
    vmem = pl.BlockSpec(memory_space=pltpu.VMEM)
    return pl.pallas_call(
        body,
        out_shape=(
            jax.ShapeDtypeStruct((128, WIDTH), BF16),
            jax.ShapeDtypeStruct((128, WIDTH), F32),
            jax.ShapeDtypeStruct((2, 16, COLS), F32),
            jax.ShapeDtypeStruct((2, 16, 1024), F32),
        ),
        in_specs=[vmem, vmem, vmem, pl.BlockSpec(memory_space=pltpu.SMEM), vmem, vmem, vmem],
        out_specs=(vmem, vmem, vmem, vmem),
        scratch_shapes=scratch,
        compiler_params=pltpu.CompilerParams(
            collective_id=0, has_side_effects=True, vmem_limit_bytes=60 << 20
        ),
        name="whole_step",
    )(x_in, cotangent, own, lengths, vec, conv, head)


def shards(
    x_in, cotangent, seq_lengths, gain_in, w_zx, w_bc, w_dt, conv_x, conv_bc,
    bias_x, bias_bc, dt_bias, a_log, skip, gain_gate, w_out,
):
    def wide(part, width):
        return jnp.pad(part, ((0, 0), (0, 0), (0, width - part.shape[-1])))

    own = jnp.concatenate(
        [w_zx.reshape(2, 16, ZX), w_bc, wide(w_dt, DT), jnp.swapaxes(w_out, 1, 2)], axis=2
    )
    vec = jnp.stack([gain_in, gain_gate, jnp.repeat(skip, 64, axis=1)], axis=1)
    vec = jnp.pad(vec, ((0, 0), (0, 5), (0, 0))).astype(F32)
    conv = jnp.concatenate(
        [
            jnp.concatenate([conv_x, conv_bc], axis=2),
            jnp.concatenate([bias_x, bias_bc], axis=1)[:, None, :],
        ],
        axis=1,
    )
    conv = jnp.pad(conv, ((0, 0), (0, 3), (0, 0))).astype(F32)
    head = wide(jnp.stack([dt_bias, a_log], axis=1), 128)
    head = jnp.pad(head, ((0, 0), (0, 6), (0, 0))).astype(F32)
    act_out, grad_in, grad_w, small = whole_step(
        x_in, cotangent, own, seq_lengths, vec, conv, head
    )
    return (
        act_out,
        grad_in,
        small[:, 0],
        grad_w[:, :, :ZX].reshape(2, 16, 2, INNER_OWN),
        grad_w[:, :, ZX : ZX + PAIR],
        grad_w[:, :, ZX + PAIR : ZX + PAIR + HEADS_OWN],
        small[:, 4:8],
        small[:, 8].reshape(2, 4, PAIR),
        small[:, 3],
        small[:, 9, :PAIR],
        small[:, 9, 256 : 256 + HEADS_OWN],
        small[:, 9, 384 : 384 + HEADS_OWN],
        small[:, 2].reshape(2, HEADS_OWN, 64).sum(axis=2),
        small[:, 1],
        jnp.swapaxes(grad_w[:, :, IN_COLS:], 1, 2),
    )


def solution(mesh):
    placed = (
        P(("fsdp", "tp"), None),
        P(("fsdp", "tp"), None),
        P("fsdp", None),
        P(),
        P(None, "fsdp", None, "tp"),
        P(None, "fsdp", None),
        P(None, "fsdp", "tp"),
        P(None, None, "tp"),
        P(),
        P(None, "tp"),
        P(),
        P(None, "tp"),
        P(None, "tp"),
        P(None, "tp"),
        P(None, "tp"),
        P(None, "tp", "fsdp"),
    )
    return jax.shard_map(
        shards,
        mesh=mesh,
        in_specs=placed,
        out_specs=(
            P(("fsdp", "tp"), None),
            P(("fsdp", "tp"), None),
            P(),
            P(None, "fsdp", None, "tp"),
            P(None, "fsdp", None),
            P(None, "fsdp", "tp"),
            P(None, None, "tp"),
            P(),
            P(None, "tp"),
            P(),
            P(None, "tp"),
            P(None, "tp"),
            P(None, "tp"),
            P(None, "tp"),
            P(None, "tp", "fsdp"),
        ),
        check_vma=False,
    )
```

time: 804 us -> 225 us (0.28); the launches traced: 795 us -> 224 us
  waiting for transfers between devices: 153 us -> 0 us
  matrix products: 139 us -> 0 us
  blocking collectives: 131 us -> 0 us
  local copies, waits for them, and re-layouts: 125 us -> 16.2 us
  other arithmetic: 62.3 us -> 3.31 us
  Pallas kernels: 151 us -> 204 us
  between operations: 17.5 us -> 0.81 us
  starting transfers between devices: 15.9 us -> 0 us
    dot_general x50 -> x0, matrix products: 139 us -> none  [the longest x6 35.1 us: one_block(): jnp.einsum('tsh,shp->thp', weights, block_values, precision=highest)]
    psum x1 -> x0, waiting for transfers between devices: 123 us -> none  [shards(): lax.psum((gains_all, taps_x_all, taps_bc_all, shift_x_all, shift_bc_all,...]
    psum x5 -> x0, blocking collectives: 91.6 us -> none  [the longest x1 63.4 us: shards(): lax.psum((gains_all, taps_x_all, taps_bc_all, shift_x_all, shift_bc_all,...]
    pallas_call x2 -> x1, Pallas kernels: 151 us -> 204 us  [whole_step(): pl.pallas_call(body, out_shape=(jax.ShapeDtypeStruct((128, WIDTH), BF16),...]
    slice x29 -> x7, local copies, waits for them, and re-layouts: 48.6 us -> 7.33 us  [the longest x1 1.46 us: shards(): small[:, 4:8]]
    reshape x19 -> x2, local copies, waits for them, and re-layouts: 41.7 us -> 1 us  [the longest x1 0.92 us: shards(): grad_w[:, :, :ZX].reshape(2, 16, 2, INNER_OWN)]
    all_gather x4 -> x0, blocking collectives: 39.7 us -> none  [the longest x2 21.8 us: shards(): gathered = lax.all_gather(normed_own, 'tp', axis=0, tiled=True)]
    reduce_scatter x2 -> x0, waiting for transfers between devices: 20.7 us -> none  [shards(): lax.psum_scatter(partial_mix, 'tp', scatter_dimension=0, tiled=True)]
  transfers between devices with their start and end apart: 7 -> 0, of which waited for: 4 -> 0; matrix products, arithmetic and copies ran while one was open for 5% -> 0% of each run, Pallas kernels for 0% -> 0%
where the time goes in v2:
time: 225 us; the launch traced here: 224 us
  Pallas kernels  204 us (91%)
  local copies, waits for them, and re-layouts  16.2 us (7%)
  other arithmetic  3.31 us (1%)
    pallas_call x1, Pallas kernels, whole_step(): pl.pallas_call(body, out_shape=(jax.ShapeDtypeStruct((128, WIDTH), BF16),...  204 us
    unnamed x37, local copies, waits for them, and re-layouts  5.44 us

profile of v2, /device:TPU:0, one launch (start us, length us, event | category | flops | bytes accessed | tf_op | source)
XLA Modules:
  0.0 224.1 jit_solution(10945714520150667573)
XLA Ops:
  0.6 0.0 copy-start.14
  0.7 0.0 copy-start.15
  0.7 0.0 copy-start.11
  0.7 0.6 copy-done.14
  1.3 0.0 copy-done.15
  1.3 0.0 copy-done.11
  1.4 0.6 copy-done.12
  2.0 0.0 copy-start.9
  2.0 0.0 copy-start.13
  2.0 0.0 copy-start.10
  2.1 0.0 copy-start.8
  2.1 0.0 copy-start.3
  2.1 0.6 pad_convert_fusion.head_ref
  2.7 0.0 copy-done.9
  2.7 0.0 copy-done.13
  2.7 0.1 broadcast_in_dim.6
  2.8 0.1 stack_reshape.4
  2.9 0.0 copy-done.10
  2.9 0.0 copy-start.6
  2.9 0.7 fusion.15.vec_ref
  3.6 0.0 copy-done.8
  3.6 0.0 copy-done.6
  3.6 0.7 fusion.12.conv_ref
  4.3 0.0 copy-done.3
  4.3 0.1 reshape.36
  4.4 0.7 copy-done.4
  5.1 0.0 copy-done.5
  5.1 0.0 copy-done.7
  5.1 0.7 fusion.3.own_ref
  5.8 203.7 %whole_step.1 = (bf16[128,1024]{1,0:T(8,128)(2,1)}, f32[128,1024]{1,0:T(8,128)}, f32[2,16,3456]{2,1,0:T(8,128)}, f32[2,16,1024]{2,1,0:T(8,128)}) custom-call(bf16[128,1024]{1,0:T(8,128)(2,1)} %x_ref.1, bf16[128,1024]{1,0:T(8,128)(2,1)} %cot_ref.1, bf16[2,16,3456]{2,1,0:T(8,128)(2,1)} %fusion.3.own_ref, s32[1,4]{1,0:T(1,128)} %lens_ref.1, ...), custom_call_target="tpu_custom_call" | custom-call | tf_op jit(solution)/shard_map/whole_step/pallas_call | solution.py:865
  209.6 0.0 copy-start.1
  209.6 0.8 slice.46
  210.3 0.6 copy.48
  210.9 1.3 fusion.19
  212.2 1.3 slice.42
  213.5 1.5 slice.43
  215.0 1.1 slice_reduce_fusion
  216.1 0.1 reshape_squeeze.7
  216.2 0.7 reduce_sum.9
  216.8 0.6 reshape_squeeze.6
  217.4 0.6 copy.47
  218.1 0.6 copy_bitcast_fusion
  218.7 1.4 slice.41
  220.0 1.6 slice_bitcast_fusion
  221.6 0.0 copy-done.1
  221.6 0.9 reshape.37
  222.6 0.7 copy.51
  223.3 0.8 copy.52
  (16 shorter events, 0.1 us)
Async XLA Ops:
  0.6 0.7 copy-start.14
  0.7 0.7 copy-start.15
  0.7 0.7 copy-start.11
  1.3 0.7 copy-start.12
  2.0 0.7 copy-start.9
  2.0 0.7 copy-start.13
  2.0 0.8 copy-start.10
  2.1 1.5 copy-start.8
  2.1 2.2 copy-start.3
  2.9 0.7 copy-start.6
  4.3 0.8 copy-start.4
  4.3 0.8 copy-start.5
  4.3 0.8 copy-start.7
  209.6 12.0 %copy-start.1 = (f32[2,16,3456]{2,1,0:T(8,128)S(1)}, f32[2,16,3456]{2,1,0:T(8,128)}, u32[]{:S(2)}) copy-start(f32[2,16,3456]{2,1,0:T(8,128)} %get-tuple-element.22) | copy-start | bytes 1327108
  221.6 1.0 copy-start.2
  221.6 1.6 copy-start

commit v3 on v2

--- a/solution.py
+++ b/solution.py
@@ -57,7 +57,7 @@
     return copy
 
 
-GATHER_COPIES = 28
+GATHER_COPIES = 30
 
 
 class Gather:
@@ -87,14 +87,14 @@
         for copy in self.first:
             copy.wait_recv()
         self.second = []
-        for step in range(1, 4):
+        for slot, step in enumerate((1, 3)):
             ref = self.whole.at[y, :, :, c, :, cols_a]
             self.second.append(
-                send(ref, ref, self.sems, 14 + step - 1, fsdp=index_of((y + step) % 4, z, x, c))
+                send(ref, ref, self.sems, 14 + slot, fsdp=index_of((y + step) % 4, z, x, c))
             )
             ref = self.whole.at[:, :, x, c, :, cols_b]
             self.second.append(
-                send(ref, ref, self.sems, 17 + step - 1, fsdp=index_of(y, z, (x + step) % 4, c))
+                send(ref, ref, self.sems, 16 + slot, fsdp=index_of(y, z, (x + step) % 4, c))
             )
         self.third = []
         self.hand_over(0)
@@ -103,31 +103,51 @@
         y, z, x, c = place()
         cols_a, cols_b = self.cols
         ref = self.whole.at[(y - step + 4) % 4, :, :, c, :, cols_a]
-        self.third.append(send(ref, ref, self.sems, 20 + step, fsdp=index_of(y, z, x, 1 - c)))
+        self.third.append(send(ref, ref, self.sems, 22 + step, fsdp=index_of(y, z, x, 1 - c)))
         ref = self.whole.at[:, :, (x - step + 4) % 4, c, :, cols_b]
-        self.third.append(send(ref, ref, self.sems, 24 + step, fsdp=index_of(y, z, x, 1 - c)))
+        self.third.append(send(ref, ref, self.sems, 26 + step, fsdp=index_of(y, z, x, 1 - c)))
+
+    def relay(self):
+        y, z, x, c = place()
+        cols_a, cols_b = self.cols
+        self.fourth = []
+        for slot, step in enumerate((1, 3)):
+            self.second[2 * slot].wait_recv()
+            ref = self.whole.at[(y - step + 4) % 4, slot, :, c, :, cols_a]
+            self.fourth.append(
+                send(ref, ref, self.sems, 18 + slot, fsdp=index_of((y + step) % 4, z, x, c))
+            )
+            self.second[2 * slot + 1].wait_recv()
+            ref = self.whole.at[:, slot, (x - step + 4) % 4, c, :, cols_b]
+            self.fourth.append(
+                send(ref, ref, self.sems, 20 + slot, fsdp=index_of(y, z, (x + step) % 4, c))
+            )
+        self.hand_over(1)
+        self.hand_over(3)
 
     def core(self):
-        for step in (1, 3, 2):
-            self.second[2 * (step - 1)].wait_recv()
-            self.second[2 * (step - 1) + 1].wait_recv()
-            self.hand_over(step)
+        for copy in self.fourth:
+            copy.wait_recv()
+        self.hand_over(2)
 
     def finish(self):
         for copy in self.third:
             copy.wait_recv()
-        for copy in self.first + self.second + self.third:
+        for copy in self.first + self.second + self.third + self.fourth:
             copy.wait_send()
 
 
-REDUCE_COPIES = 21
+REDUCE_COPIES = 27
 
 
 class Reduce:
-    def __init__(self, grad, from_core, from_line_a, from_line_b, from_plane_a, from_plane_b, sems, half, end):
+    def __init__(
+        self, grad, from_core, from_line_a, from_line_b, from_plane_a, from_plane_b, relay_a, relay_b, sems, half, end
+    ):
         self.grad, self.from_core, self.sems = grad, from_core, sems
         self.line_a, self.line_b = from_line_a, from_line_b
         self.plane_a, self.plane_b = from_plane_a, from_plane_b
+        self.relay_a, self.relay_b = relay_a, relay_b
         self.cols = (pl.ds(0, half), pl.ds(half, end - half))
 
     def core(self):
@@ -154,26 +174,70 @@
             theirs = self.from_core[iy, iz, ix].astype(jnp.float32)
             self.from_core[iy, iz, ix] = (mine + theirs).astype(jnp.bfloat16)
 
-        self.second = []
-        for step in range(1, 4):
-            to = (y + step) % 4
+        self.relays, self.second = [], []
+        for slot, step in enumerate((1, 3)):
+            to, far = (y + step) % 4, (y + 2) % 4
+            where = index_of(to, z, x, c)
+            self.relays.append(
+                send(self.from_core.at[far, slot, :, :, cols_a], self.relay_a.at[slot], self.sems, 1 + slot, fsdp=where)
+            )
             self.second.append(
                 send(
-                    self.from_core.at[to, :, :, :, cols_a],
-                    self.line_a.at[step - 1],
+                    self.from_core.at[to, 1 - slot, :, :, cols_a],
+                    self.line_a.at[slot, 1 - slot],
                     self.sems,
-                    step,
-                    fsdp=index_of(to, z, x, c),
+                    3 + slot,
+                    fsdp=where,
                 )
             )
-            to = (x + step) % 4
+            to, far = (x + step) % 4, (x + 2) % 4
+            where = index_of(y, z, to, c)
+            self.relays.append(
+                send(self.from_core.at[:, slot, far, :, cols_b], self.relay_b.at[slot], self.sems, 5 + slot, fsdp=where)
+            )
             self.second.append(
                 send(
-                    self.from_core.at[:, :, to, :, cols_b],
-                    self.line_b.at[step - 1],
+                    self.from_core.at[:, 1 - slot, to, :, cols_b],
+                    self.line_b.at[slot, :, 1 - slot],
                     self.sems,
-                    3 + step,
-                    fsdp=index_of(y, z, to, c),
+                    7 + slot,
+                    fsdp=where,
+                )
+            )
+
+    def relay(self):
+        y, z, x, c = place()
+        cols_a, cols_b = self.cols
+        for copy in self.relays:
+            copy.wait_recv()
+        for slot, step in enumerate((1, 3)):
+            to_y, to_x = (y + step) % 4, (x + step) % 4
+
+            @pl.loop(0, 4)
+            def _(block):
+                mine = self.from_core[to_y, slot, block, :, cols_a].astype(jnp.float32)
+                mine = mine + self.relay_a[slot, block].astype(jnp.float32)
+                self.from_core[to_y, slot, block, :, cols_a] = mine.astype(jnp.bfloat16)
+                mine = self.from_core[block, slot, to_x, :, cols_b].astype(jnp.float32)
+                mine = mine + self.relay_b[slot, block].astype(jnp.float32)
+                self.from_core[block, slot, to_x, :, cols_b] = mine.astype(jnp.bfloat16)
+
+            self.second.append(
+                send(
+                    self.from_core.at[to_y, slot, :, :, cols_a],
+                    self.line_a.at[slot, slot],
+                    self.sems,
+                    9 + slot,
+                    fsdp=index_of(to_y, z, x, c),
+                )
+            )
+            self.second.append(
+                send(
+                    self.from_core.at[:, slot, to_x, :, cols_b],
+                    self.line_b.at[slot, :, slot],
+                    self.sems,
+                    11 + slot,
+                    fsdp=index_of(y, z, to_x, c),
                 )
             )
 
@@ -187,12 +251,12 @@
         def _(block):
             iz, ix = block // 4, block % 4
             total = self.from_core[y, iz, ix, :, cols_a].astype(jnp.float32)
-            for step in range(3):
+            for step in range(2):
                 total = total + self.line_a[step, iz, ix].astype(jnp.float32)
             self.line_a[0, iz, ix] = total.astype(jnp.bfloat16)
             iy, iz = block // 2, block % 2
             total = self.from_core[iy, iz, x, :, cols_b].astype(jnp.float32)
-            for step in range(3):
+            for step in range(2):
                 total = total + self.line_b[step, iy, iz].astype(jnp.float32)
             self.line_b[0, iy, iz] = total.astype(jnp.bfloat16)
 
@@ -204,7 +268,7 @@
                     self.line_a.at[0, tz, tx],
                     self.plane_a.at[slot],
                     self.sems,
-                    7 + slot,
+                    13 + slot,
                     fsdp=index_of(y, tz, tx, c),
                 )
             )
@@ -215,7 +279,7 @@
                     self.line_b.at[0, ty, tz],
                     self.plane_b.at[slot],
                     self.sems,
-                    14 + slot,
+                    20 + slot,
                     fsdp=index_of(ty, tz, x, c),
                 )
             )
@@ -233,15 +297,16 @@
         for slot in range(7):
             total = total + self.plane_b[slot].astype(jnp.float32)
         out[:, cols_b] = total
-        for copy in self.copies + self.second + self.third:
+        for copy in self.copies + self.relays + self.second + self.third:
             copy.wait_send()
 
 
 ROWS, WIDTH, INNER_OWN, STATE, HEADS_OWN = 256, 1024, 1024, 128, 16
 ZX, PAIR, DT, OUT = 2048, 256, 128, 1024
-IN_COLS = ZX + PAIR + DT
-COLS = IN_COLS + OUT
 SIGNAL = INNER_OWN + PAIR
+XS = SIGNAL + DT
+PARTS = (XS, INNER_OWN, OUT)
+HALVES = (768, 512, 512)
 F32, BF16 = jnp.float32, jnp.bfloat16
 NN = (((1,), (0,)), ((), ()))
 NT = (((1,), (1,)), ((), ()))
@@ -273,23 +338,20 @@
 
 def body(
     x_ref, cot_ref, own_ref, lens_ref, vec_ref, conv_ref, head_ref,
-    act_ref, gin_ref, gw_ref, small_ref,
-    wz0, wo0, w1, hid, norm_t, proj, vals, ssd, ngate, steps, cums, cums_t, scales, gscales, sig_dt,
-    xs, cots, normed, cot_b, cot_t, grad, du, dact, dproj, scores, dscores, mask, same, live, acc, dcum, dstep,
+    act_ref, gin_ref, gx_ref, gg_ref, go_ref, small_ref,
+    wx0, wg0, wo0, wx1, wg1, wo1,
+    hid, norm_t, proj, vals, ssd, ngate, steps, cums, cums_t, scales, gscales, sig_dt,
+    xs, cots, normed, cot_t, grad, dact, dproj, scores, dscores, mask, same, live, acc, dcum, dstep,
     mixs, mixr, row_s, row_r, smalls, slots, bc_s, bc_r,
-    core1, la1, lb1, pa1, pb1, core0, la0, lb0, pa0, pb0, coreo, lao, lbo, pao, pbo,
-    gsem, rsem, tsem, ssem, lsem,
+    *rest,
 ):
+    buffers, (gg0, gx0, gsem, rsem, tsem, ssem, lsem) = rest[:42], rest[42:]
     y, z, x, c = place()
     t = lax.axis_index("tp")
     other = 1 - t
     own_rows = pl.ds(pl.multiple_of(t * 128, 128), 128)
     peer_rows = pl.ds(pl.multiple_of(other * 128, 128), 128)
 
-    def wz(layer, cols):
-        ref = wz0 if layer == 0 else w1
-        return ref.at[:, :, :, :, :, cols]
-
     def load_cols(ref, cols):
         part = ref[:, :, :, :, :, cols]
         return part.reshape(WIDTH, part.shape[-1])
@@ -297,26 +359,31 @@
     def store_cols(ref, cols, part):
         ref[:, :, :, :, :, cols] = part.astype(BF16).reshape(4, 2, 4, 2, 16, part.shape[-1])
 
-    z_ref = (wz0, w1)
-    o_ref = (wo0, w1)
-    o_first = (0, IN_COLS)
-
-    keeps = [
-        pltpu.make_async_copy(own_ref.at[0, :, pl.ds(0, IN_COLS)], wz0.at[y, z, x, c], lsem.at[0]),
-        pltpu.make_async_copy(own_ref.at[0, :, pl.ds(IN_COLS, OUT)], wo0.at[y, z, x, c], lsem.at[1]),
-        pltpu.make_async_copy(own_ref.at[1], w1.at[y, z, x, c], lsem.at[2]),
+    x_w, g_w, o_w = (wx0, wx1), (wg0, wg1), (wo0, wo1)
+    whole = (wx0, wg0, wo0, wx1, wg1, wo1)
+    gate_grads, signal_grads = (gg0, wg1), (gx0, wx1)
+    all_grads = (gx0, gg0, wo0, wx1, wg1, wo1)
+
+    keeps = []
+    for slot, ref in enumerate(whole):
+        first = sum(PARTS[: slot % 3])
+        keeps.append(
+            pltpu.make_async_copy(
+                own_ref.at[slot // 3, :, pl.ds(first, PARTS[slot % 3])],
+                ref.at[y, z, x, c],
+                lsem.at[slot],
+            )
+        )
+        keeps[-1].start()
+    greet_all(True)
+    gather_x0, gather_g0, gather_o0, gather_x1, gather_g1, gather_o1 = [
+        Gather(ref, gsem.at[slot], 0, HALVES[slot % 3], PARTS[slot % 3])
+        for slot, ref in enumerate(whole)
     ]
-    for keep in keeps:
-        keep.start()
-    greet_all(True)
-    for keep in keeps:
+    keeps[0].wait()
+    gather_x0.plane()
+    for keep in keeps[1:]:
         keep.wait()
-    gather_z0 = Gather(wz0, gsem.at[0], 0, 1280, IN_COLS)
-    gather_o0 = Gather(wo0, gsem.at[1], 0, 512, OUT)
-    gather_1 = Gather(w1, gsem.at[2], 0, 1792, COLS)
-    gather_z0.plane()
-    send_x = send(x_ref, xs.at[own_rows], tsem, 0, tp=other)
-    send_cot = send(cot_ref, cots.at[own_rows], tsem, 1, tp=other)
     xs[own_rows, :] = x_ref[...]
     cots[own_rows, :] = cot_ref[...]
 
@@ -375,15 +442,20 @@
     def shift_cols(step):
         return pl.ds(pl.multiple_of(INNER_OWN + step * 256, 256), 256)
 
-    def forward_in(layer):
-        norm_layer(layer)
-
-        @pl.loop(0, 9)
+    def project_gate(layer):
+        @pl.loop(0, 4)
         def _(step):
             cols = tile(step, 256)
-            proj[layer, :, cols] = dot(normed[...], load_cols(z_ref[layer], cols)).astype(BF16)
-
-        raw = dot(normed[...], load_cols(z_ref[layer], pl.ds(ZX + PAIR, DT)))
+            proj[layer, :, cols] = dot(normed[...], load_cols(g_w[layer], cols)).astype(BF16)
+
+    def project_signal(layer):
+        @pl.loop(0, 5)
+        def _(step):
+            part = dot(normed[...], load_cols(x_w[layer], tile(step, 256)))
+            proj[layer, :, shift_cols(step)] = part.astype(BF16)
+
+    def forward_steps(layer):
+        raw = dot(normed[...], load_cols(x_w[layer], pl.ds(SIGNAL, DT)))
         raw = raw.astype(BF16).astype(F32) + head_ref[layer, 0:1, :]
         sig_dt[layer] = jax.nn.sigmoid(raw)
         step_sizes = jnp.maximum(raw, 0.0) + jnp.log1p(jnp.exp(-jnp.abs(raw)))
@@ -413,7 +485,6 @@
 
     def forward_ssd(layer):
         set_scores(layer)
-        acc[...] = jnp.zeros_like(acc)
 
         @pl.loop(0, 8)
         def _(step):
@@ -428,8 +499,15 @@
                 scaled = jnp.where(upper == (half == 1), scaled, 0.0).astype(BF16)
                 total = total + dot(weights, scaled)
             ssd[layer, :, cols] = total
+
+    def forward_gate(layer):
+        acc[...] = jnp.zeros_like(acc)
+
+        @pl.loop(0, 8)
+        def _(step):
+            cols = tile(step, 128)
             gate = proj[layer, :, cols].astype(F32)
-            gated = total * gate * jax.nn.sigmoid(gate)
+            gated = ssd[layer, :, cols] * gate * jax.nn.sigmoid(gate)
             acc[...] += gated * gated
             ngate[:, cols] = (gated * vec_ref[layer, 1:2, cols]).astype(BF16)
 
@@ -453,11 +531,9 @@
             copy.wait_send()
 
     def forward_out(layer, rows):
-        ref, first = o_ref[layer], o_first[layer]
-
         @pl.loop(0, 4)
         def _(step):
-            weight = ref[step, :, :, :, :, pl.ds(first, OUT)].reshape(256, OUT)
+            weight = o_w[layer][step].reshape(256, OUT)
             mixs[layer, :, tile(step, 256)] = dot(ngate[...], weight, NT).astype(BF16)
             mix_copy(layer, step, rows).start()
 
@@ -470,7 +546,13 @@
         part = mixs[layer, rows, :].astype(F32) + mixr[layer, rows, :].astype(F32)
         return part * (gscales[layer, rows, 0:1] * live[rows, 0:1])
 
-    gather_z0.line()
+    gather_x0.line()
+    gather_g0.plane()
+    send_x = send(x_ref, xs.at[own_rows], tsem, 0, tp=other)
+    gather_o0.plane()
+    gather_x0.relay()
+    gather_g0.line()
+    gather_x0.core()
     send_x.wait_recv()
 
     @pl.loop(0, 4)
@@ -478,35 +560,57 @@
         rows = tile(step, 64)
         hid[0, rows, :] = xs[rows, :].astype(F32)
 
-    gather_z0.core()
-    gather_o0.plane()
-    gather_1.plane()
-    gather_z0.finish()
-    forward_in(0)
+    norm_layer(0)
+    gather_x0.finish()
     gather_o0.line()
-    transposed(normed, norm_t.at[0])
+    gather_x1.plane()
+    gather_g1.plane()
+    gather_o1.plane()
+    project_signal(0)
+    gather_g0.relay()
+    forward_steps(0)
     forward_conv(0)
+    gather_g0.core()
+    gather_o0.relay()
+    gather_x1.line()
+    forward_ssd(0)
+    gather_g0.finish()
+    project_gate(0)
+    forward_gate(0)
+    squares_0 = send_rows(0)
     gather_o0.core()
-    gather_1.line()
-    forward_ssd(0)
-    squares_0 = send_rows(0)
+    gather_x1.relay()
+    gather_g1.line()
     gather_o0.finish()
     forward_out(0, pl.ds(0, ROWS))
-    gather_1.core()
+    transposed(normed, norm_t.at[0])
+    gather_x1.core()
+    gather_g1.relay()
+    gather_o1.line()
     take_gate_scale(0, squares_0)
+    gather_x1.finish()
     wait_mix(0, pl.ds(0, ROWS))
+    send_cot = send(cot_ref, cots.at[own_rows], tsem, 1, tp=other)
 
     @pl.loop(0, 4)
     def _(step):
         rows = tile(step, 64)
         hid[1, rows, :] = hid[0, rows, :] + mixed_rows(0, rows)
 
-    gather_1.finish()
-    forward_in(1)
+    norm_layer(1)
+    project_signal(1)
+    gather_g1.core()
+    forward_steps(1)
+    gather_o1.relay()
+    forward_conv(1)
     transposed(normed, norm_t.at[1])
-    forward_conv(1)
     forward_ssd(1)
+    gather_o1.core()
+    gather_g1.finish()
+    project_gate(1)
+    forward_gate(1)
     squares_1 = send_rows(1)
+    gather_o1.finish()
     forward_out(1, peer_rows)
     send_cot.wait_recv()
 
@@ -521,16 +625,15 @@
         @pl.loop(0, 4)
         def _(step):
             rows = tile(step, 64)
-            cot_b[rows, :] = (live[rows, 0:1] * grad[rows, :]).astype(BF16)
-
-        transposed(cot_b, cot_t)
+            normed[rows, :] = (live[rows, 0:1] * grad[rows, :]).astype(BF16)
+
+        transposed(normed, cot_t)
         acc[...] = jnp.zeros_like(acc)
 
         @pl.loop(0, 4)
         def _(step):
             cols = tile(step, 256)
-            first = pl.ds(pl.multiple_of(o_first[layer] + step * 256, 128), 256)
-            d_normed_gate = dot(cot_b[...], load_cols(o_ref[layer], first))
+            d_normed_gate = dot(normed[...], load_cols(o_w[layer], cols))
             gate = proj[layer, :, cols].astype(F32)
             gated = ssd[layer, :, cols] * gate * jax.nn.sigmoid(gate)
             normal = gated * twice(gscales[layer])
@@ -538,17 +641,15 @@
             ngate[:, cols] = (normal * gain).astype(BF16)
             smalls[layer, 1:2, cols] = jnp.sum(d_normed_gate * normal, axis=0, keepdims=True)
             weighted = d_normed_gate * gain
-            du[:, cols] = weighted
+            dact[:, cols] = weighted
             inner = weighted * gated
             acc[...] += inner[:, :128] + inner[:, 128:]
 
     def backward_wo(layer):
-        ref, first = o_ref[layer], o_first[layer]
-
         @pl.loop(0, 4)
         def _(step):
             part = dot(cot_t[tile(step, 256), :], ngate[...]).astype(BF16)
-            ref[step, :, :, :, :, pl.ds(first, OUT)] = part.reshape(2, 4, 2, 16, OUT)
+            o_w[layer][step] = part.reshape(2, 4, 2, 16, OUT)
 
     def backward_ssd(layer, copy, which):
         copy.wait_recv()
@@ -569,7 +670,7 @@
             out = ssd[layer, :, cols]
             sigmoid = jax.nn.sigmoid(gate)
             silu = gate * sigmoid
-            d_gated = gscales[layer] * du[:, cols] - out * silu * acc[...]
+            d_gated = gscales[layer] * dact[:, cols] - out * silu * acc[...]
             d_out = d_gated * silu
             dproj[:, cols] = (d_gated * out * sigmoid * (1.0 + gate * (1.0 - sigmoid))).astype(BF16)
             values = vals[layer, :, cols].astype(F32)
@@ -650,27 +751,31 @@
             smalls[layer, 8:9, pl.ds((3 - back) * PAIR, PAIR)] = d_taps[back]
 
     def backward_in(layer, which, rows):
-        ref = z_ref[layer]
-
         @pl.loop(0, 4)
         def _(step):
             cols = tile(step, 256)
-            weight = ref[step, :, :, :, :, pl.ds(0, IN_COLS)].reshape(256, IN_COLS)
-            part = dot(dproj[...], weight, NT)
+            part = dot(dproj[:, :INNER_OWN], g_w[layer][step].reshape(256, INNER_OWN), NT)
+            part = part + dot(dproj[:, INNER_OWN:], x_w[layer][step].reshape(256, XS), NT)
             mixs[which, :, cols] = part.astype(BF16)
             mix_copy(which, step, rows).start()
             smalls[layer, 0:1, cols] = jnp.sum(
                 part * hid[layer, :, cols] * twice(scales[layer]), axis=0, keepdims=True
             )
 
-    def backward_wz(layer):
-        @pl.loop(0, 9)
+    def backward_wg(layer):
+        @pl.loop(0, 4)
         def _(step):
             cols = tile(step, 256)
-            store_cols(z_ref[layer], cols, dot(norm_t[layer], dproj[:, cols]))
-
-        cols = pl.ds(ZX + PAIR, DT)
-        store_cols(z_ref[layer], cols, dot(norm_t[layer], dproj[:, cols]))
+            store_cols(gate_grads[layer], cols, dot(norm_t[layer], dproj[:, cols]))
+
+    def backward_wx(layer):
+        @pl.loop(0, 5)
+        def _(step):
+            part = dot(norm_t[layer], dproj[:, shift_cols(step)])
+            store_cols(signal_grads[layer], tile(step, 256), part)
+
+        part = dot(norm_t[layer], dproj[:, pl.ds(ZX + PAIR, DT)])
+        store_cols(signal_grads[layer], pl.ds(SIGNAL, DT), part)
 
     def next_grad(layer, which, rows):
         part = mixs[which, rows, :].astype(F32) + mixr[which, rows, :].astype(F32)
@@ -733,20 +838,36 @@
             for copy in self.copies:
                 copy.wait_send()
 
-    reduce_1 = Reduce(w1, core1, la1, lb1, pa1, pb1, rsem.at[0], 1792, COLS)
-    reduce_o0 = Reduce(wo0, coreo, lao, lbo, pao, pbo, rsem.at[1], 512, OUT)
-    reduce_z0 = Reduce(wz0, core0, la0, lb0, pa0, pb0, rsem.at[2], 1280, IN_COLS)
+    reduce_x0, reduce_g0, reduce_o0, reduce_x1, reduce_g1, reduce_o1 = [
+        Reduce(ref, *buffers[7 * slot : 7 * slot + 7], rsem.at[slot], HALVES[slot % 3], PARTS[slot % 3])
+        for slot, ref in enumerate(all_grads)
+    ]
     smalls_1, smalls_0 = Smalls(1), Smalls(0)
+
+    def send_pair(layer):
+        bc_s[layer] = gx_ref[layer, :, pl.ds(INNER_OWN, PAIR)]
+        return send(bc_s.at[layer], bc_r.at[layer], tsem, 6 + layer, tp=other)
+
+    def take_pair(layer, copy):
+        copy.wait_recv()
+        gx_ref[layer, :, pl.ds(INNER_OWN, PAIR)] = bc_s[layer] + bc_r[layer]
+        copy.wait_send()
 
     backward_gate(1)
     inner_1 = send_rows(2)
     backward_wo(1)
+    reduce_o1.core()
     backward_ssd(1, inner_1, 2)
+    reduce_o1.line()
     backward_conv(1)
     backward_in(1, 2, pl.ds(0, ROWS))
-    backward_wz(1)
-    reduce_1.core()
-    smalls_1.core()
+    backward_wg(1)
+    reduce_g1.core()
+    backward_wx(1)
+    reduce_x1.core()
+    reduce_o1.relay()
+    reduce_g1.line()
+    reduce_x1.line()
     wait_mix(2, pl.ds(0, ROWS))
 
     @pl.loop(0, 4)
@@ -754,48 +875,57 @@
         rows = tile(step, 64)
         grad[rows, :] = next_grad(1, 2, rows)
 
-    reduce_1.line()
+    smalls_1.core()
+    backward_gate(0)
+    inner_0 = send_rows(3)
+    reduce_g1.relay()
+    backward_wo(0)
+    reduce_o0.core()
+    reduce_o1.plane()
     smalls_1.along_x()
     wait_mix(1, peer_rows)
     act_ref[...] = (hid[1, own_rows, :] + mixed_rows(1, own_rows)).astype(BF16)
-
-    backward_gate(0)
-    inner_0 = send_rows(3)
-    backward_wo(0)
-    reduce_o0.core()
+    reduce_x1.relay()
     backward_ssd(0, inner_0, 3)
+    reduce_o0.line()
+    reduce_g1.plane()
+    reduce_x1.plane()
     smalls_1.along_y()
-    reduce_1.plane()
-    reduce_o0.line()
+    backward_wg(0)
+    reduce_g0.core()
     backward_conv(0)
+    backward_wx(0)
+    reduce_x0.core()
+    reduce_o0.relay()
+    reduce_g0.line()
+    backward_in(0, 3, peer_rows)
+    smalls_0.core()
+    reduce_x0.line()
+    reduce_o1.finish(go_ref.at[1])
+    reduce_g0.relay()
     smalls_1.along_z()
-    backward_in(0, 3, peer_rows)
+    smalls_0.along_x()
     reduce_o0.plane()
-    reduce_1.finish(gw_ref.at[1])
-    bc_s[1] = gw_ref[1, :, pl.ds(ZX, PAIR)]
-    bc_1 = send(bc_s.at[1], bc_r.at[1], tsem, 6, tp=other)
+    reduce_g1.finish(gg_ref.at[1])
+    reduce_x1.finish(gx_ref.at[1])
+    pair_1 = send_pair(1)
+    reduce_x0.relay()
+    reduce_g0.plane()
+    smalls_0.along_y()
     smalls_1.across()
-    backward_wz(0)
-    reduce_z0.core()
-    smalls_0.core()
     wait_mix(3, peer_rows)
     gin_ref[...] = next_grad(0, 3, own_rows)
-    reduce_z0.line()
-    smalls_0.along_x()
+    reduce_o0.finish(go_ref.at[0])
+    reduce_x0.plane()
+    smalls_0.along_z()
+    take_pair(1, pair_1)
     smalls_1.finish()
-    reduce_o0.finish(gw_ref.at[0, :, pl.ds(IN_COLS, OUT)])
-    smalls_0.along_y()
-    reduce_z0.plane()
-    smalls_0.along_z()
-    reduce_z0.finish(gw_ref.at[0, :, pl.ds(0, IN_COLS)])
-    bc_s[0] = gw_ref[0, :, pl.ds(ZX, PAIR)]
-    bc_0 = send(bc_s.at[0], bc_r.at[0], tsem, 7, tp=other)
+    reduce_g0.finish(gg_ref.at[0])
     smalls_0.across()
-    for layer, copy in ((1, bc_1), (0, bc_0)):
-        copy.wait_recv()
-        gw_ref[layer, :, pl.ds(ZX, PAIR)] = bc_s[layer] + bc_r[layer]
-        copy.wait_send()
+    reduce_x0.finish(gx_ref.at[0])
+    pair_0 = send_pair(0)
     smalls_0.finish()
+    take_pair(0, pair_0)
     for copy in (send_x, send_cot, squares_0, squares_1, inner_1, inner_0):
         copy.wait_send()
 
@@ -803,18 +933,18 @@
 def reduce_scratch(width, half):
     return [
         pltpu.VMEM((4, 2, 4, 16, width), BF16),
-        pltpu.VMEM((3, 2, 4, 16, half), BF16),
-        pltpu.VMEM((3, 4, 2, 16, width - half), BF16),
+        pltpu.VMEM((2, 2, 4, 16, half), BF16),
+        pltpu.VMEM((2, 4, 2, 16, width - half), BF16),
         pltpu.VMEM((7, 16, half), BF16),
         pltpu.VMEM((7, 16, width - half), BF16),
+        pltpu.VMEM((2, 4, 16, half), BF16),
+        pltpu.VMEM((2, 4, 16, width - half), BF16),
     ]
 
 
 def whole_step(x_in, cotangent, own, lengths, vec, conv, head):
     scratch = [
-        pltpu.VMEM((4, 2, 4, 2, 16, IN_COLS), BF16),
-        pltpu.VMEM((4, 2, 4, 2, 16, OUT), BF16),
-        pltpu.VMEM((4, 2, 4, 2, 16, COLS), BF16),
+        *[pltpu.VMEM((4, 2, 4, 2, 16, width), BF16) for width in PARTS + PARTS],
         pltpu.VMEM((2, ROWS, WIDTH), F32),
         pltpu.VMEM((2, WIDTH, ROWS), BF16),
         pltpu.VMEM((2, ROWS, ZX + PAIR), BF16),
@@ -830,12 +960,10 @@
         pltpu.VMEM((ROWS, WIDTH), BF16),
         pltpu.VMEM((ROWS, WIDTH), BF16),
         pltpu.VMEM((ROWS, WIDTH), BF16),
-        pltpu.VMEM((ROWS, WIDTH), BF16),
         pltpu.VMEM((WIDTH, ROWS), BF16),
         pltpu.VMEM((ROWS, WIDTH), F32),
-        pltpu.VMEM((ROWS, INNER_OWN), F32),
         pltpu.VMEM((ROWS, SIGNAL), F32),
-        pltpu.VMEM((ROWS, IN_COLS), BF16),
+        pltpu.VMEM((ROWS, INNER_OWN + XS), BF16),
         pltpu.VMEM((ROWS, ROWS), F32),
         pltpu.VMEM((ROWS, ROWS), F32),
         pltpu.VMEM((ROWS, ROWS), F32),
@@ -852,14 +980,18 @@
         pltpu.VMEM((2, 14, 16, 1024), F32),
         pltpu.VMEM((2, 16, PAIR), F32),
         pltpu.VMEM((2, 16, PAIR), F32),
-        *reduce_scratch(COLS, 1792),
-        *reduce_scratch(IN_COLS, 1280),
-        *reduce_scratch(OUT, 512),
-        pltpu.SemaphoreType.DMA((3, 2, GATHER_COPIES)),
-        pltpu.SemaphoreType.DMA((3, 2, REDUCE_COPIES)),
+        *[
+            buffer
+            for width, half in zip(PARTS + PARTS, HALVES + HALVES)
+            for buffer in reduce_scratch(width, half)
+        ],
+        pltpu.VMEM((4, 2, 4, 2, 16, INNER_OWN), BF16),
+        pltpu.VMEM((4, 2, 4, 2, 16, XS), BF16),
+        pltpu.SemaphoreType.DMA((6, 2, GATHER_COPIES)),
+        pltpu.SemaphoreType.DMA((6, 2, REDUCE_COPIES)),
         pltpu.SemaphoreType.DMA((2, 24)),
         pltpu.SemaphoreType.DMA((2, 2, 9)),
-        pltpu.SemaphoreType.DMA((3,)),
+        pltpu.SemaphoreType.DMA((6,)),
     ]
     vmem = pl.BlockSpec(memory_space=pltpu.VMEM)
     return pl.pallas_call(
@@ -867,11 +999,13 @@
         out_shape=(
             jax.ShapeDtypeStruct((128, WIDTH), BF16),
             jax.ShapeDtypeStruct((128, WIDTH), F32),
-            jax.ShapeDtypeStruct((2, 16, COLS), F32),
+            jax.ShapeDtypeStruct((2, 16, XS), F32),
+            jax.ShapeDtypeStruct((2, 16, INNER_OWN), F32),
+            jax.ShapeDtypeStruct((2, 16, OUT), F32),
             jax.ShapeDtypeStruct((2, 16, 1024), F32),
         ),
         in_specs=[vmem, vmem, vmem, pl.BlockSpec(memory_space=pltpu.SMEM), vmem, vmem, vmem],
-        out_specs=(vmem, vmem, vmem, vmem),
+        out_specs=(vmem,) * 6,
         scratch_shapes=scratch,
         compiler_params=pltpu.CompilerParams(
             collective_id=0, has_side_effects=True, vmem_limit_bytes=60 << 20
@@ -880,6 +1014,55 @@
     )(x_in, cotangent, own, lengths, vec, conv, head)
 
 
+def finish_kernel(
+    act_ref, gin_ref, gx_ref, gg_ref, go_ref, small_ref,
+    act_out, grad_in, gain_in, w_zx, w_bc, w_dt, conv_x, conv_bc,
+    bias_x, bias_bc, dt_bias, a_log, skip, gain_gate, w_out,
+):
+    w_out[...] = go_ref[...]
+    act_out[...] = act_ref[...]
+    grad_in[...] = gin_ref[...]
+    w_bc[...] = gx_ref[:, :, INNER_OWN:SIGNAL]
+    w_dt[...] = gx_ref[:, :, SIGNAL : SIGNAL + HEADS_OWN]
+    channel = lax.broadcasted_iota(jnp.int32, (INNER_OWN, 128), 0) // 64
+    head = lax.broadcasted_iota(jnp.int32, (INNER_OWN, 128), 1)
+    members = (channel == head).astype(F32)
+    for layer in range(2):
+        for row in range(16):
+            w_zx[layer, row, 0:1, :] = gg_ref[layer, row : row + 1, :]
+            w_zx[layer, row, 1:2, :] = gx_ref[layer, row : row + 1, :INNER_OWN]
+        one = slice(layer, layer + 1)
+        gain_in[one, :] = small_ref[layer, 0:1, :]
+        gain_gate[one, :] = small_ref[layer, 1:2, :]
+        by_head = exact_dot(small_ref[layer], members)
+        skip[one, :] = by_head[2:3, :HEADS_OWN]
+        bias_x[one, :] = small_ref[layer, 3:4, :]
+        conv_x[layer] = small_ref[layer, 4:8, :]
+        for tap in range(4):
+            conv_bc[layer, tap : tap + 1, :] = small_ref[layer, 8:9, tap * PAIR : (tap + 1) * PAIR]
+        bias_bc[one, :] = small_ref[layer, 9:10, :PAIR]
+        dt_bias[one, :] = small_ref[layer, 9:10, 256 : 256 + HEADS_OWN]
+        a_log[one, :] = small_ref[layer, 9:10, 384 : 384 + HEADS_OWN]
+
+
+def finish_step(*parts):
+    shapes = [
+        ((128, WIDTH), BF16), ((128, WIDTH), F32), ((2, WIDTH), F32), ((2, 16, 2, INNER_OWN), F32),
+        ((2, 16, PAIR), F32), ((2, 16, HEADS_OWN), F32), ((2, 4, INNER_OWN), F32), ((2, 4, PAIR), F32),
+        ((2, INNER_OWN), F32), ((2, PAIR), F32), ((2, HEADS_OWN), F32), ((2, HEADS_OWN), F32),
+        ((2, HEADS_OWN), F32), ((2, INNER_OWN), F32), ((2, 16, INNER_OWN), F32),
+    ]
+    vmem = pl.BlockSpec(memory_space=pltpu.VMEM)
+    return pl.pallas_call(
+        finish_kernel,
+        out_shape=[jax.ShapeDtypeStruct(*shape) for shape in shapes],
+        in_specs=[vmem] * 6,
+        out_specs=[vmem] * 15,
+        compiler_params=pltpu.CompilerParams(vmem_limit_bytes=60 << 20),
+        name="finish_step",
+    )(*parts)
+
+
 def shards(
     x_in, cotangent, seq_lengths, gain_in, w_zx, w_bc, w_dt, conv_x, conv_bc,
     bias_x, bias_bc, dt_bias, a_log, skip, gain_gate, w_out,
@@ -888,7 +1071,7 @@
         return jnp.pad(part, ((0, 0), (0, 0), (0, width - part.shape[-1])))
 
     own = jnp.concatenate(
-        [w_zx.reshape(2, 16, ZX), w_bc, wide(w_dt, DT), jnp.swapaxes(w_out, 1, 2)], axis=2
+        [w_zx[:, :, 1], w_bc, wide(w_dt, DT), w_zx[:, :, 0], jnp.swapaxes(w_out, 1, 2)], axis=2
     )
     vec = jnp.stack([gain_in, gain_gate, jnp.repeat(skip, 64, axis=1)], axis=1)
     vec = jnp.pad(vec, ((0, 0), (0, 5), (0, 0))).astype(F32)
@@ -902,26 +1085,9 @@
     conv = jnp.pad(conv, ((0, 0), (0, 3), (0, 0))).astype(F32)
     head = wide(jnp.stack([dt_bias, a_log], axis=1), 128)
     head = jnp.pad(head, ((0, 0), (0, 6), (0, 0))).astype(F32)
-    act_out, grad_in, grad_w, small = whole_step(
-        x_in, cotangent, own, seq_lengths, vec, conv, head
-    )
-    return (
-        act_out,
-        grad_in,
-        small[:, 0],
-        grad_w[:, :, :ZX].reshape(2, 16, 2, INNER_OWN),
-        grad_w[:, :, ZX : ZX + PAIR],
-        grad_w[:, :, ZX + PAIR : ZX + PAIR + HEADS_OWN],
-        small[:, 4:8],
-        small[:, 8].reshape(2, 4, PAIR),
-        small[:, 3],
-        small[:, 9, :PAIR],
-        small[:, 9, 256 : 256 + HEADS_OWN],
-        small[:, 9, 384 : 384 + HEADS_OWN],
-        small[:, 2].reshape(2, HEADS_OWN, 64).sum(axis=2),
-        small[:, 1],
-        jnp.swapaxes(grad_w[:, :, IN_COLS:], 1, 2),
-    )
+    parts = whole_step(x_in, cotangent, own, seq_lengths, vec, conv, head)
+    done = finish_step(*parts)
+    return (*done[:-1], jnp.swapaxes(done[-1], 1, 2))
 
 
 def solution(mesh):

time: 225 us -> 171 us (0.76)
  Pallas kernels: 204 us -> 163 us
  local copies, waits for them, and re-layouts: 16.2 us -> 4.7 us
    pallas_call x1, Pallas kernels: 204 us -> 160 us  [whole_step(): pl.pallas_call(body, out_shape=(jax.ShapeDtypeStruct((128, WIDTH), BF16),...]
    slice x7 -> x1, local copies, waits for them, and re-layouts: 7.33 us -> 0.18 us  [shards(): w_zx[:, :, 0]]
    pallas_call x0 -> x1, Pallas kernels: none -> 2.88 us  [finish_step(): pl.pallas_call(finish_kernel, out_shape=[jax.ShapeDtypeStruct(*shape) for...]
    unnamed x37 -> x32, local copies, waits for them, and re-layouts: 5.44 us -> 4.31 us
where the time goes in v3:
time: 171 us
  Pallas kernels  163 us (95%)
  local copies, waits for them, and re-layouts  4.7 us (3%)
  other arithmetic  1.95 us (1%)
    pallas_call x1, Pallas kernels, whole_step(): pl.pallas_call(body, out_shape=(jax.ShapeDtypeStruct((128, WIDTH), BF16),...  160 us
    unnamed x32, local copies, waits for them, and re-layouts  4.31 us

profile of v3, /device:TPU:0, one launch (start us, length us, event | category | flops | bytes accessed | tf_op | source)
XLA Modules:
  0.0 170.9 jit_solution(4696694806590504170)
XLA Ops:
  0.6 0.0 copy-start.12
  0.7 0.0 copy-start.13
  0.7 0.0 copy-start.9
  0.7 0.6 copy-done.12
  1.3 0.0 copy-done.13
  1.3 0.0 copy-start.10
  1.3 0.0 copy-done.9
  1.4 0.6 copy-done.10
  2.0 0.0 copy-start.7
  2.0 0.0 copy-start.11
  2.0 0.0 copy-start.8
  2.1 0.0 copy-start.6
  2.1 0.0 copy-start
  2.1 0.6 pad_convert_fusion.head_ref
  2.7 0.0 copy-done.7
  2.7 0.0 copy-done.11
  2.7 0.1 broadcast_in_dim.6
  2.8 0.1 stack_reshape.4
  2.9 0.0 copy-done.8
  2.9 0.0 copy-start.3
  2.9 0.7 fusion.13.vec_ref
  3.6 0.0 copy-done.6
  3.6 0.0 copy-done.3
  3.6 0.7 fusion.10.conv_ref
  4.3 0.0 copy-done
  4.3 0.2 fusion.17
  4.5 0.0 copy-start.4
  4.5 0.7 copy-done.4
  5.2 0.0 copy-start.5
  5.2 0.7 copy-done.5
  5.9 0.0 copy-start.2
  5.9 0.8 copy-done.2
  6.8 0.0 copy-start.1
  6.8 0.7 copy-done.1
  7.4 160.5 %whole_step.1 = (bf16[128,1024]{1,0:T(8,128)(2,1)}, f32[128,1024]{1,0:T(8,128)}, f32[2,16,1408]{2,1,0:T(8,128)}, f32[2,16,1024]{2,1,0:T(8,128)}, f32[2,16,1024]{2,1,0:T(8,128)}, /*index=5*/f32[2,16,1024]{2,1,0:T(8,128)}) custom-call(bf16[128,1024]{1,0:T(8,128)(2,1)} %x_ref.1, bf16[128,1024]{1,0:T(8,128)(2,1)} %cot_ref.1, bf16[2,16,3456]{2,1,0:T(8,128)(2,1)} %copy-done.1, ...), custom_call_target="tpu_custom_call" | custom-call | tf_op jit(solution)/shard_map/whole_step/pallas_call | solution.py:997
  167.9 2.9 %finish_step.1 = (bf16[128,1024]{1,0:T(8,128)(2,1)}, f32[128,1024]{1,0:T(8,128)}, f32[2,1024]{1,0:T(2,128)}, f32[2,16,2,1024]{3,2,1,0:T(2,128)}, f32[2,16,256]{2...) custom-call(bf16[128,1024]{1,0:T(8,128)(2,1)} %get-tuple-element.36., ...), custom_call_target="tpu_custom_call" | custom-call | tf_op jit(solution)/shard_map/finish_step/pallas_call | solution.py:1056
  (12 shorter events, 0.1 us)
Async XLA Ops:
  0.6 0.7 copy-start.12
  0.7 0.7 copy-start.13
  0.7 0.7 copy-start.9
  1.3 0.7 copy-start.10
  2.0 0.7 copy-start.7
  2.0 0.7 copy-start.11
  2.0 0.8 copy-start.8
  2.1 1.5 copy-start.6
  2.1 2.2 %copy-start = (bf16[2,16,2,1024]{3,2,1,0:T(2,128)(2,1)S(1)}, bf16[2,16,2,1024]{3,2,1,0:T(2,128)(2,1)}, u32[]{:S(2)}) copy-start(bf16[2,16,2,1024]{3,2,1,0:T(2,128)(2,1)} %param.20) | copy-start | bytes 393220
  2.9 0.7 copy-start.3
  4.5 0.7 copy-start.4
  5.2 0.7 copy-start.5
  5.9 0.8 copy-start.2
  6.8 0.7 copy-start.1

commit v4 on v3

--- a/solution.py
+++ b/solution.py
@@ -66,10 +66,30 @@
         self.cols = (pl.ds(first, half - first), pl.ds(half, end - half))
         self.started = []
 
+    def pair(self):
+        y, z, x, c = place()
+        ref = self.whole.at[y, z, x, c]
+        self.pairs = [send(ref, ref, self.sems, 0, fsdp=index_of(y, 1 - z, x, c))]
+
+    def spread(self):
+        y, z, x, c = place()
+        cols_a, cols_b = self.cols
+        self.pairs[0].wait_recv()
+        self.first = []
+        for step in range(1, 4):
+            ref = self.whole.at[y, :, x, c, :, cols_a]
+            self.first.append(
+                send(ref, ref, self.sems, step, fsdp=index_of(y, z, (x + step) % 4, c))
+            )
+            ref = self.whole.at[y, :, x, c, :, cols_b]
+            self.first.append(
+                send(ref, ref, self.sems, 3 + step, fsdp=index_of((y + step) % 4, z, x, c))
+            )
+
     def plane(self):
         y, z, x, c = place()
         cols_a, cols_b = self.cols
-        self.first = []
+        self.pairs, self.first = [], []
         for slot, (dz, dx) in enumerate(PLANE_ZX):
             ref = self.whole.at[y, z, x, c, :, cols_a]
             self.first.append(
@@ -133,7 +153,7 @@
     def finish(self):
         for copy in self.third:
             copy.wait_recv()
-        for copy in self.first + self.second + self.third + self.fourth:
+        for copy in self.pairs + self.first + self.second + self.third + self.fourth:
             copy.wait_send()
 
 
@@ -331,16 +351,29 @@
     return jnp.concatenate([part, part], axis=1)
 
 
-def column(part, head):
-    lane = lax.broadcasted_iota(jnp.int32, part.shape, 1)
-    return jnp.sum(jnp.where(lane == head, part, 0.0), axis=1, keepdims=True)
+def three_parts(value):
+    high = value.astype(BF16)
+    rest = value - high.astype(F32)
+    middle = rest.astype(BF16)
+    return high, middle, (rest - middle.astype(F32)).astype(BF16)
+
+
+def parts_by_lane(value):
+    lane = lax.broadcasted_iota(jnp.int32, value.shape, 1)
+    terms = [part.astype(F32) for part in three_parts(jnp.where(lane < 16, value, 0.0))]
+    return (terms[0] + pltpu.roll(terms[1], 16, 1) + pltpu.roll(terms[2], 32, 1)).astype(BF16)
+
+
+def picked(parts, heads):
+    row = lax.broadcasted_iota(jnp.int32, heads.shape, 0)
+    return dot(parts, jnp.where(((row & 15) == heads) & (row < 48), 1.0, 0.0).astype(BF16))
 
 
 def body(
     x_ref, cot_ref, own_ref, lens_ref, vec_ref, conv_ref, head_ref,
     act_ref, gin_ref, gx_ref, gg_ref, go_ref, small_ref,
     wx0, wg0, wo0, wx1, wg1, wo1,
-    hid, norm_t, proj, vals, ssd, ngate, steps, cums, cums_t, scales, gscales, sig_dt,
+    hid, norm_t, proj, vals, ssd, ngate, steps, step_parts, cum_parts, cums_t, scales, gscales, sig_dt,
     xs, cots, normed, cot_t, grad, dact, dproj, scores, dscores, mask, same, live, acc, dcum, dstep,
     mixs, mixr, row_s, row_r, smalls, slots, bc_s, bc_r,
     *rest,
@@ -384,6 +417,8 @@
     gather_x0.plane()
     for keep in keeps[1:]:
         keep.wait()
+    gather_g0.pair()
+    gather_o0.pair()
     xs[own_rows, :] = x_ref[...]
     cots[own_rows, :] = cot_ref[...]
 
@@ -463,7 +498,8 @@
         rate = -jnp.exp(head_ref[layer, 1:2, :])
         lower = (src <= at).astype(F32)
         summed = exact_dot(lower, step_sizes * rate)
-        cums[layer] = summed
+        cum_parts[layer] = parts_by_lane(summed)
+        step_parts[layer] = parts_by_lane(step_sizes)
         cums_t[layer] = summed.T
 
     def forward_conv(layer):
@@ -479,9 +515,13 @@
         scores[...] = dot(c_mat, b_mat, NT)
 
     def decays(layer, head):
+        heads = jnp.full((128, ROWS), head, jnp.int32)
         return jnp.exp(
-            column(cums[layer], head) - cums_t[layer, pl.ds(head, 1), :] + mask[...]
+            picked(cum_parts[layer], heads) - cums_t[layer, pl.ds(head, 1), :] + mask[...]
         )
+
+    def pair_heads(step):
+        return 2 * step + lax.broadcasted_iota(jnp.int32, (128, 128), 1) // 64
 
     def forward_ssd(layer):
         set_scores(layer)
@@ -492,12 +532,11 @@
             values = vals[layer, :, cols].astype(F32)
             upper = lax.broadcasted_iota(jnp.int32, (ROWS, 128), 1) >= 64
             total = vec_ref[layer, 2:3, cols] * values
+            scaled = values * picked(step_parts[layer], pair_heads(step))
             for half in range(2):
-                head = 2 * step + half
-                weights = (scores[...] * decays(layer, head)).astype(BF16)
-                scaled = values * column(steps[layer], head)
-                scaled = jnp.where(upper == (half == 1), scaled, 0.0).astype(BF16)
-                total = total + dot(weights, scaled)
+                weights = (scores[...] * decays(layer, 2 * step + half)).astype(BF16)
+                mine = jnp.where(upper == (half == 1), scaled, 0.0).astype(BF16)
+                total = total + dot(weights, mine)
             ssd[layer, :, cols] = total
 
     def forward_gate(layer):
@@ -547,12 +586,15 @@
         return part * (gscales[layer, rows, 0:1] * live[rows, 0:1])
 
     gather_x0.line()
-    gather_g0.plane()
+    gather_g0.spread()
+    gather_o0.spread()
     send_x = send(x_ref, xs.at[own_rows], tsem, 0, tp=other)
-    gather_o0.plane()
     gather_x0.relay()
     gather_g0.line()
     gather_x0.core()
+    gather_o0.line()
+    for job in (gather_x1, gather_g1, gather_o1):
+        job.pair()
     send_x.wait_recv()
 
     @pl.loop(0, 4)
@@ -562,23 +604,21 @@
 
     norm_layer(0)
     gather_x0.finish()
-    gather_o0.line()
-    gather_x1.plane()
-    gather_g1.plane()
-    gather_o1.plane()
+    gather_g0.relay()
+    for job in (gather_x1, gather_g1, gather_o1):
+        job.spread()
     project_signal(0)
-    gather_g0.relay()
+    gather_g0.core()
+    gather_o0.relay()
     forward_steps(0)
     forward_conv(0)
-    gather_g0.core()
-    gather_o0.relay()
     gather_x1.line()
+    gather_o0.core()
     forward_ssd(0)
     gather_g0.finish()
     project_gate(0)
     forward_gate(0)
     squares_0 = send_rows(0)
-    gather_o0.core()
     gather_x1.relay()
     gather_g1.line()
     gather_o0.finish()
@@ -627,7 +667,6 @@
             rows = tile(step, 64)
             normed[rows, :] = (live[rows, 0:1] * grad[rows, :]).astype(BF16)
 
-        transposed(normed, cot_t)
         acc[...] = jnp.zeros_like(acc)
 
         @pl.loop(0, 4)
@@ -646,12 +685,14 @@
             acc[...] += inner[:, :128] + inner[:, 128:]
 
     def backward_wo(layer):
+        transposed(normed, cot_t)
+
         @pl.loop(0, 4)
         def _(step):
             part = dot(cot_t[tile(step, 256), :], ngate[...]).astype(BF16)
             o_w[layer][step] = part.reshape(2, 4, 2, 16, OUT)
 
-    def backward_ssd(layer, copy, which):
+    def backward_ssd(layer, copy, which, between):
         copy.wait_recv()
         inner = spread_rows(row_s[which] + row_r[which])
         gs = gscales[layer]
@@ -661,11 +702,9 @@
         dcum[...] = jnp.zeros_like(dcum)
         dstep[...] = jnp.zeros_like(dstep)
 
-        @pl.loop(0, 8)
-        def _(step):
+        def one(step):
             cols = tile(step, 128)
-            lane = lax.broadcasted_iota(jnp.int32, (ROWS, 128), 1)
-            upper = lane >= 64
+            upper = lax.broadcasted_iota(jnp.int32, (ROWS, 128), 1) >= 64
             gate = proj[layer, :, cols].astype(F32)
             out = ssd[layer, :, cols]
             sigmoid = jax.nn.sigmoid(gate)
@@ -674,9 +713,7 @@
             d_out = d_gated * silu
             dproj[:, cols] = (d_gated * out * sigmoid * (1.0 + gate * (1.0 - sigmoid))).astype(BF16)
             values = vals[layer, :, cols].astype(F32)
-            size = jnp.where(
-                upper, column(steps[layer], 2 * step + 1), column(steps[layer], 2 * step)
-            )
+            size = picked(step_parts[layer], pair_heads(step))
             scaled = (values * size).astype(BF16)
             back = jnp.zeros((ROWS, 128), F32)
             for half in range(2):
@@ -692,20 +729,17 @@
             inside = out - skip * values
             turn = d_out.astype(BF16).astype(F32) * inside - scaled.astype(F32) * back
             size_turn = values * back
-            for half in range(2):
-                head = 2 * step + half
-                mine = upper == (half == 1)
-                dcum[...] += jnp.where(
-                    lane == head,
-                    jnp.sum(jnp.where(mine, turn, 0.0), axis=1, keepdims=True),
-                    0.0,
-                )
-                dstep[...] += jnp.where(
-                    lane == head,
-                    jnp.sum(jnp.where(mine, size_turn, 0.0), axis=1, keepdims=True),
-                    0.0,
-                )
-
+            lane = lax.broadcasted_iota(jnp.int32, (128, 128), 0)
+            to = lax.broadcasted_iota(jnp.int32, (128, 128), 1)
+            members = jnp.where(to == 2 * step + lane // 64, 1.0, 0.0).astype(BF16)
+            for part in three_parts(turn):
+                dcum[...] += dot(part, members)
+            for part in three_parts(size_turn)[:2]:
+                dstep[...] += dot(part, members)
+
+        pl.loop(0, 4)(one)
+        between()
+        pl.loop(4, 8)(one)
         rate = -jnp.exp(head_ref[layer, 1:2, :])
         later = (src >= at).astype(F32)
         d_log = exact_dot(later, dcum[...])
@@ -857,7 +891,7 @@
     inner_1 = send_rows(2)
     backward_wo(1)
     reduce_o1.core()
-    backward_ssd(1, inner_1, 2)
+    backward_ssd(1, inner_1, 2, lambda: None)
     reduce_o1.line()
     backward_conv(1)
     backward_in(1, 2, pl.ds(0, ROWS))
@@ -886,7 +920,7 @@
     wait_mix(1, peer_rows)
     act_ref[...] = (hid[1, own_rows, :] + mixed_rows(1, own_rows)).astype(BF16)
     reduce_x1.relay()
-    backward_ssd(0, inner_0, 3)
+    backward_ssd(0, inner_0, 3, lambda: None)
     reduce_o0.line()
     reduce_g1.plane()
     reduce_x1.plane()
@@ -952,7 +986,8 @@
         pltpu.VMEM((2, ROWS, INNER_OWN), F32),
         pltpu.VMEM((ROWS, INNER_OWN), BF16),
         pltpu.VMEM((2, ROWS, 128), F32),
-        pltpu.VMEM((2, ROWS, 128), F32),
+        pltpu.VMEM((2, ROWS, 128), BF16),
+        pltpu.VMEM((2, ROWS, 128), BF16),
         pltpu.VMEM((2, 128, ROWS), F32),
         pltpu.VMEM((2, ROWS, 128), F32),
         pltpu.VMEM((2, ROWS, 128), F32),
@@ -1063,28 +1098,66 @@
     )(*parts)
 
 
+def pack_kernel(
+    gain_in, w_zx, w_bc, w_dt, conv_x, conv_bc, bias_x, bias_bc, dt_bias, a_log, skip, gain_gate, w_out,
+    own, vec, conv, head,
+):
+    heads = lax.broadcasted_iota(jnp.int32, (HEADS_OWN, INNER_OWN), 0)
+    channel = lax.broadcasted_iota(jnp.int32, (HEADS_OWN, INNER_OWN), 1)
+    members = jnp.where(heads == channel // 64, 1.0, 0.0)
+    skips = exact_dot(skip[...].astype(F32), members)
+    gains, gates = gain_in[...].astype(F32), gain_gate[...].astype(F32)
+    shift_x, shift_bc = bias_x[...].astype(F32), bias_bc[...].astype(F32)
+    sizes, rates = dt_bias[...].astype(F32), a_log[...].astype(F32)
+    own[...] = jnp.zeros_like(own)
+    vec[...] = jnp.zeros_like(vec)
+    conv[...] = jnp.zeros_like(conv)
+    head[...] = jnp.zeros_like(head)
+    gate_at, out_at = XS, XS + INNER_OWN
+    for layer in range(2):
+        one = slice(layer, layer + 1)
+        rows = [w_zx[layer, row].astype(F32) for row in range(16)]
+        own[layer, :, :INNER_OWN] = jnp.concatenate([row[1:2] for row in rows], axis=0).astype(BF16)
+        own[layer, :, INNER_OWN:SIGNAL] = w_bc[layer]
+        own[layer, :, SIGNAL : SIGNAL + HEADS_OWN] = w_dt[layer]
+        own[layer, :, gate_at:out_at] = jnp.concatenate([row[0:1] for row in rows], axis=0).astype(BF16)
+        own[layer, :, out_at:] = w_out[layer]
+        vec[layer, 0:1, :] = gains[one]
+        vec[layer, 1:2, :] = gates[one]
+        vec[layer, 2:3, :] = skips[one]
+        conv[layer, 0:4, :INNER_OWN] = conv_x[layer].astype(F32)
+        conv[layer, 0:4, INNER_OWN:] = conv_bc[layer].astype(F32)
+        conv[layer, 4:5, :INNER_OWN] = shift_x[one]
+        conv[layer, 4:5, INNER_OWN:] = shift_bc[one]
+        head[layer, 0:1, :HEADS_OWN] = sizes[one]
+        head[layer, 1:2, :HEADS_OWN] = rates[one]
+
+
+def pack_step(*params):
+    vmem = pl.BlockSpec(memory_space=pltpu.VMEM)
+    return pl.pallas_call(
+        pack_kernel,
+        out_shape=[
+            jax.ShapeDtypeStruct((2, 16, XS + INNER_OWN + OUT), BF16),
+            jax.ShapeDtypeStruct((2, 8, WIDTH), F32),
+            jax.ShapeDtypeStruct((2, 8, SIGNAL), F32),
+            jax.ShapeDtypeStruct((2, 8, 128), F32),
+        ],
+        in_specs=[vmem] * 13,
+        out_specs=[vmem] * 4,
+        compiler_params=pltpu.CompilerParams(vmem_limit_bytes=60 << 20),
+        name="pack_step",
+    )(*params)
+
+
 def shards(
     x_in, cotangent, seq_lengths, gain_in, w_zx, w_bc, w_dt, conv_x, conv_bc,
     bias_x, bias_bc, dt_bias, a_log, skip, gain_gate, w_out,
 ):
-    def wide(part, width):
-        return jnp.pad(part, ((0, 0), (0, 0), (0, width - part.shape[-1])))
-
-    own = jnp.concatenate(
-        [w_zx[:, :, 1], w_bc, wide(w_dt, DT), w_zx[:, :, 0], jnp.swapaxes(w_out, 1, 2)], axis=2
+    own, vec, conv, head = pack_step(
+        gain_in, w_zx, w_bc, w_dt, conv_x, conv_bc, bias_x, bias_bc,
+        dt_bias, a_log, skip, gain_gate, jnp.swapaxes(w_out, 1, 2),
     )
-    vec = jnp.stack([gain_in, gain_gate, jnp.repeat(skip, 64, axis=1)], axis=1)
-    vec = jnp.pad(vec, ((0, 0), (0, 5), (0, 0))).astype(F32)
-    conv = jnp.concatenate(
-        [
-            jnp.concatenate([conv_x, conv_bc], axis=2),
-            jnp.concatenate([bias_x, bias_bc], axis=1)[:, None, :],
-        ],
-        axis=1,
-    )
-    conv = jnp.pad(conv, ((0, 0), (0, 3), (0, 0))).astype(F32)
-    head = wide(jnp.stack([dt_bias, a_log], axis=1), 128)
-    head = jnp.pad(head, ((0, 0), (0, 6), (0, 0))).astype(F32)
     parts = whole_step(x_in, cotangent, own, seq_lengths, vec, conv, head)
     done = finish_step(*parts)
     return (*done[:-1], jnp.swapaxes(done[-1], 1, 2))

time: 171 us -> 166 us (0.971)
  local copies, waits for them, and re-layouts: 4.7 us -> 0 us
  Pallas kernels: 163 us -> 165 us
  other arithmetic: 1.95 us -> 0 us
    unnamed x32 -> x0, local copies, waits for them, and re-layouts: 4.31 us -> none
    pallas_call x0 -> x1, Pallas kernels: none -> 2.01 us  [pack_step(): pl.pallas_call(pack_kernel, out_shape=[jax.ShapeDtypeStruct((2, 16, XS +...]
    convert_element_type x3 -> x0, other arithmetic: 1.93 us -> none  [the longest x1 0.67 us: shards(): vec = jnp.pad(vec, ((0, 0), (0, 5), (0, 0))).astype(F32)]
where the time goes in v4:
time: 166 us; the launch traced here: 165 us
  Pallas kernels  165 us (99%)
    pallas_call x1, Pallas kernels, whole_step(): pl.pallas_call(body, out_shape=(jax.ShapeDtypeStruct((128, WIDTH), BF16),...  160 us

profile of v4, /device:TPU:0, one launch (start us, length us, event | category | flops | bytes accessed | tf_op | source)
XLA Modules:
  0.0 165.3 jit_solution(12576677146891688945)
XLA Ops:
  0.7 2.0 %pack_step.1 = (bf16[2,16,3456]{2,1,0:T(8,128)(2,1)}, f32[2,8,1024]{2,1,0:T(8,128)}, f32[2,8,1280]{2,1,0:T(8,128)}, f32[2,8,128]{2,1,0:T(8,128)}) custom-call(bf16[2,1024]{1,0:T(2,128)(2,1)} %gain_in.1, bf16[2,16,2,1024]{3,2,1,0:T(2,128)(2,1)} %w_zx.1, bf16[2,16,256]{2,1,0:T(8,128)(2,1)} %w_bc.1, bf16[2,16,16]{2,1,0:T(8,128)(2,1)} %w_dt.1, ...), custom_call_target="tpu_custom_call" | custom-call | tf_op jit(solution)/shard_map/pack_step/pallas_call | solution.py:1138
  2.7 159.7 %whole_step.1 = (bf16[128,1024]{1,0:T(8,128)(2,1)}, f32[128,1024]{1,0:T(8,128)}, f32[2,16,1408]{2,1,0:T(8,128)}, f32[2,16,1024]{2,1,0:T(8,128)}, f32[2,16,1024]{2,1,0:T(8,128)}, /*index=5*/f32[2,16,1024]{2,1,0:T(8,128)}) custom-call(bf16[128,1024]{1,0:T(8,128)(2,1)} %x_ref.1, bf16[128,1024]{1,0:T(8,128)(2,1)} %cot_ref.1, ...), custom_call_target="tpu_custom_call" | custom-call | tf_op jit(solution)/shard_map/whole_step/pallas_call | solution.py:1032
  162.3 2.9 %finish_step.1 = (bf16[128,1024]{1,0:T(8,128)(2,1)}, f32[128,1024]{1,0:T(8,128)}, f32[2,1024]{1,0:T(2,128)}, f32[2,16,2,1024]{3,2,1,0:T(2,128)}, f32[2,16,256]{2...) custom-call(bf16[128,1024]{1,0:T(8,128)(2,1)} %get-tuple-element.44., ...), custom_call_target="tpu_custom_call" | custom-call | tf_op jit(solution)/shard_map/finish_step/pallas_call | solution.py:1091

commit v5 on v4

--- a/solution.py
+++ b/solution.py
@@ -643,7 +643,6 @@
     forward_steps(1)
     gather_o1.relay()
     forward_conv(1)
-    transposed(normed, norm_t.at[1])
     forward_ssd(1)
     gather_o1.core()
     gather_g1.finish()
@@ -652,6 +651,7 @@
     squares_1 = send_rows(1)
     gather_o1.finish()
     forward_out(1, peer_rows)
+    transposed(normed, norm_t.at[1])
     send_cot.wait_recv()
 
     @pl.loop(0, 4)
@@ -902,6 +902,9 @@
     reduce_o1.relay()
     reduce_g1.line()
     reduce_x1.line()
+    smalls_1.core()
+    wait_mix(1, peer_rows)
+    act_ref[...] = (hid[1, own_rows, :] + mixed_rows(1, own_rows)).astype(BF16)
     wait_mix(2, pl.ds(0, ROWS))
 
     @pl.loop(0, 4)
@@ -909,7 +912,6 @@
         rows = tile(step, 64)
         grad[rows, :] = next_grad(1, 2, rows)
 
-    smalls_1.core()
     backward_gate(0)
     inner_0 = send_rows(3)
     reduce_g1.relay()
@@ -917,8 +919,6 @@
     reduce_o0.core()
     reduce_o1.plane()
     smalls_1.along_x()
-    wait_mix(1, peer_rows)
-    act_ref[...] = (hid[1, own_rows, :] + mixed_rows(1, own_rows)).astype(BF16)
     reduce_x1.relay()
     backward_ssd(0, inner_0, 3, lambda: None)
     reduce_o0.line()

time: 166 us -> 165 us (level)
  no operation moved by 1% of the time
where the time goes in v5:
time: 165 us; the launch traced here: 164 us
  Pallas kernels  164 us (99%)
    pallas_call x1, Pallas kernels, whole_step(): pl.pallas_call(body, out_shape=(jax.ShapeDtypeStruct((128, WIDTH), BF16),...  159 us

profile of v5, /device:TPU:0, one launch (start us, length us, event | category | flops | bytes accessed | tf_op | source)
XLA Modules:
  0.0 164.4 jit_solution(3006282075994064458)
XLA Ops:
  0.7 2.0 %pack_step.1 = (bf16[2,16,3456]{2,1,0:T(8,128)(2,1)}, f32[2,8,1024]{2,1,0:T(8,128)}, f32[2,8,1280]{2,1,0:T(8,128)}, f32[2,8,128]{2,1,0:T(8,128)}) custom-call(bf16[2,1024]{1,0:T(2,128)(2,1)} %gain_in.1, bf16[2,16,2,1024]{3,2,1,0:T(2,128)(2,1)} %w_zx.1, bf16[2,16,256]{2,1,0:T(8,128)(2,1)} %w_bc.1, bf16[2,16,16]{2,1,0:T(8,128)(2,1)} %w_dt.1, ...), custom_call_target="tpu_custom_call" | custom-call | tf_op jit(solution)/shard_map/pack_step/pallas_call | solution.py:1138
  2.7 158.7 %whole_step.1 = (bf16[128,1024]{1,0:T(8,128)(2,1)}, f32[128,1024]{1,0:T(8,128)}, f32[2,16,1408]{2,1,0:T(8,128)}, f32[2,16,1024]{2,1,0:T(8,128)}, f32[2,16,1024]{2,1,0:T(8,128)}, /*index=5*/f32[2,16,1024]{2,1,0:T(8,128)}) custom-call(bf16[128,1024]{1,0:T(8,128)(2,1)} %x_ref.1, bf16[128,1024]{1,0:T(8,128)(2,1)} %cot_ref.1, ...), custom_call_target="tpu_custom_call" | custom-call | tf_op jit(solution)/shard_map/whole_step/pallas_call | solution.py:1032
  161.4 2.9 %finish_step.1 = (bf16[128,1024]{1,0:T(8,128)(2,1)}, f32[128,1024]{1,0:T(8,128)}, f32[2,1024]{1,0:T(2,128)}, f32[2,16,2,1024]{3,2,1,0:T(2,128)}, f32[2,16,256]{2...) custom-call(bf16[128,1024]{1,0:T(8,128)(2,1)} %get-tuple-element.44., ...), custom_call_target="tpu_custom_call" | custom-call | tf_op jit(solution)/shard_map/finish_step/pallas_call | solution.py:1091
